TPU v7x, 512 devices: a whole 4x8x8 slice. The times are simulated.
512 devices in a mesh: tm: 8 (over x, core), tile: 64 (over y, z).
Axes of the slice: x: 4, y: 8, z: 8, core: 2. Of those that a mesh axis runs over, the one named last changes fastest.
Arguments:
- features: bfloat16 [2, 32, 128, 16, 512], P(None, 'tm', 'tile')
- lengths: int32 [2], replicated, may hold values from 1 to 32, as said below
- gain_in: float32 [512], replicated, may hold values from 0.5 to 1.5
- bias_in: float32 [512], replicated, may hold values from -3 to 3
- conv_in: bfloat16 [512, 27, 256], P('tile'), may hold values from -0.0546875 to 0.0546875
- skip_weight: bfloat16 [512, 256], P('tile'), may hold values from -0.25 to 0.25
Outputs:
- decoded: bfloat16 [2, 32, 128, 16, 256], P(None, 'tm', 'tile')
Inputs may be any that keep to these rules, and one draw needn't show every extreme that they name: `lengths`: every video has one or more valid frames, the first ones of its buffer; in every draw one video fills all 32 frames.
All inputs are finite; a program needn't handle non-finite values.
Results may differ from a plain program's by a relative error of at most 0.0021.
Values may be sent and summed in bfloat16 or wider, within the bound.
No kernel may reach another device: no remote copies, remote signals or barrier semaphores. Data moves between devices by JAX's collectives and lax.ppermute only.
A program may use at most 64 MiB of HBM per device.

v0:
```python
import jax
import jax.numpy as jnp
from jax import lax
from jax.sharding import PartitionSpec as P

GROUPS = 32


EPS = 1e-06


def carried_in(part, axis, combine, identity):
    place = lax.axis_index(axis)
    gathered = jax.tree.map(lambda a: lax.all_gather(a, axis), part)
    state = jax.tree.map(lambda a, e: jnp.zeros_like(a) + jnp.asarray(e, a.dtype), part, identity)

    def one(lap, state):
        return combine(
            state, jax.tree.map(lambda a: lax.dynamic_index_in_dim(a, lap, 0, False), gathered)
        )

    return lax.fori_loop(0, place, one, state)


def passed_along(shard, axis, by):
    count = lax.axis_size(axis)
    pairs = [(i, i + by) for i in range(count) if 0 <= i + by < count]
    return lax.ppermute(shard, axis, pairs)


def padded_2(block, sides, width):
    for axis, dim in sides:
        count = lax.axis_size(axis)
        forward = [(i, i + 1) for i in range(count - 1)]
        backward = [(target, source) for source, target in forward]
        low = lax.ppermute(
            lax.slice_in_dim(block, block.shape[dim] - width, None, axis=dim), axis, forward
        )
        high = lax.ppermute(lax.slice_in_dim(block, 0, width, axis=dim), axis, backward)
        block = jnp.concatenate([low, block, high], axis=dim)
    return block


def span_valid(lengths, frames):
    stamps = lax.axis_index("tm") * frames + jnp.arange(frames, dtype=jnp.int32)
    return (stamps[None, :] < lengths[:, None]).astype(jnp.float32)


def group_sums(signal, present):
    videos, frames, row_count, col_count, channels = signal.shape
    grouped = signal.reshape(videos, frames, row_count * col_count, GROUPS, channels // GROUPS)
    grouped = grouped * present[:, :, None, None, None]
    return (jnp.sum(grouped, axis=(1, 2, 4)), jnp.sum(grouped * grouped, axis=(1, 2, 4)))


def add_pair(earlier, later):
    return (earlier[0] + later[0], earlier[1] + later[1])


def prefix_sums(linear, square):
    total_linear, total_square = lax.psum((linear, square), "tile")
    blank = jnp.zeros_like(total_linear)
    before_linear, before_square = carried_in(
        (total_linear, total_square), "tm", add_pair, (blank, blank)
    )
    return (before_linear + total_linear, before_square + total_square)


def norm_act(signal, present, lengths, norm_gain, norm_bias):
    videos, frames, row_count, col_count, channels = signal.shape
    per_group = channels // GROUPS
    linear, square = group_sums(signal, present)
    linear, square = prefix_sums(linear, square)
    frames_seen = jnp.minimum(lengths, (lax.axis_index("tm") + 1) * frames).astype(jnp.float32)
    cell_count = frames_seen * float(row_count * lax.axis_size("tile") * col_count * per_group)
    centre = linear / cell_count[:, None]
    inverse = lax.rsqrt(square / cell_count[:, None] - centre * centre + EPS)
    grouped = signal.reshape(videos, frames, row_count, col_count, GROUPS, per_group)
    normed = (grouped - centre[:, None, None, None, :, None]) * inverse[
        :, None, None, None, :, None
    ]
    normed = normed.reshape(signal.shape) * norm_gain + norm_bias
    return (jax.nn.silu(normed) * present[:, :, None, None, None]).astype(jnp.bfloat16)


def add_cache(active, received):
    first_frame = jnp.broadcast_to(active[:, :1], received.shape)
    earlier = jnp.where(lax.axis_index("tm") == 0, first_frame, received)
    return jnp.concatenate([earlier, active], axis=1)


def fix_rows(padded):
    row_total = padded.shape[2]
    row_index = jnp.arange(row_total, dtype=jnp.int32)[None, None, :, None, None]
    upper_row = padded[:, :, 1:2]
    bottom = padded[:, :, row_total - 2 : row_total - 1]
    padded = jnp.where((lax.axis_index("tile") == 0) & (row_index < 1), upper_row, padded)
    return jnp.where(
        (lax.axis_index("tile") == lax.axis_size("tile") - 1) & (row_index >= row_total - 1),
        bottom,
        padded,
    )


def conv_terms(padded, weight_rows, frames, row_count, col_count):
    channel_count = weight_rows.shape[0]
    summed = jnp.zeros(
        (padded.shape[0] * frames * row_count * col_count, weight_rows.shape[2]), jnp.float32
    )
    for tap_t in range(3):
        windows = []
        for tap_r in range(3):
            for tap_c in range(3):
                windows.append(
                    padded[
                        :,
                        tap_t : tap_t + frames,
                        tap_r : tap_r + row_count,
                        tap_c : tap_c + col_count,
                        :,
                    ]
                )
        patches = jnp.concatenate(windows, axis=4).reshape(-1, 9 * channel_count)
        tap_rows = (
            weight_rows[:, tap_t * 9 : tap_t * 9 + 9, :]
            .transpose(1, 0, 2)
            .reshape(9 * channel_count, -1)
        )
        summed = summed + jnp.dot(patches, tap_rows, preferred_element_type=jnp.float32)
    return summed


def per_device(features, lengths, gain_in, bias_in, conv_in, skip_weight):
    videos, frames, row_count, col_count, wide_in = features.shape
    wide_out = conv_in.shape[2]
    present = span_valid(lengths, frames)
    signal = features.astype(jnp.float32)
    active = norm_act(signal, present, lengths, gain_in, bias_in)
    received = passed_along(active[:, frames - 2 :], "tm", 1)
    extended = add_cache(active, received)
    padded = fix_rows(padded_2(extended, (("tile", 2),), 1))
    padded = jnp.pad(padded, ((0, 0), (0, 0), (0, 0), (1, 1), (0, 0)), mode="edge")
    flat_in = features.reshape(-1, wide_in)
    output = conv_terms(
        padded, lax.all_gather(conv_in, "tile", axis=0, tiled=True), frames, row_count, col_count
    )
    skipped = jnp.dot(
        flat_in,
        lax.all_gather(skip_weight, "tile", axis=0, tiled=True),
        preferred_element_type=jnp.float32,
    )
    result = (output + skipped).reshape(videos, frames, row_count, col_count, wide_out)
    return (result * present[:, :, None, None, None]).astype(jnp.bfloat16)


def solution(mesh):
    placed = (
        P(None, "tm", "tile", None, None),
        P(),
        P(),
        P(),
        P("tile", None, None),
        P("tile", None),
    )
    return jax.shard_map(
        per_device,
        mesh=mesh,
        in_specs=placed,
        out_specs=P(None, "tm", "tile", None, None),
        check_vma=False,
    )
```

profile of v0, /device:TPU:26, one launch (start us, length us, event | category | flops | bytes accessed | tf_op | source)
XLA Modules:
  0.0 263.5 jit_solution(9290296648267192699)
XLA Ops:
  6.5 0.7 all-gather.6.cloned.1.call-update
  7.3 0.7 compare_convert_fusion
  8.0 1.1 fusion.3
  9.5 136.4 %all-reduce = (f32[2,32]{1,0:T(2,128)S(1)}, f32[2,32]{1,0:T(2,128)S(1)}) all-reduce(f32[2,32]{1,0:T(2,128)S(1)} %reduce_sum.25, f32[2,32]{1,0:T(2,128)S(1)} %reduce_sum.37), channel_id=1, replica_groups=mesh['tm'=8,'tile'=64] {'tile'}, use_global_device_ids=true, to_apply=%region_2.0 | all-reduce | flops 128 | bytes 1024 | tf_op jit(solution)/shard_map/psum | solution.py:61
  145.9 8.6 %all-gather.2 = f32[8,2,32]{2,1,0:T(2,128)S(1)} all-gather(f32[1,2,32]{2,1,0:T(2,128)S(1)} %bitcast.44), channel_id=2, replica_groups=mesh['tm'=8,'tile'=64] {'tm'}, dimensions={0}, use_global_device_ids=true | all-gather | bytes 2304 | tf_op jit(solution)/shard_map/all_gather | solution.py:14
  154.5 10.4 %all-gather.3 = f32[8,2,32]{2,1,0:T(2,128)S(1)} all-gather(f32[1,2,32]{2,1,0:T(2,128)S(1)} %bitcast.45), channel_id=3, replica_groups=mesh['tm'=8,'tile'=64] {'tm'}, dimensions={0}, use_global_device_ids=true | all-gather | bytes 2304 | tf_op jit(solution)/shard_map/all_gather | solution.py:14
  164.9 0.7 convert_multiply_fusion.1
  166.0 1.2 fusion.13
  167.2 2.3 collective-permute-start
  169.5 4.0 %collective-permute-done = bf16[2,2,2,16,512]{4,3,2,1,0:T(8,128)(2,1)S(1)} collective-permute-done((bf16[2,2,2,16,512]{4,3,2,1,0:T(8,128)(2,1)S(1)}, bf16[2,2,2,16,512]{4,3,2,1,0:T(8,128)(2,1)S(1)}, u32[]{:S(2)}, u32[]{:S(2)}) %collective-permute-start) | collective-permute-done | bytes 131104 | tf_op jit(solution)/shard_map/ppermute | solution.py:28
  173.6 2.9 %collective-permute-start.1 = (bf16[2,6,1,16,512]{4,3,2,1,0:T(8,128)(2,1)S(1)}, bf16[2,6,1,16,512]{4,3,2,1,0:T(8,128)(2,1)S(1)}, u32[]{:S(2)}, u32[]{:S(2)}) collective-permute-start(bf16[2,6,1,16,512]{4,3,2,1,0:T(8,128)(2,1)S(1)} %get-tuple-element.81), channel_id=1, source_target_pairs={{0,1},{1,2},{2,3},{3,4},{4,5},{5,6},{6,7},{7,8},{8,9},{9,10},{10,1... | collective-permute-start | bytes 589832 | tf_op jit(solution)/shard_map/ppermute | solution.py:36
  176.5 5.1 %collective-permute-start.2 = (bf16[2,6,1,16,512]{4,3,2,1,0:T(8,128)(2,1)S(1)}, bf16[2,6,1,16,512]{4,3,2,1,0:T(8,128)(2,1)S(1)}, u32[]{:S(2)}, u32[]{:S(2)}) collective-permute-start(bf16[2,6,1,16,512]{4,3,2,1,0:T(8,128)(2,1)S(1)} %get-tuple-element.82), channel_id=1, source_target_pairs={{1,0},{2,1},{3,2},{4,3},{5,4},{6,5},{7,6},{8,7},{9,8},{10,9},{11,1... | collective-permute-start | bytes 589832 | tf_op jit(solution)/shard_map/ppermute | solution.py:39
  181.6 61.1 %all_gather.23 = bf16[512,256]{1,0:T(8,128)(2,1)S(1)} all-gather(bf16[8,256]{1,0:T(8,128)(2,1)S(1)} %copy-done.5), channel_id=1, replica_groups=mesh['tm'=8,'tile'=64] {'tile'}, dimensions={0}, use_global_device_ids=true | all-gather | bytes 266240 | tf_op jit(solution)/shard_map/all_gather | solution.py:149
  242.7 0.2 fusion
  242.9 0.2 fusion.50
  243.2 0.1 fusion.29
  243.4 0.1 fusion.15
  243.6 0.3 fusion.47
  243.9 0.4 fusion.46
  244.6 0.2 fusion.43
  244.8 1.0 copy-done.2
  245.8 0.2 fusion.27
  246.2 1.2 copy-done
  247.6 3.8 %fusion.49 = (bf16[512,9,256]{2,0,1:T(8,128)(2,1)S(1)}, bf16[512,9,256]{2,0,1:T(8,128)(2,1)S(1)}, bf16[512,9,256]{2,0,1:T(8,128)(2,1)S(1)}) fusion(bf16[512,27,256]{2,0,1:T(8,128)(2,1)} %all-gather.6.cloned.1.call-done), kind=kLoop, calls=%fused_computation.114 | loop fusion | bytes 14155776 | tf_op jit(solution)/shard_map/slice | solution.py:125
  251.4 0.8 fusion.51
  252.2 0.9 copy-done.1
  253.1 0.8 convolution_add_fusion.2
  253.9 0.9 copy-done.3
  254.7 0.8 convolution_add_fusion.1
  255.5 0.2 copy-done.4
  255.7 0.2 convolution_add_fusion
  255.9 0.7 multiply_convert_fusion
  (43 shorter events, 1.8 us)
Async XLA Ops:
  6.5 175.0 %copy-start.5 = (bf16[8,256]{1,0:T(8,128)(2,1)S(1)}, bf16[8,256]{1,0:T(8,128)(2,1)}, u32[]{:S(2)}) copy-start(bf16[8,256]{1,0:T(8,128)(2,1)} %param.13) | copy-start | bytes 12292
  6.5 241.0 %all-gather.6.cloned.1.call-start = ((), (), s32[]{:S(2)}) async-start(), calls=%async_computation | async-start | bytes 7188480 | tf_op jit(solution)/shard_map/all_gather | solution.py:145
  167.2 6.3 %collective-permute-start = (bf16[2,2,2,16,512]{4,3,2,1,0:T(8,128)(2,1)S(1)}, bf16[2,2,2,16,512]{4,3,2,1,0:T(8,128)(2,1)S(1)}, u32[]{:S(2)}, u32[]{:S(2)}) collective-permute-start(bf16[2,2,2,16,512]{4,3,2,1,0:T(8,128)(2,1)S(1)} %slice.176), channel_id=1, source_target_pairs={{0,64},{64,128},{128,192},{192,256},{256,320},{320,384},{384,448},... | collective-permute-start | bytes 393224 | tf_op jit(solution)/shard_map/ppermute | solution.py:28
  173.6 69.1 %collective-permute-start.1 = (bf16[2,6,1,16,512]{4,3,2,1,0:T(8,128)(2,1)S(1)}, bf16[2,6,1,16,512]{4,3,2,1,0:T(8,128)(2,1)S(1)}, u32[]{:S(2)}, u32[]{:S(2)}) collective-permute-start(bf16[2,6,1,16,512]{4,3,2,1,0:T(8,128)(2,1)S(1)} %get-tuple-element.81), channel_id=1, source_target_pairs={{0,1},{1,2},{2,3},{3,4},{4,5},{5,6},{6,7},{7,8},{8,9},{9,10},{10,1... | collective-permute-start | bytes 589832 | tf_op jit(solution)/shard_map/ppermute | solution.py:36
  176.5 66.2 %collective-permute-start.2 = (bf16[2,6,1,16,512]{4,3,2,1,0:T(8,128)(2,1)S(1)}, bf16[2,6,1,16,512]{4,3,2,1,0:T(8,128)(2,1)S(1)}, u32[]{:S(2)}, u32[]{:S(2)}) collective-permute-start(bf16[2,6,1,16,512]{4,3,2,1,0:T(8,128)(2,1)S(1)} %get-tuple-element.82), channel_id=1, source_target_pairs={{1,0},{2,1},{3,2},{4,3},{5,4},{6,5},{7,6},{8,7},{9,8},{10,9},{11,1... | collective-permute-start | bytes 589832 | tf_op jit(solution)/shard_map/ppermute | solution.py:39
  244.3 1.5 copy-start.2
  246.0 1.4 copy-start
  251.4 1.7 copy-start.1
  253.1 1.7 copy-start.3
  254.7 0.9 copy-start.4
Sparse Core Ops, SparseCore 0:
  10.3 106.7 all-gather.5
where the time goes:
time: 264 us
  blocking collectives  217 us (82%)
  between operations  13.7 us (5%)
  starting transfers between devices  10.2 us (4%)
  local copies, waits for them, and re-layouts  8.84 us (3%)
  other arithmetic  6.93 us (3%)
  waiting for transfers between devices  4.72 us (2%)
    psum x1, blocking collectives, prefix_sums(): total_linear, total_square = lax.psum((linear, square), 'tile')  136 us
    all_gather x1, blocking collectives, per_device(): lax.all_gather(skip_weight, 'tile', axis=0, tiled=True)  61.1 us
    all_gather x2, blocking collectives, carried_in(): gathered = jax.tree.map(lambda a: lax.all_gather(a, axis), part)  19 us
  transfers between devices with their start and end apart: 4, of which 1 were waited for; matrix products, arithmetic and copies ran while one was open for 3% of the time, Pallas kernels for 0%

commit v1 on v0

v1 whole, which is shorter than its diff:
```python
import jax
import jax.numpy as jnp
from jax import lax
from jax.sharding import Mesh
from jax.sharding import PartitionSpec as P

GROUPS = 32
EPS = 1e-06
TM = ("xh", "xl", "core")
TILE = ("y", "z")
TEAM = ("xl", "core")
TEAM_SIZE = 4


def three_parts(value):
    high = lax.reduce_precision(value, 8, 7)
    rest = value - high
    middle = lax.reduce_precision(rest, 8, 7)
    low = rest - middle
    return jnp.stack([high, middle, low]).astype(jnp.bfloat16)


def to_all(block, axis):
    count = lax.axis_size(axis)
    copies = jnp.broadcast_to(block[None], (count,) + block.shape)
    return lax.all_to_all(copies, axis, 0, 0, tiled=True)


def local_sums(features, present):
    videos, frames, row_count, col_count, channels = features.shape
    masked = features.astype(jnp.float32) * present[:, :, None, None, None]
    linear = jnp.sum(masked, axis=(1, 2, 3)).reshape(videos, GROUPS, channels // GROUPS)
    square = jnp.sum(masked * masked, axis=(1, 2, 3)).reshape(videos, GROUPS, channels // GROUPS)
    return jnp.stack([jnp.sum(linear, axis=2), jnp.sum(square, axis=2)])


def with_rows(features):
    place, count = lax.axis_index(TILE), lax.axis_size(TILE)
    forward = [(i, i + 1) for i in range(count - 1)]
    backward = [(i + 1, i) for i in range(count - 1)]
    first, last = features[:, :, :1], features[:, :, -1:]
    low = lax.ppermute(last, TILE, forward)
    high = lax.ppermute(first, TILE, backward)
    low = jnp.where(place == 0, first, low)
    high = jnp.where(place == count - 1, last, high)
    return jnp.concatenate([low, features, high], axis=2)


def by_member(block):
    channels = block.shape[-1]
    share = channels // TEAM_SIZE
    column = jnp.arange(channels, dtype=jnp.int32)
    member, rest = column // share, column % share
    source = (rest // 2) * 8 + member * 2 + rest % 2
    chosen = (jnp.arange(channels, dtype=jnp.int32)[:, None] == source[None, :]).astype(jnp.bfloat16)
    flat = jnp.dot(block.reshape(-1, channels), chosen, preferred_element_type=jnp.float32)
    flat = flat.astype(jnp.bfloat16).reshape(-1, TEAM_SIZE, share).transpose(1, 0, 2)
    return flat.reshape((TEAM_SIZE,) + block.shape[:-1] + (share,))


def spans_of_team(shares):
    me = lax.axis_index(TEAM)
    arrived = [lax.dynamic_index_in_dim(shares, me, 0, False)]
    for step in range(1, TEAM_SIZE):
        pairs = [(i, i ^ step) for i in range(TEAM_SIZE)]
        outgoing = lax.dynamic_index_in_dim(shares, me ^ step, 0, False)
        arrived.append(lax.ppermute(outgoing, TEAM, pairs))
    arrived = jnp.stack(arrived)
    return [lax.dynamic_index_in_dim(arrived, me ^ span, 0, False) for span in range(TEAM_SIZE)]


def per_device(features, lengths, gain_in, bias_in, conv_in, skip_weight):
    videos, frames, row_count, col_count, wide_in = features.shape
    wide_out = conv_in.shape[2]
    share = wide_in // TEAM_SIZE
    taps = conv_in.shape[1]
    me = lax.axis_index(TEAM)
    team_first = lax.axis_index("xh") * TEAM_SIZE
    span = team_first + me

    stamps = span * frames + jnp.arange(frames, dtype=jnp.int32)
    present = (stamps[None, :] < lengths[:, None]).astype(jnp.float32)
    sums = local_sums(features, present)

    weights = jnp.concatenate([conv_in, skip_weight[:, None, :]], axis=1)
    mine = conv_in.shape[0] // TEAM_SIZE
    weights = lax.dynamic_slice_in_dim(weights, me * mine, mine, axis=0)
    weights = weights.transpose(1, 0, 2).reshape((taps + 1) * mine, wide_out)
    parts = three_parts(sums.reshape(-1)).reshape(-1)
    parts = jnp.pad(parts, (0, 8 * wide_out - parts.shape[0])).reshape(8, wide_out)
    around_z = to_all(jnp.concatenate([weights, parts], axis=0), "z")
    rows = (taps + 1) * mine
    z_count = lax.axis_size("z")
    weights = around_z[:, :rows].reshape(z_count, taps + 1, mine, wide_out).transpose(1, 0, 2, 3)
    weights = lax.all_gather(
        weights.reshape(taps + 1, z_count * mine, wide_out), "y", axis=1, tiled=True
    )
    parts = around_z[:, rows:].astype(jnp.float32).reshape(z_count, -1)[:, : 3 * sums.size]
    sums = jnp.sum(parts.reshape(z_count, 3, sums.size), axis=(0, 1)).reshape(1, -1)
    sums = jnp.sum(to_all(sums, "y"), axis=0)
    sums = to_all(sums, TM).reshape(-1, 2, videos, GROUPS)
    sums = jnp.cumsum(sums, axis=0)

    spans = spans_of_team(by_member(with_rows(features)))
    cached = lax.ppermute(spans[-1][:, frames - 2 :], "xh", [(0, 1)])
    first = jnp.broadcast_to(spans[0][:, :1], cached.shape)
    cached = jnp.where(team_first == 0, first, cached)
    signal = jnp.concatenate([cached] + spans, axis=1)

    span_count = sums.shape[0]
    ends = (jnp.arange(span_count, dtype=jnp.int32) + 1) * frames
    seen = jnp.minimum(lengths[None, :], ends[:, None]).astype(jnp.float32)
    cells = seen * float(row_count * lax.axis_size(TILE) * col_count * (wide_in // GROUPS))
    centre = sums[:, 0] / cells[:, :, None]
    inverse = lax.rsqrt(sums[:, 1] / cells[:, :, None] - centre * centre + EPS)
    gain = lax.dynamic_index_in_dim(gain_in.reshape(-1, TEAM_SIZE, mine), me, 1, False).reshape(-1)
    bias = lax.dynamic_index_in_dim(bias_in.reshape(-1, TEAM_SIZE, mine), me, 1, False).reshape(-1)
    centre = jnp.repeat(centre, share // GROUPS, axis=2)
    scale = jnp.repeat(inverse, share // GROUPS, axis=2) * gain
    stamps = team_first * frames - 2 + jnp.arange(signal.shape[1], dtype=jnp.int32)
    stamps = jnp.maximum(stamps, 0)
    centre = jnp.take(centre, stamps // frames, axis=0).transpose(1, 0, 2)
    scale = jnp.take(scale, stamps // frames, axis=0).transpose(1, 0, 2)
    shown = (stamps[None, :] < lengths[:, None]).astype(jnp.float32)
    normed = (signal.astype(jnp.float32) - centre[:, :, None, None, :]) * scale[:, :, None, None, :] + bias
    active = (jax.nn.silu(normed) * shown[:, :, None, None, None]).astype(jnp.bfloat16)
    active = jnp.pad(active, ((0, 0), (0, 0), (0, 0), (1, 1), (0, 0)), mode="edge")

    length = TEAM_SIZE * frames
    windows = []
    for a in range(3):
        for b in range(3):
            for e in range(3):
                windows.append(active[:, a : a + length, b : b + row_count, e : e + col_count])
    windows.append(signal[:, 2:, 1 : 1 + row_count])
    patches = jnp.concatenate(windows, axis=4).reshape(-1, (taps + 1) * share)
    total = jnp.dot(patches, weights.reshape(-1, wide_out), preferred_element_type=jnp.float32)
    total = total.reshape(videos, 2, 2, frames, row_count, col_count, wide_out)

    core, xl = lax.axis_index("core"), lax.axis_index("xl")
    swap = [(0, 1), (1, 0)]
    other = lax.ppermute(lax.dynamic_index_in_dim(total, 1 - core, 2, False), "core", swap)
    total = lax.dynamic_index_in_dim(total, core, 2, False) + other
    other = lax.ppermute(lax.dynamic_index_in_dim(total, 1 - xl, 1, False), "xl", swap)
    total = lax.dynamic_index_in_dim(total, xl, 1, False) + other
    return (total * present[:, :, None, None, None]).astype(jnp.bfloat16)


def solution(mesh):
    spans, tiles = mesh.devices.shape
    fine = Mesh(
        mesh.devices.reshape(spans // TEAM_SIZE, 2, 2, 8, tiles // 8), TM + TILE
    )
    placed = (
        P(None, TM, TILE, None, None),
        P(),
        P(),
        P(),
        P(TILE, None, None),
        P(TILE, None),
    )
    return jax.shard_map(
        per_device,
        mesh=fine,
        in_specs=placed,
        out_specs=P(None, TM, TILE, None, None),
        check_vma=False,
    )
```

time: 264 us -> 145 us (0.55)
  the two profiles are of different devices: /device:TPU:26 before, /device:TPU:1 now
where the time goes in v1:
time: 145 us
  starting transfers between devices  55.7 us (38%)
  waiting for transfers between devices  29 us (20%)
  other arithmetic  25.2 us (17%)
  local copies, waits for them, and re-layouts  14.7 us (10%)
  between operations  13.9 us (10%)
  matrix products  6.12 us (4%)
    all_to_all x3, starting transfers between devices, to_all(): return lax.all_to_all(copies, axis, 0, 0, tiled=True)  26.8 us
    unnamed x19, other arithmetic  15.6 us
    all_to_all x3, waiting for transfers between devices, to_all(): return lax.all_to_all(copies, axis, 0, 0, tiled=True)  9.8 us
    ppermute x3, starting transfers between devices, spans_of_team(): arrived.append(lax.ppermute(outgoing, TEAM, pairs))  8.6 us
    unnamed x19, local copies, waits for them, and re-layouts  6.97 us
    ppermute x1, starting transfers between devices, per_device(): lax.ppermute(lax.dynamic_index_in_dim(total, 1 - core, 2, False), 'core',...  6.73 us
    all_gather x1, waiting for transfers between devices, per_device(): lax.all_gather(weights.reshape(taps + 1, z_count * mine, wide_out), 'y',...  6.71 us
    ppermute x1, waiting for transfers between devices, per_device(): lax.ppermute(lax.dynamic_index_in_dim(total, 1 - xl, 1, False), 'xl', swap)  6.31 us
  transfers between devices with their start and end apart: 12, of which 7 were waited for; matrix products, arithmetic and copies ran while one was open for 26% of the time, Pallas kernels for 0%

profile of v1, /device:TPU:1, one launch (start us, length us, event | category | flops | bytes accessed | tf_op | source)
XLA Modules:
  0.0 144.6 jit_solution(11116478200903865562)
XLA Ops:
  6.5 1.0 fusion.61
  7.6 4.8 %collective-permute-start = (bf16[2,4,1,16,512]{4,3,2,1,0:T(8,128)(2,1)S(1)}, bf16[2,4,1,16,512]{4,3,2,1,0:T(8,128)(2,1)S(1)}, u32[]{:S(2)}, u32[]{:S(2)}) collective-permute-start(bf16[2,4,1,16,512]{4,3,2,1,0:T(8,128)(2,1)S(1)} %get-tuple-element.22), channel_id=1, source_target_pairs={{0,1},{1,2},{2,3},{3,4},{4,5},{5,6},{6,7},{7,8},{8,9},{9,10},{10,1... | collective-permute-start | bytes 393224 | tf_op jit(solution)/shard_map/ppermute | solution.py:42
  12.4 1.3 collective-permute-start.1
  14.5 1.1 fusion
  16.1 1.0 fusion.40
  17.8 11.2 %all-to-all-start = ((bf16[8,64,256]{2,1,0:T(8,128)(2,1)}), bf16[8,64,256]{2,1,0:T(8,128)(2,1)S(1)}, u32[]{:S(2)}, u32[]{:S(2)}) async-start(bf16[8,64,256]{2,1,0:T(8,128)(2,1)} %broadcast_in_dim.25), calls=%async_computation | async-start | bytes 524288 | tf_op jit(solution)/shard_map/all_to_all | solution.py:26
  30.5 1.0 broadcast_select_fusion.1
  31.5 1.0 pad_maximum_fusion
  33.4 4.5 %collective-permute-start.4 = (bf16[2,4,4,16,128]{4,3,2,1,0:T(8,128)(2,1)S(1)}, bf16[2,4,4,16,128]{4,3,2,1,0:T(8,128)(2,1)S(1)}, u32[]{:S(2)}, u32[]{:S(2)}) collective-permute-start(bf16[2,4,4,16,128]{4,3,2,1,0:T(8,128)(2,1)S(1)} %get-tuple-element.17), channel_id=1, source_target_pairs={{0,192},{64,128},{128,64},{192,0},{1,193},{65,129},{129,65},{193,1... | collective-permute-start | bytes 393224 | tf_op jit(solution)/shard_map/ppermute | solution.py:67
  37.9 1.9 %collective-permute-start.2 = (bf16[2,4,4,16,128]{4,3,2,1,0:T(8,128)(2,1)S(1)}, bf16[2,4,4,16,128]{4,3,2,1,0:T(8,128)(2,1)S(1)}, u32[]{:S(2)}, u32[]{:S(2)}) collective-permute-start(bf16[2,4,4,16,128]{4,3,2,1,0:T(8,128)(2,1)S(1)} %get-tuple-element.19), channel_id=1, source_target_pairs={{0,64},{64,0},{128,192},{192,128},{1,65},{65,1},{129,193},{193,129... | collective-permute-start | bytes 393224 | tf_op jit(solution)/shard_map/ppermute | solution.py:67
  39.8 2.2 %collective-permute-start.3 = (bf16[2,4,4,16,128]{4,3,2,1,0:T(8,128)(2,1)S(1)}, bf16[2,4,4,16,128]{4,3,2,1,0:T(8,128)(2,1)S(1)}, u32[]{:S(2)}, u32[]{:S(2)}) collective-permute-start(bf16[2,4,4,16,128]{4,3,2,1,0:T(8,128)(2,1)S(1)} %get-tuple-element.18), channel_id=1, source_target_pairs={{0,128},{64,192},{128,0},{192,64},{1,129},{65,193},{129,1},{193,65... | collective-permute-start | bytes 393224 | tf_op jit(solution)/shard_map/ppermute | solution.py:67
  43.0 3.3 %collective-permute-done.3 = bf16[2,4,4,16,128]{4,3,2,1,0:T(8,128)(2,1)S(1)} collective-permute-done((bf16[2,4,4,16,128]{4,3,2,1,0:T(8,128)(2,1)S(1)}, bf16[2,4,4,16,128]{4,3,2,1,0:T(8,128)(2,1)S(1)}, u32[]{:S(2)}, u32[]{:S(2)}) %collective-permute-start.3) | collective-permute-done | bytes 131104 | tf_op jit(solution)/shard_map/ppermute | solution.py:67
  46.4 4.4 %collective-permute-start.5 = (bf16[2,2,4,16,128]{4,3,2,1,0:T(8,128)(2,1)S(1)}, bf16[2,2,4,16,128]{4,3,2,1,0:T(8,128)(2,1)S(1)}, u32[]{:S(2)}, u32[]{:S(2)}) collective-permute-start(bf16[2,2,4,16,128]{4,3,2,1,0:T(8,128)(2,1)S(1)} %slice.195), channel_id=1, source_target_pairs={{0,256},{1,257},{2,258},{3,259},{4,260},{5,261},{6,262},{7,263},{8... | collective-permute-start | bytes 196616 | tf_op jit(solution)/shard_map/ppermute | solution.py:105
  50.8 1.3 collective-permute-done.5
  52.9 6.8 %all-to-all-start.1 = ((f32[8,1,128]{2,1,0:T(1,128)}), f32[8,1,128]{2,1,0:T(1,128)S(1)}, u32[]{:S(2)}, u32[]{:S(2)}) async-start(f32[8,1,128]{2,1,0:T(1,128)} %broadcast_in_dim.26), calls=%async_computation.1 | async-start | bytes 8192 | tf_op jit(solution)/shard_map/all_to_all | solution.py:26
  59.7 6.4 %all-to-all-done.1 = f32[8,1,128]{2,1,0:T(1,128)S(1)} async-done(((f32[8,1,128]{2,1,0:T(1,128)}), f32[8,1,128]{2,1,0:T(1,128)S(1)}, u32[]{:S(2)}, u32[]{:S(2)}) %all-to-all-start.1) | async-done | bytes 4128 | tf_op jit(solution)/shard_map/all_to_all | solution.py:26
  66.8 8.8 %all-to-all-start.2 = ((f32[8,1,128]{2,1,0:T(1,128)}), f32[8,1,128]{2,1,0:T(1,128)S(1)}, u32[]{:S(2)}, u32[]{:S(2)}) async-start(f32[8,1,128]{2,1,0:T(1,128)} %broadcast_in_dim.27), calls=%async_computation.2 | async-start | bytes 8192 | tf_op jit(solution)/shard_map/all_to_all | solution.py:26
  76.6 3.4 %all-to-all-done.2 = f32[8,1,128]{2,1,0:T(1,128)S(1)} async-done(((f32[8,1,128]{2,1,0:T(1,128)}), f32[8,1,128]{2,1,0:T(1,128)S(1)}, u32[]{:S(2)}, u32[]{:S(2)}) %all-to-all-start.2) | async-done | bytes 4128 | tf_op jit(solution)/shard_map/all_to_all | solution.py:26
  85.2 0.9 fusion.5
  86.1 0.9 fusion.23
  90.2 0.9 fusion.9
  91.1 0.9 fusion.27
  92.7 0.9 fusion.11
  97.7 0.9 fusion.15
  100.2 0.9 fusion.17
  105.2 0.9 fusion.35
  106.8 6.7 %all-gather.2.cloned.1.call-done = bf16[28,128,256]{2,1,0:T(8,128)(2,1)} async-done(((bf16[28,16,256]{2,1,0:T(8,128)(2,1)}), bf16[28,128,256]{2,1,0:T(8,128)(2,1)}) %all-gather.2.cloned.1.call-update) | async-done | bytes 1835024 | tf_op jit(solution)/shard_map/all_gather | solution.py:95
  113.5 5.6 %fusion.62 = f32[2,2,2,4,2,16,256]{6,5,4,3,2,1,0:T(8,128)S(1)} fusion(bf16[2,2,2,4,2,16,3584]{6,5,4,3,2,1,0:T(8,128)(2,1)} %bitcast.29, bf16[3584,256,1,1,1,1,1]{1,0,6,5,4,3,2:T(8,128)(2,1)} %bitcast.99), kind=kOutput, calls=%fused_computation.176 | convolution fusion | flops 1879048192 | bytes 10223616 | tf_op jit(solution)/shard_map/dot_general | solution.py:137
  119.2 6.7 %collective-permute-start.6 = (f32[2,2,4,2,16,256]{5,4,3,2,1,0:T(8,128)S(1)}, f32[2,2,4,2,16,256]{5,4,3,2,1,0:T(8,128)S(1)}, u32[]{:S(2)}, u32[]{:S(2)}) collective-permute-start(f32[2,2,4,2,16,256]{5,4,3,2,1,0:T(8,128)S(1)} %dynamic-slice_bitcast_fusion), channel_id=1, source_target_pairs={{0,64},{64,0},{1,65},{65,1},{2,66},{66,2},{3,67},{67,3},{4,68},{68... | collective-permute-start | bytes 1572872 | tf_op jit(solution)/shard_map/ppermute | solution.py:142
  126.0 1.5 %collective-permute-done.6 = f32[2,2,4,2,16,256]{5,4,3,2,1,0:T(8,128)S(1)} collective-permute-done((f32[2,2,4,2,16,256]{5,4,3,2,1,0:T(8,128)S(1)}, f32[2,2,4,2,16,256]{5,4,3,2,1,0:T(8,128)S(1)}, u32[]{:S(2)}, u32[]{:S(2)}) %collective-permute-start.6) | collective-permute-done | bytes 524320 | tf_op jit(solution)/shard_map/ppermute | solution.py:142
  127.6 3.1 %collective-permute-start.7 = (f32[2,4,2,16,256]{4,3,2,1,0:T(8,128)S(1)}, f32[2,4,2,16,256]{4,3,2,1,0:T(8,128)S(1)}, u32[]{:S(2)}, u32[]{:S(2)}) collective-permute-start(f32[2,4,2,16,256]{4,3,2,1,0:T(8,128)S(1)} %dynamic-slice_bitcast_fusion.1), channel_id=1, source_target_pairs={{0,128},{128,0},{1,129},{129,1},{2,130},{130,2},{3,131},{131,3},{4... | collective-permute-start | bytes 786440 | tf_op jit(solution)/shard_map/ppermute | solution.py:144
  130.7 6.3 %collective-permute-done.7 = f32[2,4,2,16,256]{4,3,2,1,0:T(8,128)S(1)} collective-permute-done((f32[2,4,2,16,256]{4,3,2,1,0:T(8,128)S(1)}, f32[2,4,2,16,256]{4,3,2,1,0:T(8,128)S(1)}, u32[]{:S(2)}, u32[]{:S(2)}) %collective-permute-start.7) | collective-permute-done | bytes 262176 | tf_op jit(solution)/shard_map/ppermute | solution.py:144
  (106 shorter events, 28.2 us)
Async XLA Ops:
  6.5 35.5 %copy-start = (f32[512]{0:T(512)S(1)}, f32[512]{0:T(512)}, u32[]{:S(2)}) copy-start(f32[512]{0:T(512)} %param.10) | copy-start | bytes 6148
  6.5 35.7 %copy-start.1 = (f32[512]{0:T(512)S(1)}, f32[512]{0:T(512)}, u32[]{:S(2)}) copy-start(f32[512]{0:T(512)} %param.11) | copy-start | bytes 6148
  7.6 22.9 %collective-permute-start = (bf16[2,4,1,16,512]{4,3,2,1,0:T(8,128)(2,1)S(1)}, bf16[2,4,1,16,512]{4,3,2,1,0:T(8,128)(2,1)S(1)}, u32[]{:S(2)}, u32[]{:S(2)}) collective-permute-start(bf16[2,4,1,16,512]{4,3,2,1,0:T(8,128)(2,1)S(1)} %get-tuple-element.22), channel_id=1, source_target_pairs={{0,1},{1,2},{2,3},{3,4},{4,5},{5,6},{6,7},{7,8},{8,9},{9,10},{10,1... | collective-permute-start | bytes 393224 | tf_op jit(solution)/shard_map/ppermute | solution.py:42
  12.4 18.1 %collective-permute-start.1 = (bf16[2,4,1,16,512]{4,3,2,1,0:T(8,128)(2,1)S(1)}, bf16[2,4,1,16,512]{4,3,2,1,0:T(8,128)(2,1)S(1)}, u32[]{:S(2)}, u32[]{:S(2)}) collective-permute-start(bf16[2,4,1,16,512]{4,3,2,1,0:T(8,128)(2,1)S(1)} %get-tuple-element.23), channel_id=1, source_target_pairs={{1,0},{2,1},{3,2},{4,3},{5,4},{6,5},{7,6},{8,7},{9,8},{10,9},{11,1... | collective-permute-start | bytes 393224 | tf_op jit(solution)/shard_map/ppermute | solution.py:43
  17.8 34.4 %all-to-all-start = ((bf16[8,64,256]{2,1,0:T(8,128)(2,1)}), bf16[8,64,256]{2,1,0:T(8,128)(2,1)S(1)}, u32[]{:S(2)}, u32[]{:S(2)}) async-start(bf16[8,64,256]{2,1,0:T(8,128)(2,1)} %broadcast_in_dim.25), calls=%async_computation | async-start | bytes 524288 | tf_op jit(solution)/shard_map/all_to_all | solution.py:26
  33.4 9.6 %collective-permute-start.4 = (bf16[2,4,4,16,128]{4,3,2,1,0:T(8,128)(2,1)S(1)}, bf16[2,4,4,16,128]{4,3,2,1,0:T(8,128)(2,1)S(1)}, u32[]{:S(2)}, u32[]{:S(2)}) collective-permute-start(bf16[2,4,4,16,128]{4,3,2,1,0:T(8,128)(2,1)S(1)} %get-tuple-element.17), channel_id=1, source_target_pairs={{0,192},{64,128},{128,64},{192,0},{1,193},{65,129},{129,65},{193,1... | collective-permute-start | bytes 393224 | tf_op jit(solution)/shard_map/ppermute | solution.py:67
  37.9 5.1 %collective-permute-start.2 = (bf16[2,4,4,16,128]{4,3,2,1,0:T(8,128)(2,1)S(1)}, bf16[2,4,4,16,128]{4,3,2,1,0:T(8,128)(2,1)S(1)}, u32[]{:S(2)}, u32[]{:S(2)}) collective-permute-start(bf16[2,4,4,16,128]{4,3,2,1,0:T(8,128)(2,1)S(1)} %get-tuple-element.19), channel_id=1, source_target_pairs={{0,64},{64,0},{128,192},{192,128},{1,65},{65,1},{129,193},{193,129... | collective-permute-start | bytes 393224 | tf_op jit(solution)/shard_map/ppermute | solution.py:67
  39.8 6.5 %collective-permute-start.3 = (bf16[2,4,4,16,128]{4,3,2,1,0:T(8,128)(2,1)S(1)}, bf16[2,4,4,16,128]{4,3,2,1,0:T(8,128)(2,1)S(1)}, u32[]{:S(2)}, u32[]{:S(2)}) collective-permute-start(bf16[2,4,4,16,128]{4,3,2,1,0:T(8,128)(2,1)S(1)} %get-tuple-element.18), channel_id=1, source_target_pairs={{0,128},{64,192},{128,0},{192,64},{1,129},{65,193},{129,1},{193,65... | collective-permute-start | bytes 393224 | tf_op jit(solution)/shard_map/ppermute | solution.py:67
  46.4 5.7 %collective-permute-start.5 = (bf16[2,2,4,16,128]{4,3,2,1,0:T(8,128)(2,1)S(1)}, bf16[2,2,4,16,128]{4,3,2,1,0:T(8,128)(2,1)S(1)}, u32[]{:S(2)}, u32[]{:S(2)}) collective-permute-start(bf16[2,2,4,16,128]{4,3,2,1,0:T(8,128)(2,1)S(1)} %slice.195), channel_id=1, source_target_pairs={{0,256},{1,257},{2,258},{3,259},{4,260},{5,261},{6,262},{7,263},{8... | collective-permute-start | bytes 196616 | tf_op jit(solution)/shard_map/ppermute | solution.py:105
  52.9 13.3 %all-to-all-start.1 = ((f32[8,1,128]{2,1,0:T(1,128)}), f32[8,1,128]{2,1,0:T(1,128)S(1)}, u32[]{:S(2)}, u32[]{:S(2)}) async-start(f32[8,1,128]{2,1,0:T(1,128)} %broadcast_in_dim.26), calls=%async_computation.1 | async-start | bytes 8192 | tf_op jit(solution)/shard_map/all_to_all | solution.py:26
  66.8 13.3 %all-to-all-start.2 = ((f32[8,1,128]{2,1,0:T(1,128)}), f32[8,1,128]{2,1,0:T(1,128)S(1)}, u32[]{:S(2)}, u32[]{:S(2)}) async-start(f32[8,1,128]{2,1,0:T(1,128)} %broadcast_in_dim.27), calls=%async_computation.2 | async-start | bytes 8192 | tf_op jit(solution)/shard_map/all_to_all | solution.py:26
  75.5 38.0 %all-gather.2.cloned.1.call-start = ((), (), s32[]{:S(2)}) async-start(), calls=%async_computation.3 | async-start | bytes 2064384 | tf_op jit(solution)/shard_map/all_gather | solution.py:95
  119.2 8.3 %collective-permute-start.6 = (f32[2,2,4,2,16,256]{5,4,3,2,1,0:T(8,128)S(1)}, f32[2,2,4,2,16,256]{5,4,3,2,1,0:T(8,128)S(1)}, u32[]{:S(2)}, u32[]{:S(2)}) collective-permute-start(f32[2,2,4,2,16,256]{5,4,3,2,1,0:T(8,128)S(1)} %dynamic-slice_bitcast_fusion), channel_id=1, source_target_pairs={{0,64},{64,0},{1,65},{65,1},{2,66},{66,2},{3,67},{67,3},{4,68},{68... | collective-permute-start | bytes 1572872 | tf_op jit(solution)/shard_map/ppermute | solution.py:142
  127.6 9.4 %collective-permute-start.7 = (f32[2,4,2,16,256]{4,3,2,1,0:T(8,128)S(1)}, f32[2,4,2,16,256]{4,3,2,1,0:T(8,128)S(1)}, u32[]{:S(2)}, u32[]{:S(2)}) collective-permute-start(f32[2,4,2,16,256]{4,3,2,1,0:T(8,128)S(1)} %dynamic-slice_bitcast_fusion.1), channel_id=1, source_target_pairs={{0,128},{128,0},{1,129},{129,1},{2,130},{130,2},{3,131},{131,3},{4... | collective-permute-start | bytes 786440 | tf_op jit(solution)/shard_map/ppermute | solution.py:144
Sparse Core Ops, SparseCore 0:
  78.4 35.0 all-gather.1

commit v2 on v1

v2 whole, which is shorter than its diff:
```python
import functools

import jax
import jax.numpy as jnp
from jax import lax
from jax.experimental import pallas as pl
from jax.experimental.pallas import tpu as pltpu
from jax.sharding import Mesh
from jax.sharding import PartitionSpec as P

GROUPS = 32
EPS = 1e-06
TM = ("x", "core")
TILE = ("y", "z")
SPANS = 8
VIDEOS = 2
FRAMES = 4
COLS = 16
SHARE = 64
ROWS = 4
WIDE = ROWS * SHARE
OUT = 256


def three_parts(value):
    high = lax.reduce_precision(value, 8, 7)
    rest = value - high
    middle = lax.reduce_precision(rest, 8, 7)
    low = rest - middle
    return jnp.stack([high, middle, low]).astype(jnp.bfloat16)


def to_all(block, axis):
    count = lax.axis_size(axis)
    copies = jnp.broadcast_to(block[None], (count,) + block.shape)
    return lax.all_to_all(copies, axis, 0, 0, tiled=True)


def local_sums(features, present):
    videos, channels = features.shape[0], features.shape[-1]
    masked = features.astype(jnp.float32) * present[:, :, None, None, None]
    linear = jnp.sum(masked, axis=(1, 2, 3)).reshape(videos, GROUPS, channels // GROUPS)
    square = jnp.sum(masked * masked, axis=(1, 2, 3)).reshape(videos, GROUPS, channels // GROUPS)
    return jnp.stack([jnp.sum(linear, axis=2), jnp.sum(square, axis=2)])


def with_rows(features):
    place, count = lax.axis_index(TILE), lax.axis_size(TILE)
    forward = [(i, i + 1) for i in range(count - 1)]
    backward = [(i + 1, i) for i in range(count - 1)]
    first, last = features[:, :, 0], features[:, :, 1]
    low = lax.ppermute(last, TILE, forward)
    high = lax.ppermute(first, TILE, backward)
    low = jnp.where(place == 0, first, low)
    high = jnp.where(place == count - 1, last, high)
    return low, first, last, high


def by_member(low, first, last, high):
    channels = low.shape[-1]
    pairs = jnp.stack(
        [jnp.concatenate([low, first], axis=-1), jnp.concatenate([last, high], axis=-1)]
    )
    pairs = pairs.reshape(-1, 2 * channels)
    column = jnp.arange(2 * channels, dtype=jnp.int32)
    member, row, tile = column // (2 * SHARE), column // SHARE % 2, column % SHARE
    source = row * channels + tile * SPANS + member
    chosen = (column[:, None] == source[None, :]).astype(jnp.bfloat16)
    flat = jnp.dot(pairs, chosen, preferred_element_type=jnp.float32).astype(jnp.bfloat16)
    flat = flat.reshape(2, -1, SPANS, 2 * SHARE).transpose(2, 1, 0, 3)
    return flat.reshape(SPANS, -1, WIDE)


def conv_kernel(
    lengths, core, totals, gain, bias, signal, weights, send, keep, shifted, *, cells
):
    summed = [totals[0:1, :]]
    for span in range(1, SPANS):
        summed.append(summed[-1] + totals[span : span + 1, :])
    summed = jnp.concatenate(summed, axis=0)
    entry = lax.broadcasted_iota(jnp.int32, (128, WIDE), 0)
    group = lax.broadcasted_iota(jnp.int32, (128, WIDE), 1) % SHARE // 2
    ends = (lax.broadcasted_iota(jnp.int32, (SPANS, WIDE), 0) + 1) * FRAMES

    def spread(which):
        chosen = (entry == group + which * GROUPS).astype(jnp.float32)
        return jnp.dot(
            summed, chosen, precision=lax.Precision.HIGHEST, preferred_element_type=jnp.float32
        )

    offset = bias[...].reshape(1, 1, WIDE)
    for video in range(VIDEOS):
        seen = jnp.minimum(ends, lengths[video]).astype(jnp.float32) * cells
        centre = spread(video) / seen
        scale = lax.rsqrt(spread(VIDEOS + video) / seen - centre * centre + EPS) * gain[...]
        for span in range(SPANS):
            block = signal[span, video * FRAMES : (video + 1) * FRAMES].astype(jnp.float32)
            block = (block - centre[span : span + 1].reshape(1, 1, WIDE)) * scale[
                span : span + 1
            ].reshape(1, 1, WIDE) + offset
            block = block / (1.0 + jnp.exp(-block))
            frame = lax.broadcasted_iota(jnp.int32, block.shape, 0) + span * FRAMES
            block = jnp.where(frame < lengths[video], block, 0.0)
            left = jnp.concatenate([block[:, :1], block[:, :-1]], axis=1).astype(jnp.bfloat16)
            right = jnp.concatenate([block[:, 1:], block[:, -1:]], axis=1).astype(jnp.bfloat16)
            place = slice(2 + span * FRAMES, 2 + (span + 1) * FRAMES)
            for side, value in enumerate((left, block.astype(jnp.bfloat16), right)):
                shifted[side, video, place] = value
                if span == 0:
                    shifted[side, video, 0] = value[0]
                    shifted[side, video, 1] = value[0]

    pieces = SPANS // 2
    for target, parity in ((send, 1 - core[0]), (keep, core[0])):
        for half in range(2):
            rows = slice(SHARE, SHARE + WIDE) if half == 0 else slice(0, WIDE)
            total = None
            for tap in range(10):
                blocks = []
                for piece in range(pieces):
                    span = 2 * piece + parity
                    for video in range(VIDEOS):
                        if tap < 9:
                            blocks.append(
                                shifted[tap % 3, video, pl.ds(span * FRAMES + tap // 3, FRAMES)]
                            )
                        else:
                            blocks.append(signal[span, video * FRAMES : (video + 1) * FRAMES])
                left = jnp.concatenate(blocks, axis=0).reshape(-1, WIDE)
                term = jnp.dot(left, weights[tap, rows, :], preferred_element_type=jnp.float32)
                total = term if total is None else total + term
            target[:, :, half * OUT : (half + 1) * OUT] = total.reshape(pieces, -1, OUT)


def per_device(features, lengths, gain_in, bias_in, conv_in, skip_weight):
    videos, frames, row_count, col_count, wide_in = features.shape
    span, core = lax.axis_index(TM), lax.axis_index("core")
    tiles = lax.axis_size(TILE)
    taps = conv_in.shape[1]

    stamps = span * frames + jnp.arange(frames, dtype=jnp.int32)
    present = (stamps[None, :] < lengths[:, None]).astype(jnp.float32)
    sums = local_sums(features, present)

    weights = jnp.concatenate([conv_in, skip_weight[:, None, :]], axis=1)
    weights = lax.dynamic_index_in_dim(weights, span, 0, False)
    parts = three_parts(sums.reshape(-1)).reshape(-1)
    parts = jnp.pad(parts, (0, 4 * OUT - parts.shape[0])).reshape(4, OUT)
    arrived = to_all(jnp.concatenate([weights, parts], axis=0), TILE)

    signal = lax.all_to_all(by_member(*with_rows(features)), TM, 0, 0, tiled=True)
    signal = signal.reshape(SPANS, videos * frames, col_count, WIDE)

    parts = arrived[:, taps + 1 :].astype(jnp.float32).reshape(tiles, -1)[:, : 3 * sums.size]
    sums = jnp.sum(parts.reshape(tiles, 3, sums.size), axis=(0, 1)).reshape(1, -1)
    totals = to_all(sums, TM).reshape(SPANS, -1)

    conv = arrived[:, :taps].reshape(tiles, 3, 3, 3, OUT).transpose(1, 3, 2, 0, 4)
    conv = jnp.pad(conv.reshape(9, 3 * SHARE, OUT), ((0, 0), (SHARE, SHARE), (0, 0)))
    skip = jnp.pad(arrived[:, taps][None], ((0, 0), (2 * SHARE, 2 * SHARE), (0, 0)))
    weights = jnp.concatenate([conv, skip], axis=0)

    def lanes(vector):
        own = lax.dynamic_index_in_dim(vector.reshape(SHARE, SPANS), span, 1, False)
        return jnp.tile(own, ROWS).reshape(1, WIDE)

    cells = float(row_count * tiles * col_count * (wide_in // GROUPS))
    shape = jax.ShapeDtypeStruct((SPANS // 2, videos * frames * col_count, 2 * OUT), jnp.float32)
    on_chip = pl.BlockSpec(memory_space=pltpu.VMEM)
    scalar = pl.BlockSpec(memory_space=pltpu.SMEM)
    send, keep = pl.pallas_call(
        functools.partial(conv_kernel, cells=cells),
        out_shape=(shape, shape),
        in_specs=[scalar, scalar] + [on_chip] * 5,
        out_specs=(on_chip, on_chip),
        scratch_shapes=[
            pltpu.VMEM((3, videos, SPANS * frames + 2, col_count, WIDE), jnp.bfloat16)
        ],
        compiler_params=pltpu.CompilerParams(vmem_limit_bytes=40 * 1024 * 1024),
        cost_estimate=pl.CostEstimate(
            flops=2 * 10 * 1024 * 256 * 512, bytes_accessed=6 << 20, transcendentals=1 << 19
        ),
        name="norm_conv",
    )(lengths, core.reshape(1), totals, lanes(gain_in), lanes(bias_in), signal, weights)

    total = keep + lax.ppermute(send, "core", [(0, 1), (1, 0)])
    total = jnp.sum(lax.all_to_all(total, "x", 0, 0, tiled=True), axis=0)
    total = total.reshape(videos, frames, col_count, row_count, OUT).transpose(0, 1, 3, 2, 4)
    return (total * present[:, :, None, None, None]).astype(jnp.bfloat16)


def solution(mesh):
    spans, tiles = mesh.devices.shape
    fine = Mesh(mesh.devices.reshape(spans // 2, 2, 8, tiles // 8), TM + TILE)
    placed = (
        P(None, TM, TILE, None, None),
        P(),
        P(),
        P(),
        P(TILE, None, None),
        P(TILE, None),
    )
    return jax.shard_map(
        per_device,
        mesh=fine,
        in_specs=placed,
        out_specs=P(None, TM, TILE, None, None),
        check_vma=False,
    )
```

time: 145 us -> 107 us (0.74)
  the two profiles are of different devices: /device:TPU:1 before, /device:TPU:24 now
where the time goes in v2:
time: 107 us
  waiting for transfers between devices  38.9 us (36%)
  starting transfers between devices  33.9 us (32%)
  blocking collectives  18.1 us (17%)
  local copies, waits for them, and re-layouts  7.55 us (7%)
  Pallas kernels  4.3 us (4%)
  other arithmetic  2.86 us (3%)
    ppermute x1, waiting for transfers between devices, with_rows(): low = lax.ppermute(last, TILE, forward)  22.4 us
    all_to_all x2, starting transfers between devices, to_all(): return lax.all_to_all(copies, axis, 0, 0, tiled=True)  19.7 us
    all_to_all x1, blocking collectives, per_device(): total = jnp.sum(lax.all_to_all(total, 'x', 0, 0, tiled=True), axis=0)  18.1 us
    all_to_all x1, waiting for transfers between devices, per_device(): lax.all_to_all(by_member(*with_rows(features)), TM, 0, 0, tiled=True)  8.94 us
    all_to_all x2, waiting for transfers between devices, to_all(): return lax.all_to_all(copies, axis, 0, 0, tiled=True)  4.98 us
    ppermute x1, starting transfers between devices, with_rows(): high = lax.ppermute(first, TILE, backward)  4.57 us
    pallas_call x1, Pallas kernels, per_device(): pl.pallas_call(functools.partial(conv_kernel, cells=cells), out_shape=(sh...  4.3 us
    all_to_all x1, starting transfers between devices, per_device(): lax.all_to_all(by_member(*with_rows(features)), TM, 0, 0, tiled=True)  4.29 us
  transfers between devices with their start and end apart: 6, of which 4 were waited for; matrix products, arithmetic and copies ran while one was open for 4% of the time, Pallas kernels for 0%

profile of v2, /device:TPU:24, one launch (start us, length us, event | category | flops | bytes accessed | tf_op | source)
XLA Modules:
  0.0 106.9 jit_solution(7483538566517308589)
XLA Ops:
  0.0 0.7 copy.39
  0.7 0.7 compare_convert_fusion
  1.4 1.1 %fusion.7 = (f32[2,512]{1,0:T(2,128)S(1)}, f32[2,512]{1,0:T(2,128)S(1)}) fusion(bf16[2,4,2,16,512]{4,3,2,1,0:T(8,128)(2,1)} %param.6, f32[2,4]{1,0:T(2,128)S(1)} %compare_convert_fusion), kind=kLoop, calls=%fused_computation.14 | loop fusion | flops 653312 | bytes 270368 | tf_op jit(solution)/shard_map/reduce_sum | solution.py:42
  2.7 0.1 reduce_sum.62
  2.8 0.1 reduce_sum.64
  3.1 0.9 copy.38
  4.0 1.1 %broadcast_in_dim.7 = bf16[64,32,256]{2,1,0:T(8,128)(2,1)} broadcast(bf16[32,256]{1,0:T(8,128)(2,1)S(1)} %pad_maximum_fusion.1), dimensions={1,2} | broadcast | bytes 1064960 | tf_op jit(solution)/shard_map/broadcast_in_dim | solution.py:35
  5.1 16.4 %all-to-all-start = ((bf16[64,32,256]{2,1,0:T(8,128)(2,1)}), bf16[64,32,256]{2,1,0:T(8,128)(2,1)S(1)}, u32[]{:S(2)}, u32[]{:S(2)}) async-start(bf16[64,32,256]{2,1,0:T(8,128)(2,1)} %broadcast_in_dim.7), calls=%async_computation | async-start | bytes 2097152 | tf_op jit(solution)/shard_map/all_to_all | solution.py:36
  21.6 3.4 %collective-permute-start = (bf16[2,4,16,512]{3,2,1,0:T(8,128)(2,1)S(1)}, bf16[2,4,16,512]{3,2,1,0:T(8,128)(2,1)S(1)}, u32[]{:S(2)}, u32[]{:S(2)}) collective-permute-start(bf16[2,4,16,512]{3,2,1,0:T(8,128)(2,1)S(1)} %get-tuple-element.13), channel_id=1, source_target_pairs={{0,1},{1,2},{2,3},{3,4},{4,5},{5,6},{6,7},{7,8},{8,9},{9,10},{10,1... | collective-permute-start | bytes 393224 | tf_op jit(solution)/shard_map/ppermute | solution.py:52
  25.0 4.6 %collective-permute-start.1 = (bf16[2,4,16,512]{3,2,1,0:T(8,128)(2,1)S(1)}, bf16[2,4,16,512]{3,2,1,0:T(8,128)(2,1)S(1)}, u32[]{:S(2)}, u32[]{:S(2)}) collective-permute-start(bf16[2,4,16,512]{3,2,1,0:T(8,128)(2,1)S(1)} %get-tuple-element.14), channel_id=1, source_target_pairs={{1,0},{2,1},{3,2},{4,3},{5,4},{6,5},{7,6},{8,7},{9,8},{10,9},{11,1... | collective-permute-start | bytes 393224 | tf_op jit(solution)/shard_map/ppermute | solution.py:53
  29.6 22.4 %collective-permute-done = bf16[2,4,16,512]{3,2,1,0:T(8,128)(2,1)S(1)} collective-permute-done((bf16[2,4,16,512]{3,2,1,0:T(8,128)(2,1)S(1)}, bf16[2,4,16,512]{3,2,1,0:T(8,128)(2,1)S(1)}, u32[]{:S(2)}, u32[]{:S(2)}) %collective-permute-start) | collective-permute-done | bytes 131104 | tf_op jit(solution)/shard_map/ppermute | solution.py:52
  52.1 1.0 fusion.6
  53.1 0.1 copy.50
  53.3 0.5 copy.41
  53.8 1.1 %reshape.185 = bf16[8,128,256]{2,1,0:T(8,128)(2,1)} reshape(bf16[8,128,2,128]{3,2,1,0:T(2,128)(2,1)S(1)} %copy.41) | data formatting | bytes 1048576 | tf_op jit(solution)/shard_map/reshape | solution.py:71
  55.0 4.3 %all-to-all-start.2 = ((bf16[8,128,256]{2,1,0:T(8,128)(2,1)}), bf16[8,128,256]{2,1,0:T(8,128)(2,1)S(1)}, u32[]{:S(2)}, u32[]{:S(2)}) async-start(bf16[8,128,256]{2,1,0:T(8,128)(2,1)} %reshape.185), calls=%async_computation.2 | async-start | bytes 1048576 | tf_op jit(solution)/shard_map/all_to_all | solution.py:151
  59.5 0.2 dynamic-slice_reduce_fusion
  60.0 0.5 copy.47
  60.7 8.9 %all-to-all-done.2 = bf16[8,128,256]{2,1,0:T(8,128)(2,1)S(1)} async-done(((bf16[8,128,256]{2,1,0:T(8,128)(2,1)}), bf16[8,128,256]{2,1,0:T(8,128)(2,1)S(1)}, u32[]{:S(2)}, u32[]{:S(2)}) %all-to-all-start.2) | async-done | bytes 524320 | tf_op jit(solution)/shard_map/all_to_all | solution.py:151
  69.6 0.6 broadcast_in_dim.8
  70.2 3.3 %all-to-all-start.1 = ((f32[8,1,128]{2,1,0:T(1,128)}), f32[8,1,128]{2,1,0:T(1,128)S(1)}, u32[]{:S(2)}, u32[]{:S(2)}) async-start(f32[8,1,128]{2,1,0:T(1,128)} %broadcast_in_dim.8), calls=%async_computation.1 | async-start | bytes 8192 | tf_op jit(solution)/shard_map/all_to_all | solution.py:36
  73.5 0.1 fusion.4.weights
  73.7 5.0 %all-to-all-done.1 = f32[8,1,128]{2,1,0:T(1,128)S(1)} async-done(((f32[8,1,128]{2,1,0:T(1,128)}), f32[8,1,128]{2,1,0:T(1,128)S(1)}, u32[]{:S(2)}, u32[]{:S(2)}) %all-to-all-start.1) | async-done | bytes 4128 | tf_op jit(solution)/shard_map/all_to_all | solution.py:36
  78.7 4.3 %norm_conv.1 = (f32[4,128,512]{2,1,0:T(8,128)S(1)}, f32[4,128,512]{2,1,0:T(8,128)S(1)}) custom-call(s32[2]{0:T(128)S(1)} %copy-done, s32[1]{0:T(128)} %bitcast.core, f32[8,128]{1,0:T(8,128)S(1)} %bitcast.49, f32[1,256]{1,0:T(1,128)S(1)} %reshape_tile.6.gain, f32[1,256]{1,0:T(1,128)S(1)} %reshape_tile.7.bias, bf16[8,8,16,256]{3,2,1,0:T(8,128)(2,1)S(1)} %bitcast.48, ...), custom_call_target="tpu_custom_call" | custom-call | flops 2684354560 | bytes 6291456 | tf_op jit(solution)/shard_map/norm_conv/pallas_call | solution.py:171
  83.0 1.9 %collective-permute-start.2 = (f32[4,128,512]{2,1,0:T(8,128)S(1)}, f32[4,128,512]{2,1,0:T(8,128)S(1)}, u32[]{:S(2)}, u32[]{:S(2)}) collective-permute-start(f32[4,128,512]{2,1,0:T(8,128)S(1)} %get-tuple-element.8), channel_id=1, source_target_pairs={{0,64},{64,0},{1,65},{65,1},{2,66},{66,2},{3,67},{67,3},{4,68},{68... | collective-permute-start | bytes 3145736 | tf_op jit(solution)/shard_map/ppermute | solution.py:186
  84.9 2.6 %collective-permute-done.2 = f32[4,128,512]{2,1,0:T(8,128)S(1)} collective-permute-done((f32[4,128,512]{2,1,0:T(8,128)S(1)}, f32[4,128,512]{2,1,0:T(8,128)S(1)}, u32[]{:S(2)}, u32[]{:S(2)}) %collective-permute-start.2) | collective-permute-done | bytes 1048608 | tf_op jit(solution)/shard_map/ppermute | solution.py:186
  87.5 0.2 add.83
  87.7 18.1 %all_to_all.20 = f32[4,128,512]{2,1,0:T(8,128)S(1)} all-to-all(f32[4,128,512]{2,1,0:T(8,128)S(1)} %add.83), channel_id=1, replica_groups=mesh['x'=4,'core'=2,'y'=8,'z'=8] {'x'}, dimensions={0} | all-to-all | bytes 2097152 | tf_op jit(solution)/shard_map/all_to_all | solution.py:187
  105.8 0.1 reduce_sum.68
  105.9 0.2 reshape.189
  106.1 0.2 fusion.8
  106.3 0.7 copy.45
  (40 shorter events, 1.2 us)
Async XLA Ops:
  4.0 17.6 %copy-start.1 = (bf16[2,4,2,16,512]{4,3,2,1,0:T(8,128)(2,1)S(1)}, bf16[2,4,2,16,512]{4,3,2,1,0:T(8,128)(2,1)}, u32[]{:S(2)}) copy-start(bf16[2,4,2,16,512]{4,3,2,1,0:T(8,128)(2,1)} %param.6) | copy-start | bytes 786436
  5.1 49.8 %all-to-all-start = ((bf16[64,32,256]{2,1,0:T(8,128)(2,1)}), bf16[64,32,256]{2,1,0:T(8,128)(2,1)S(1)}, u32[]{:S(2)}, u32[]{:S(2)}) async-start(bf16[64,32,256]{2,1,0:T(8,128)(2,1)} %broadcast_in_dim.7), calls=%async_computation | async-start | bytes 2097152 | tf_op jit(solution)/shard_map/all_to_all | solution.py:36
  21.6 30.4 %collective-permute-start = (bf16[2,4,16,512]{3,2,1,0:T(8,128)(2,1)S(1)}, bf16[2,4,16,512]{3,2,1,0:T(8,128)(2,1)S(1)}, u32[]{:S(2)}, u32[]{:S(2)}) collective-permute-start(bf16[2,4,16,512]{3,2,1,0:T(8,128)(2,1)S(1)} %get-tuple-element.13), channel_id=1, source_target_pairs={{0,1},{1,2},{2,3},{3,4},{4,5},{5,6},{6,7},{7,8},{8,9},{9,10},{10,1... | collective-permute-start | bytes 393224 | tf_op jit(solution)/shard_map/ppermute | solution.py:52
  25.0 27.0 %collective-permute-start.1 = (bf16[2,4,16,512]{3,2,1,0:T(8,128)(2,1)S(1)}, bf16[2,4,16,512]{3,2,1,0:T(8,128)(2,1)S(1)}, u32[]{:S(2)}, u32[]{:S(2)}) collective-permute-start(bf16[2,4,16,512]{3,2,1,0:T(8,128)(2,1)S(1)} %get-tuple-element.14), channel_id=1, source_target_pairs={{1,0},{2,1},{3,2},{4,3},{5,4},{6,5},{7,6},{8,7},{9,8},{10,9},{11,1... | collective-permute-start | bytes 393224 | tf_op jit(solution)/shard_map/ppermute | solution.py:53
  53.3 6.0 %copy-start.2 = (f32[512]{0:T(512)S(1)}, f32[512]{0:T(512)}, u32[]{:S(2)}) copy-start(f32[512]{0:T(512)} %param.8) | copy-start | bytes 6148
  53.3 6.1 %copy-start.3 = (f32[512]{0:T(512)S(1)}, f32[512]{0:T(512)}, u32[]{:S(2)}) copy-start(f32[512]{0:T(512)} %param.9) | copy-start | bytes 6148
  55.0 14.6 %all-to-all-start.2 = ((bf16[8,128,256]{2,1,0:T(8,128)(2,1)}), bf16[8,128,256]{2,1,0:T(8,128)(2,1)S(1)}, u32[]{:S(2)}, u32[]{:S(2)}) async-start(bf16[8,128,256]{2,1,0:T(8,128)(2,1)} %reshape.185), calls=%async_computation.2 | async-start | bytes 1048576 | tf_op jit(solution)/shard_map/all_to_all | solution.py:151
  60.6 18.0 %copy-start = (s32[2]{0:T(128)S(1)}, s32[2]{0:T(128)}, u32[]{:S(2)}) copy-start(s32[2]{0:T(128)} %lengths.1) | copy-start | bytes 28
  70.2 8.4 %all-to-all-start.1 = ((f32[8,1,128]{2,1,0:T(1,128)}), f32[8,1,128]{2,1,0:T(1,128)S(1)}, u32[]{:S(2)}, u32[]{:S(2)}) async-start(f32[8,1,128]{2,1,0:T(1,128)} %broadcast_in_dim.8), calls=%async_computation.1 | async-start | bytes 8192 | tf_op jit(solution)/shard_map/all_to_all | solution.py:36
  83.0 4.6 %collective-permute-start.2 = (f32[4,128,512]{2,1,0:T(8,128)S(1)}, f32[4,128,512]{2,1,0:T(8,128)S(1)}, u32[]{:S(2)}, u32[]{:S(2)}) collective-permute-start(f32[4,128,512]{2,1,0:T(8,128)S(1)} %get-tuple-element.8), channel_id=1, source_target_pairs={{0,64},{64,0},{1,65},{65,1},{2,66},{66,2},{3,67},{67,3},{4,68},{68... | collective-permute-start | bytes 3145736 | tf_op jit(solution)/shard_map/ppermute | solution.py:186

commit v3 on v2

v3 whole, which is shorter than its diff:
```python
import functools

import jax
import jax.numpy as jnp
from jax import lax
from jax.experimental import pallas as pl
from jax.experimental.pallas import tpu as pltpu
from jax.sharding import Mesh
from jax.sharding import PartitionSpec as P

GROUPS = 32
EPS = 1e-06
TM = ("x", "core")
TILE = ("y", "z")
SPANS = 8
VIDEOS = 2
FRAMES = 4
COLS = 16
SHARE = 64
ROWS = 4
WIDE = ROWS * SHARE
OUT = 256


def to_all(block, axis):
    count = lax.axis_size(axis)
    copies = jnp.broadcast_to(block[None], (count,) + block.shape)
    return lax.all_to_all(copies, axis, 0, 0, tiled=True)


def payload_kernel(features, conv, skip, lengths, copies, planes, taps, skips, valid, rows, done):
    moves = [
        pltpu.make_async_copy(source, target, done.at[index])
        for index, (source, target) in enumerate(
            ((features, planes), (conv, taps), (skip, skips), (lengths, valid))
        )
    ]
    for move in moves:
        move.start()
    for move in moves:
        move.wait()
    count, channels = taps.shape[0], planes.shape[-1]
    span = lax.axis_index(TM)
    pick = lax.broadcasted_iota(jnp.int32, (count, SPANS, OUT), 1) == span
    rows[...] = jnp.zeros_like(rows)
    rows[0:count, :] = jnp.sum(jnp.where(pick, taps[...].astype(jnp.float32), 0.0), axis=1)
    pick = lax.broadcasted_iota(jnp.int32, (SPANS, OUT), 0) == span
    rows[count : count + 1, :] = jnp.sum(
        jnp.where(pick, skips[...].astype(jnp.float32), 0.0), axis=0, keepdims=True
    )
    group = lax.broadcasted_iota(jnp.int32, (channels, 128), 0) // (channels // GROUPS)
    lane = lax.broadcasted_iota(jnp.int32, (channels, 128), 1)
    sums = jnp.zeros((1, 128), jnp.float32)
    for video in range(VIDEOS):
        linear = jnp.zeros((1, channels), jnp.float32)
        square = jnp.zeros((1, channels), jnp.float32)
        for frame in range(FRAMES):
            block = planes[video * FRAMES + frame].astype(jnp.float32)
            shown = (span * FRAMES + frame < valid[video]).astype(jnp.float32)
            linear += jnp.sum(block, axis=0, keepdims=True) * shown
            square += jnp.sum(block * block, axis=0, keepdims=True) * shown
        for which, value in ((video, linear), (VIDEOS + video, square)):
            chosen = (lane == group + which * GROUPS).astype(jnp.float32)
            sums += jnp.dot(
                value, chosen, precision=lax.Precision.HIGHEST, preferred_element_type=jnp.float32
            )
    high = sums.astype(jnp.bfloat16).astype(jnp.float32)
    middle = (sums - high).astype(jnp.bfloat16).astype(jnp.float32)
    rows[count + 1 : count + 2, 0:128] = high
    rows[count + 1 : count + 2, 128:256] = middle
    rows[count + 2 : count + 3, 0:128] = sums - high - middle
    value = rows[...].astype(jnp.bfloat16)
    for index in range(copies.shape[0]):
        copies[index] = value


def member_kernel(features, kept, sent):
    voxels, channels = features.shape[0] * COLS, features.shape[-1]
    column = lax.broadcasted_iota(jnp.int32, (channels, 2 * channels), 1)
    source = column % SHARE * SPANS + column // (2 * SHARE)
    match = lax.broadcasted_iota(jnp.int32, (channels, 2 * channels), 0) == source
    second = column // SHARE % 2 == 1
    left = jnp.where(match & ~second, 1.0, 0.0).astype(jnp.bfloat16)
    right = jnp.where(match & second, 1.0, 0.0).astype(jnp.bfloat16)
    first = features[:, :COLS].reshape(voxels, channels)
    last = features[:, COLS:].reshape(voxels, channels)
    flat = jnp.dot(first, left, preferred_element_type=jnp.float32)
    flat = flat + jnp.dot(last, right, preferred_element_type=jnp.float32)
    flat = flat.astype(jnp.bfloat16)
    even = lax.axis_index("core") == 0
    for chip in range(SPANS // 2):
        zero = flat[:, chip * 256 : chip * 256 + 128]
        one = flat[:, chip * 256 + 128 : chip * 256 + 256]
        kept[chip] = jnp.where(even, zero, one)
        sent[chip] = jnp.where(even, one, zero)


def conv_kernel(
    lengths, totals, gain, bias, own, above, below, weights,
    send, keep, factor, shifted, raw, moments, *, cells, tiles, tap_bound, skip_bound
):
    half = 2 * SHARE
    chips = SPANS // 2
    chip, core = lax.axis_index("x"), lax.axis_index("core")
    tile = lax.axis_index(TILE)
    summed = [totals[0:1, :]]
    for span in range(1, SPANS):
        summed.append(summed[-1] + totals[span : span + 1, :])
    summed = jnp.concatenate(summed, axis=0)
    entry = lax.broadcasted_iota(jnp.int32, (128, half), 0)
    group = lax.broadcasted_iota(jnp.int32, (128, half), 1) % SHARE // 2
    ends = (lax.broadcasted_iota(jnp.int32, (SPANS, half), 0) + 1) * FRAMES

    def spread(which):
        chosen = (entry == group + which * GROUPS).astype(jnp.float32)
        return jnp.dot(
            summed, chosen, precision=lax.Precision.HIGHEST, preferred_element_type=jnp.float32
        )

    ratio = jnp.zeros((SPANS, half), jnp.float32)
    largest = jnp.zeros((SPANS, half), jnp.float32)
    for video in range(VIDEOS):
        seen = jnp.minimum(ends, lengths[video]).astype(jnp.float32) * cells
        square = spread(VIDEOS + video)
        centre = spread(video) / seen
        inverse = lax.rsqrt(square / seen - centre * centre + EPS)
        moments[2 * video] = centre
        moments[2 * video + 1] = inverse * gain[...]
        size = jnp.sqrt(square)
        ratio = jnp.maximum(ratio, size * inverse)
        largest = jnp.maximum(largest, size)
    bound = tap_bound * (3.0 * jnp.max(ratio, keepdims=True) + 3.0)
    bound = bound + skip_bound * jnp.max(largest, keepdims=True)
    factor[...] = jnp.broadcast_to(jnp.exp2(14.0 - jnp.floor(jnp.log2(bound))), factor.shape)

    offset = bias[...].reshape(1, 1, half)
    lane = lax.broadcasted_iota(jnp.int32, (FRAMES, COLS, half), 2)
    for step in range(chips):
        for parity in range(2):
            span = lax.rem(chip - step + chips, chips) * 2 + parity
            start = span * FRAMES
            for video in range(VIDEOS):
                place = slice(video * FRAMES, (video + 1) * FRAMES)
                block = own[2 * step + parity, place]
                raw[video, pl.ds(start, FRAMES)] = block
                block = block.astype(jnp.float32)
                turned = pltpu.roll(block, SHARE, 2)
                upper = jnp.where(tile == 0, turned, above[2 * step + parity, place].astype(jnp.float32))
                lower = jnp.where(
                    tile == tiles - 1, turned, below[2 * step + parity, place].astype(jnp.float32)
                )
                edges = jnp.where(lane < SHARE, lower, upper)
                centre = moments[2 * video, pl.ds(span, 1)].reshape(1, 1, half)
                scale = moments[2 * video + 1, pl.ds(span, 1)].reshape(1, 1, half)
                shown = lax.broadcasted_iota(jnp.int32, block.shape, 0) + start < lengths[video]
                for at, value in enumerate((block, edges)):
                    value = (value - centre) * scale + offset
                    value = value / (1.0 + jnp.exp(-value))
                    value = jnp.where(shown, value, 0.0)
                    left = jnp.concatenate([value[:, :1], value[:, :-1]], axis=1)
                    right = jnp.concatenate([value[:, 1:], value[:, -1:]], axis=1)
                    lanes = slice(at * half, (at + 1) * half)
                    for side, part in enumerate((left, value, right)):
                        shifted[side, video, pl.ds(2 + start, FRAMES), :, lanes] = part.astype(jnp.bfloat16)
    for side in range(3):
        for video in range(VIDEOS):
            shifted[side, video, 0] = shifted[side, video, 2]
            shifted[side, video, 1] = shifted[side, video, 2]

    for target, parity in ((send, 1 - core), (keep, core)):
        for row in range(2):
            place = slice(0, WIDE) if row == 1 else slice(SHARE, SHARE + WIDE)
            total = None
            for tap in range(10):
                blocks = []
                for piece in range(chips):
                    start = (2 * piece + parity) * FRAMES
                    for video in range(VIDEOS):
                        if tap < 9:
                            blocks.append(shifted[tap % 3, video, pl.ds(start + tap // 3, FRAMES)])
                        else:
                            blocks.append(raw[video, pl.ds(start, FRAMES)])
                left = jnp.concatenate(blocks, axis=0)
                if tap < 9:
                    term = jnp.dot(
                        left.reshape(-1, WIDE), weights[tap, place, :], preferred_element_type=jnp.float32
                    )
                else:
                    place = slice(place.start, place.start + half)
                    term = jnp.dot(
                        left.reshape(-1, half), weights[tap, place, :], preferred_element_type=jnp.float32
                    )
                total = term if total is None else total + term
            target[:, :, row * COLS : (row + 1) * COLS, :] = total.reshape(chips, -1, COLS, OUT)


def per_device(features, lengths, gain_in, bias_in, conv_in, skip_weight):
    videos, frames, row_count, col_count, wide_in = features.shape
    span, core, chip = lax.axis_index(TM), lax.axis_index("core"), lax.axis_index("x")
    tiles, chips = lax.axis_size(TILE), lax.axis_size("x")
    taps = conv_in.shape[1]
    on_chip = pl.BlockSpec(memory_space=pltpu.VMEM)
    anywhere = pl.BlockSpec(memory_space=pl.ANY)
    scalar = pl.BlockSpec(memory_space=pltpu.SMEM)
    params = pltpu.CompilerParams(vmem_limit_bytes=40 * 1024 * 1024)
    voxels = videos * frames * col_count

    planes = features.reshape(videos * frames, row_count * col_count, wide_in)
    copies = pl.pallas_call(
        payload_kernel,
        out_shape=jax.ShapeDtypeStruct((tiles, 32, OUT), jnp.bfloat16),
        in_specs=[anywhere] * 4,
        out_specs=on_chip,
        scratch_shapes=[
            pltpu.VMEM(planes.shape, jnp.bfloat16),
            pltpu.VMEM((taps, SPANS, OUT), jnp.bfloat16),
            pltpu.VMEM((SPANS, OUT), jnp.bfloat16),
            pltpu.SMEM((videos,), jnp.int32),
            pltpu.VMEM((32, OUT), jnp.float32),
            pltpu.SemaphoreType.DMA((4,)),
        ],
        compiler_params=params,
        name="payload",
    )(planes, conv_in.transpose(1, 0, 2), skip_weight, lengths)
    arrived = lax.all_to_all(copies, TILE, 0, 0, tiled=True)

    share = jax.ShapeDtypeStruct((chips, voxels, 2 * SHARE), jnp.bfloat16)
    kept, sent = pl.pallas_call(
        member_kernel,
        out_shape=(share, share),
        in_specs=[on_chip],
        out_specs=(on_chip, on_chip),
        compiler_params=params,
        name="member_shares",
    )(planes)
    other = lax.ppermute(sent, "core", [(0, 1), (1, 0)])
    both = jnp.stack([jnp.where(core == 0, kept, other), jnp.where(core == 0, other, kept)], axis=1)
    signal = []
    for step in range(chips):
        block = lax.dynamic_index_in_dim(both, lax.rem(chip + step, chips), 0, False)
        if step:
            block = lax.ppermute(block, "x", [(i, (i + step) % chips) for i in range(chips)])
        signal.append(block)
    signal = jnp.concatenate(signal, axis=0).reshape(SPANS, videos * frames, col_count, 2 * SHARE)
    above = lax.ppermute(signal, TILE, [(i, i + 1) for i in range(tiles - 1)])
    below = lax.ppermute(signal, TILE, [(i + 1, i) for i in range(tiles - 1)])

    parts = jnp.sum(arrived[:, taps + 1 : taps + 3].astype(jnp.float32), axis=0)
    sums = parts[:1, :128] + parts[:1, 128:] + parts[1:, :128]
    totals = to_all(sums, TM).reshape(SPANS, -1)

    conv = arrived[:, :taps].reshape(tiles, 3, 3, 3, OUT).transpose(1, 3, 2, 0, 4)
    conv = conv.reshape(9, 3 * SHARE, OUT)
    conv = jnp.concatenate([jnp.pad(conv, ((0, 0), (0, SHARE), (0, 0))), conv[:, :SHARE]], axis=1)
    skip = jnp.pad(arrived[:, taps][None], ((0, 0), (SHARE, 3 * SHARE), (0, 0)))
    weights = jnp.concatenate([conv, skip], axis=0)

    def lanes(vector):
        own = lax.dynamic_index_in_dim(vector.reshape(SHARE, SPANS), span, 1, False)
        return jnp.tile(own, 2).reshape(1, 2 * SHARE)

    shape = jax.ShapeDtypeStruct((chips, videos * frames, row_count * col_count, OUT), jnp.float32)
    send, keep, factor = pl.pallas_call(
        functools.partial(
            conv_kernel,
            cells=float(row_count * tiles * col_count * (wide_in // GROUPS)),
            tiles=tiles,
            tap_bound=float(taps * SHARE) * 0.0546875,
            skip_bound=float(SHARE) * 0.25,
        ),
        out_shape=(shape, shape, jax.ShapeDtypeStruct((1, OUT), jnp.float32)),
        in_specs=[scalar] + [on_chip] * 7,
        out_specs=(on_chip, on_chip, on_chip),
        scratch_shapes=[
            pltpu.VMEM((3, videos, SPANS * frames + 2, col_count, WIDE), jnp.bfloat16),
            pltpu.VMEM((videos, SPANS * frames, col_count, 2 * SHARE), jnp.bfloat16),
            pltpu.VMEM((2 * videos, SPANS, 2 * SHARE), jnp.float32),
        ],
        compiler_params=params,
        cost_estimate=pl.CostEstimate(
            flops=2 * 10 * 1024 * 256 * 512, bytes_accessed=6 << 20, transcendentals=1 << 19
        ),
        name="norm_conv",
    )(lengths, totals, lanes(gain_in), lanes(bias_in), signal, above, below, weights)

    total = keep + lax.ppermute(send, "core", [(0, 1), (1, 0)])
    total = (total * factor).astype(jnp.float16)
    total = lax.all_to_all(total, "x", 0, 0, tiled=True)
    total = jnp.sum(total.astype(jnp.float32), axis=0) / factor
    total = total.reshape(videos, frames, row_count, col_count, OUT)
    stamps = span * frames + jnp.arange(frames, dtype=jnp.int32)
    present = stamps[None, :] < lengths[:, None]
    return jnp.where(present[:, :, None, None, None], total, 0.0).astype(jnp.bfloat16)


def solution(mesh):
    spans, tiles = mesh.devices.shape
    fine = Mesh(mesh.devices.reshape(spans // 2, 2, 8, tiles // 8), TM + TILE)
    placed = (
        P(None, TM, TILE, None, None),
        P(),
        P(),
        P(),
        P(TILE, None, None),
        P(TILE, None),
    )
    return jax.shard_map(
        per_device,
        mesh=fine,
        in_specs=placed,
        out_specs=P(None, TM, TILE, None, None),
        check_vma=False,
    )
```

time: 107 us -> 88 us (0.82)
  the two profiles are of different devices: /device:TPU:24 before, /device:TPU:1 now
where the time goes in v3:
time: 88 us; the launch traced here: 86.8 us
  starting transfers between devices  50.1 us (57%)
  waiting for transfers between devices  21.6 us (25%)
  Pallas kernels  7.51 us (9%)
  local copies, waits for them, and re-layouts  5 us (6%)
  other arithmetic  2.28 us (3%)
    all_to_all x1, starting transfers between devices, per_device(): arrived = lax.all_to_all(copies, TILE, 0, 0, tiled=True)  17.1 us
    ppermute x3, starting transfers between devices, per_device(): lax.ppermute(block, 'x', [(i, (i + step) % chips) for i in range(chips)])  10.5 us
    all_to_all x1, waiting for transfers between devices, per_device(): total = lax.all_to_all(total, 'x', 0, 0, tiled=True)  9.11 us
    all_to_all x1, starting transfers between devices, to_all(): return lax.all_to_all(copies, axis, 0, 0, tiled=True)  8.18 us
    pallas_call x1, Pallas kernels, per_device(): pl.pallas_call(functools.partial(conv_kernel, cells=float(row_count * til...  4.36 us
    all_to_all x1, waiting for transfers between devices, per_device(): arrived = lax.all_to_all(copies, TILE, 0, 0, tiled=True)  4.04 us
    ppermute x1, starting transfers between devices, per_device(): above = lax.ppermute(signal, TILE, [(i, i + 1) for i in range(tiles - 1)])  4 us
    unnamed x18, local copies, waits for them, and re-layouts  3.73 us
  transfers between devices with their start and end apart: 10, of which 6 were waited for; matrix products, arithmetic and copies ran while one was open for 3% of the time, Pallas kernels for 1%

profile of v3, /device:TPU:1, one launch (start us, length us, event | category | flops | bytes accessed | tf_op | source)
XLA Modules:
  0.0 86.8 jit_solution(18402251446531215935)
XLA Ops:
  0.0 0.9 %copy-done = bf16[2,4,2,16,512]{4,3,2,1,0:T(8,128)(2,1)S(1)} copy-done((bf16[2,4,2,16,512]{4,3,2,1,0:T(8,128)(2,1)S(1)}, bf16[2,4,2,16,512]{4,3,2,1,0:T(8,128)(2,1)}, u32[]{:S(2)}) %copy-start) | copy-done | bytes 262168
  1.0 0.9 %copy-done.2 = bf16[8,27,256]{2,0,1:T(8,128)(2,1)S(1)} copy-done((bf16[8,27,256]{2,0,1:T(8,128)(2,1)S(1)}, bf16[8,27,256]{2,0,1:T(8,128)(2,1)}, u32[]{:S(2)}) %copy-start.2) | copy-done | bytes 110616
  1.9 0.7 copy-done.3
  2.5 0.7 copy-done.4
  3.2 2.5 %payload.1 = bf16[64,32,256]{2,1,0:T(8,128)(2,1)} custom-call(bf16[8,32,512]{2,1,0:T(8,128)(2,1)S(1)} %bitcast.29, bf16[27,8,256]{2,1,0:T(8,128)(2,1)S(1)} %bitcast.31, bf16[8,256]{1,0:T(8,128)(2,1)S(1)} %copy-done.3, s32[2]{0:T(128)S(1)} %copy-done.4), custom_call_target="tpu_custom_call" | custom-call | tf_op jit(solution)/shard_map/payload/pallas_call | solution.py:209
  5.8 17.1 %all-to-all-start = ((bf16[64,32,256]{2,1,0:T(8,128)(2,1)}), bf16[64,32,256]{2,1,0:T(8,128)(2,1)S(1)}, u32[]{:S(2)}, u32[]{:S(2)}) async-start(bf16[64,32,256]{2,1,0:T(8,128)(2,1)} %payload.1), calls=%async_computation | async-start | bytes 2097152 | tf_op jit(solution)/shard_map/all_to_all | solution.py:225
  22.9 0.6 member_shares.1
  23.5 2.9 %collective-permute-start = (bf16[4,128,128]{2,1,0:T(8,128)(2,1)S(1)}, bf16[4,128,128]{2,1,0:T(8,128)(2,1)S(1)}, u32[]{:S(2)}, u32[]{:S(2)}) collective-permute-start(bf16[4,128,128]{2,1,0:T(8,128)(2,1)S(1)} %get-tuple-element.11), channel_id=1, source_target_pairs={{0,64},{64,0},{1,65},{65,1},{2,66},{66,2},{3,67},{67,3},{4,68},{68... | collective-permute-start | bytes 393224 | tf_op jit(solution)/shard_map/ppermute | solution.py:236
  26.4 0.9 %collective-permute-done = bf16[4,128,128]{2,1,0:T(8,128)(2,1)S(1)} collective-permute-done((bf16[4,128,128]{2,1,0:T(8,128)(2,1)S(1)}, bf16[4,128,128]{2,1,0:T(8,128)(2,1)S(1)}, u32[]{:S(2)}, u32[]{:S(2)}) %collective-permute-start) | collective-permute-done | bytes 131104 | tf_op jit(solution)/shard_map/ppermute | solution.py:236
  27.5 3.1 %collective-permute-start.1 = (bf16[2,128,128]{2,1,0:T(8,128)(2,1)S(1)}, bf16[2,128,128]{2,1,0:T(8,128)(2,1)S(1)}, u32[]{:S(2)}, u32[]{:S(2)}) collective-permute-start(bf16[2,128,128]{2,1,0:T(8,128)(2,1)S(1)} %get-tuple-element.16), channel_id=1, source_target_pairs={{0,128},{128,256},{256,384},{384,0},{1,129},{129,257},{257,385},{3... | collective-permute-start | bytes 196616 | tf_op jit(solution)/shard_map/ppermute | solution.py:242
  30.6 4.4 %collective-permute-start.2 = (bf16[2,128,128]{2,1,0:T(8,128)(2,1)S(1)}, bf16[2,128,128]{2,1,0:T(8,128)(2,1)S(1)}, u32[]{:S(2)}, u32[]{:S(2)}) collective-permute-start(bf16[2,128,128]{2,1,0:T(8,128)(2,1)S(1)} %get-tuple-element.17), channel_id=1, source_target_pairs={{0,256},{128,384},{256,0},{384,128},{1,257},{129,385},{257,1},{385... | collective-permute-start | bytes 196616 | tf_op jit(solution)/shard_map/ppermute | solution.py:242
  34.9 3.1 %collective-permute-start.3 = (bf16[2,128,128]{2,1,0:T(8,128)(2,1)S(1)}, bf16[2,128,128]{2,1,0:T(8,128)(2,1)S(1)}, u32[]{:S(2)}, u32[]{:S(2)}) collective-permute-start(bf16[2,128,128]{2,1,0:T(8,128)(2,1)S(1)} %get-tuple-element.18), channel_id=1, source_target_pairs={{0,384},{128,0},{256,128},{384,256},{1,385},{129,1},{257,129},{385... | collective-permute-start | bytes 196616 | tf_op jit(solution)/shard_map/ppermute | solution.py:242
  38.2 0.2 dynamic-slice_reduce_fusion
  38.5 0.1 reshape_tile.6.gain
  38.6 1.7 %collective-permute-done.3 = bf16[2,128,128]{2,1,0:T(8,128)(2,1)S(1)} collective-permute-done((bf16[2,128,128]{2,1,0:T(8,128)(2,1)S(1)}, bf16[2,128,128]{2,1,0:T(8,128)(2,1)S(1)}, u32[]{:S(2)}, u32[]{:S(2)}) %collective-permute-start.3) | collective-permute-done | bytes 65568 | tf_op jit(solution)/shard_map/ppermute | solution.py:242
  40.3 1.3 %collective-permute-start.5 = (bf16[8,8,16,128]{3,2,1,0:T(8,128)(2,1)S(1)}, bf16[8,8,16,128]{3,2,1,0:T(8,128)(2,1)S(1)}, u32[]{:S(2)}, u32[]{:S(2)}) collective-permute-start(bf16[8,8,16,128]{3,2,1,0:T(8,128)(2,1)S(1)} %pad_maximum_fusion.own), channel_id=1, source_target_pairs={{1,0},{2,1},{3,2},{4,3},{5,4},{6,5},{7,6},{8,7},{9,8},{10,9},{11,1... | collective-permute-start | bytes 786440 | tf_op jit(solution)/shard_map/ppermute | solution.py:246
  41.6 4.0 %collective-permute-start.4 = (bf16[8,8,16,128]{3,2,1,0:T(8,128)(2,1)S(1)}, bf16[8,8,16,128]{3,2,1,0:T(8,128)(2,1)S(1)}, u32[]{:S(2)}, u32[]{:S(2)}) collective-permute-start(bf16[8,8,16,128]{3,2,1,0:T(8,128)(2,1)S(1)} %pad_maximum_fusion.own), channel_id=1, source_target_pairs={{0,1},{1,2},{2,3},{3,4},{4,5},{5,6},{6,7},{7,8},{8,9},{9,10},{10,1... | collective-permute-start | bytes 786440 | tf_op jit(solution)/shard_map/ppermute | solution.py:245
  45.6 4.0 %all-to-all-done = bf16[64,32,256]{2,1,0:T(8,128)(2,1)S(1)} async-done(((bf16[64,32,256]{2,1,0:T(8,128)(2,1)}), bf16[64,32,256]{2,1,0:T(8,128)(2,1)S(1)}, u32[]{:S(2)}, u32[]{:S(2)}) %all-to-all-start) | async-done | bytes 1048608 | tf_op jit(solution)/shard_map/all_to_all | solution.py:225
  49.6 0.1 convert_reduce_fusion.1
  49.8 0.6 broadcast_in_dim.27
  50.4 8.2 %all-to-all-start.1 = ((f32[8,1,128]{2,1,0:T(1,128)}), f32[8,1,128]{2,1,0:T(1,128)S(1)}, u32[]{:S(2)}, u32[]{:S(2)}) async-start(f32[8,1,128]{2,1,0:T(1,128)} %broadcast_in_dim.27), calls=%async_computation.1 | async-start | bytes 8192 | tf_op jit(solution)/shard_map/all_to_all | solution.py:28
  58.6 0.5 copy.18
  59.3 0.1 fusion.4.weights
  59.4 3.6 %all-to-all-done.1 = f32[8,1,128]{2,1,0:T(1,128)S(1)} async-done(((f32[8,1,128]{2,1,0:T(1,128)}), f32[8,1,128]{2,1,0:T(1,128)S(1)}, u32[]{:S(2)}, u32[]{:S(2)}) %all-to-all-start.1) | async-done | bytes 4128 | tf_op jit(solution)/shard_map/all_to_all | solution.py:28
  63.1 4.4 %norm_conv.1 = (f32[4,8,32,256]{3,2,1,0:T(8,128)S(1)}, f32[4,8,32,256]{3,2,1,0:T(8,128)S(1)}, f32[1,256]{1,0:T(1,128)S(1)}) custom-call(s32[2]{0:T(128)S(1)} %copy-done.5, f32[8,128]{1,0:T(8,128)S(1)} %bitcast.34, f32[1,128]{1,0:T(1,128)S(1)} %reshape_tile.6.gain, f32[1,128]{1,0:T(1,128)S(1)} %reshape_tile.7.bias, ...), custom_call_target="tpu_custom_call" | custom-call | flops 2684354560 | bytes 6291456 | tf_op jit(solution)/shard_map/norm_conv/pallas_call | solution.py:263
  67.4 2.6 %collective-permute-start.6 = (f32[4,8,32,256]{3,2,1,0:T(8,128)S(1)}, f32[4,8,32,256]{3,2,1,0:T(8,128)S(1)}, u32[]{:S(2)}, u32[]{:S(2)}) collective-permute-start(f32[4,8,32,256]{3,2,1,0:T(8,128)S(1)} %get-tuple-element.13), channel_id=1, source_target_pairs={{0,64},{64,0},{1,65},{65,1},{2,66},{66,2},{3,67},{67,3},{4,68},{68... | collective-permute-start | bytes 3145736 | tf_op jit(solution)/shard_map/ppermute | solution.py:286
  70.0 2.3 %collective-permute-done.6 = f32[4,8,32,256]{3,2,1,0:T(8,128)S(1)} collective-permute-done((f32[4,8,32,256]{3,2,1,0:T(8,128)S(1)}, f32[4,8,32,256]{3,2,1,0:T(8,128)S(1)}, u32[]{:S(2)}, u32[]{:S(2)}) %collective-permute-start.6) | collective-permute-done | bytes 1048608 | tf_op jit(solution)/shard_map/ppermute | solution.py:286
  72.3 1.0 %multiply_convert_fusion = f16[4,8,32,256]{3,2,1,0:T(8,128)(2,1)} fusion(f32[4,8,32,256]{3,2,1,0:T(8,128)S(1)} %get-tuple-element.12, f32[4,8,32,256]{3,2,1,0:T(8,128)S(1)} %collective-permute-done.6, f32[256]{0:T(256)S(1)} %bitcast.32), kind=kLoop, calls=%fused_computation.10 | loop fusion | flops 786432 | bytes 2622464 | tf_op jit(solution)/shard_map/convert_element_type | solution.py:287
  73.3 3.5 %all-to-all-start.2 = ((f16[4,8,32,256]{3,2,1,0:T(8,128)(2,1)}), f16[4,8,32,256]{3,2,1,0:T(8,128)(2,1)S(1)}, u32[]{:S(2)}, u32[]{:S(2)}) async-start(f16[4,8,32,256]{3,2,1,0:T(8,128)(2,1)} %multiply_convert_fusion), calls=%async_computation.2 | async-start | bytes 1048576 | tf_op jit(solution)/shard_map/all_to_all | solution.py:288
  76.9 9.1 %all-to-all-done.2 = f16[4,8,32,256]{3,2,1,0:T(8,128)(2,1)S(1)} async-done(((f16[4,8,32,256]{3,2,1,0:T(8,128)(2,1)}), f16[4,8,32,256]{3,2,1,0:T(8,128)(2,1)S(1)}, u32[]{:S(2)}, u32[]{:S(2)}) %all-to-all-start.2) | async-done | bytes 524320 | tf_op jit(solution)/shard_map/all_to_all | solution.py:288
  86.0 0.1 convert_reduce_fusion
  86.1 0.7 select_convert_fusion
  (31 shorter events, 0.6 us)
Async XLA Ops:
  0.0 0.9 %copy-start = (bf16[2,4,2,16,512]{4,3,2,1,0:T(8,128)(2,1)S(1)}, bf16[2,4,2,16,512]{4,3,2,1,0:T(8,128)(2,1)}, u32[]{:S(2)}) copy-start(bf16[2,4,2,16,512]{4,3,2,1,0:T(8,128)(2,1)} %param.6) | copy-start | bytes 786436
  1.0 0.9 %copy-start.2 = (bf16[8,27,256]{2,0,1:T(8,128)(2,1)S(1)}, bf16[8,27,256]{2,0,1:T(8,128)(2,1)}, u32[]{:S(2)}) copy-start(bf16[8,27,256]{2,0,1:T(8,128)(2,1)} %param.10) | copy-start | bytes 331780
  1.8 0.7 copy-start.3
  2.5 0.7 copy-start.4
  3.2 19.7 %copy-start.1 = (bf16[2,4,2,16,512]{4,3,2,1,0:T(8,128)(2,1)S(1)}, bf16[2,4,2,16,512]{4,3,2,1,0:T(8,128)(2,1)}, u32[]{:S(2)}) copy-start(bf16[2,4,2,16,512]{4,3,2,1,0:T(8,128)(2,1)} %param.6) | copy-start | bytes 786436
  5.7 32.3 %copy-start.6 = (f32[512]{0:T(512)S(1)}, f32[512]{0:T(512)}, u32[]{:S(2)}) copy-start(f32[512]{0:T(512)} %param.8) | copy-start | bytes 6148
  5.8 32.4 %copy-start.7 = (f32[512]{0:T(512)S(1)}, f32[512]{0:T(512)}, u32[]{:S(2)}) copy-start(f32[512]{0:T(512)} %param.9) | copy-start | bytes 6148
  5.8 43.9 %all-to-all-start = ((bf16[64,32,256]{2,1,0:T(8,128)(2,1)}), bf16[64,32,256]{2,1,0:T(8,128)(2,1)S(1)}, u32[]{:S(2)}, u32[]{:S(2)}) async-start(bf16[64,32,256]{2,1,0:T(8,128)(2,1)} %payload.1), calls=%async_computation | async-start | bytes 2097152 | tf_op jit(solution)/shard_map/all_to_all | solution.py:225
  23.5 3.8 %collective-permute-start = (bf16[4,128,128]{2,1,0:T(8,128)(2,1)S(1)}, bf16[4,128,128]{2,1,0:T(8,128)(2,1)S(1)}, u32[]{:S(2)}, u32[]{:S(2)}) collective-permute-start(bf16[4,128,128]{2,1,0:T(8,128)(2,1)S(1)} %get-tuple-element.11), channel_id=1, source_target_pairs={{0,64},{64,0},{1,65},{65,1},{2,66},{66,2},{3,67},{67,3},{4,68},{68... | collective-permute-start | bytes 393224 | tf_op jit(solution)/shard_map/ppermute | solution.py:236
  27.5 11.1 %collective-permute-start.1 = (bf16[2,128,128]{2,1,0:T(8,128)(2,1)S(1)}, bf16[2,128,128]{2,1,0:T(8,128)(2,1)S(1)}, u32[]{:S(2)}, u32[]{:S(2)}) collective-permute-start(bf16[2,128,128]{2,1,0:T(8,128)(2,1)S(1)} %get-tuple-element.16), channel_id=1, source_target_pairs={{0,128},{128,256},{256,384},{384,0},{1,129},{129,257},{257,385},{3... | collective-permute-start | bytes 196616 | tf_op jit(solution)/shard_map/ppermute | solution.py:242
  30.6 8.0 %collective-permute-start.2 = (bf16[2,128,128]{2,1,0:T(8,128)(2,1)S(1)}, bf16[2,128,128]{2,1,0:T(8,128)(2,1)S(1)}, u32[]{:S(2)}, u32[]{:S(2)}) collective-permute-start(bf16[2,128,128]{2,1,0:T(8,128)(2,1)S(1)} %get-tuple-element.17), channel_id=1, source_target_pairs={{0,256},{128,384},{256,0},{384,128},{1,257},{129,385},{257,1},{385... | collective-permute-start | bytes 196616 | tf_op jit(solution)/shard_map/ppermute | solution.py:242
  34.9 5.3 %collective-permute-start.3 = (bf16[2,128,128]{2,1,0:T(8,128)(2,1)S(1)}, bf16[2,128,128]{2,1,0:T(8,128)(2,1)S(1)}, u32[]{:S(2)}, u32[]{:S(2)}) collective-permute-start(bf16[2,128,128]{2,1,0:T(8,128)(2,1)S(1)} %get-tuple-element.18), channel_id=1, source_target_pairs={{0,384},{128,0},{256,128},{384,256},{1,385},{129,1},{257,129},{385... | collective-permute-start | bytes 196616 | tf_op jit(solution)/shard_map/ppermute | solution.py:242
  40.3 19.1 %collective-permute-start.5 = (bf16[8,8,16,128]{3,2,1,0:T(8,128)(2,1)S(1)}, bf16[8,8,16,128]{3,2,1,0:T(8,128)(2,1)S(1)}, u32[]{:S(2)}, u32[]{:S(2)}) collective-permute-start(bf16[8,8,16,128]{3,2,1,0:T(8,128)(2,1)S(1)} %pad_maximum_fusion.own), channel_id=1, source_target_pairs={{1,0},{2,1},{3,2},{4,3},{5,4},{6,5},{7,6},{8,7},{9,8},{10,9},{11,1... | collective-permute-start | bytes 786440 | tf_op jit(solution)/shard_map/ppermute | solution.py:246
  41.6 17.8 %collective-permute-start.4 = (bf16[8,8,16,128]{3,2,1,0:T(8,128)(2,1)S(1)}, bf16[8,8,16,128]{3,2,1,0:T(8,128)(2,1)S(1)}, u32[]{:S(2)}, u32[]{:S(2)}) collective-permute-start(bf16[8,8,16,128]{3,2,1,0:T(8,128)(2,1)S(1)} %pad_maximum_fusion.own), channel_id=1, source_target_pairs={{0,1},{1,2},{2,3},{3,4},{4,5},{5,6},{6,7},{7,8},{8,9},{9,10},{10,1... | collective-permute-start | bytes 786440 | tf_op jit(solution)/shard_map/ppermute | solution.py:245
  50.4 12.7 %all-to-all-start.1 = ((f32[8,1,128]{2,1,0:T(1,128)}), f32[8,1,128]{2,1,0:T(1,128)S(1)}, u32[]{:S(2)}, u32[]{:S(2)}) async-start(f32[8,1,128]{2,1,0:T(1,128)} %broadcast_in_dim.27), calls=%async_computation.1 | async-start | bytes 8192 | tf_op jit(solution)/shard_map/all_to_all | solution.py:28
  59.2 3.8 %copy-start.5 = (s32[2]{0:T(128)S(1)}, s32[2]{0:T(128)}, u32[]{:S(2)}) copy-start(s32[2]{0:T(128)} %lengths.3) | copy-start | bytes 28
  67.4 4.9 %collective-permute-start.6 = (f32[4,8,32,256]{3,2,1,0:T(8,128)S(1)}, f32[4,8,32,256]{3,2,1,0:T(8,128)S(1)}, u32[]{:S(2)}, u32[]{:S(2)}) collective-permute-start(f32[4,8,32,256]{3,2,1,0:T(8,128)S(1)} %get-tuple-element.13), channel_id=1, source_target_pairs={{0,64},{64,0},{1,65},{65,1},{2,66},{66,2},{3,67},{67,3},{4,68},{68... | collective-permute-start | bytes 3145736 | tf_op jit(solution)/shard_map/ppermute | solution.py:286
  73.3 12.7 %all-to-all-start.2 = ((f16[4,8,32,256]{3,2,1,0:T(8,128)(2,1)}), f16[4,8,32,256]{3,2,1,0:T(8,128)(2,1)S(1)}, u32[]{:S(2)}, u32[]{:S(2)}) async-start(f16[4,8,32,256]{3,2,1,0:T(8,128)(2,1)} %multiply_convert_fusion), calls=%async_computation.2 | async-start | bytes 1048576 | tf_op jit(solution)/shard_map/all_to_all | solution.py:288

commit v4 on v3

v4 whole, which is shorter than its diff:
```python
import functools

import jax
import jax.numpy as jnp
from jax import lax
from jax.experimental import pallas as pl
from jax.experimental.pallas import tpu as pltpu
from jax.sharding import Mesh
from jax.sharding import PartitionSpec as P

GROUPS = 32
EPS = 1e-06
TM = ("x", "core")
TILE = ("y", "z")
SPANS = 8
VIDEOS = 2
FRAMES = 4
COLS = 16
SHARE = 64
CHIPS = 4
PART = 2 * SHARE
ROWS = 4
OUT = 256


def to_all(block, axis):
    count = lax.axis_size(axis)
    copies = jnp.broadcast_to(block[None], (count,) + block.shape)
    return lax.all_to_all(copies, axis, 0, 0, tiled=True)


def payload_kernel(features, conv, skip, lengths, copies, planes, taps, skips, valid, rows, done):
    moves = [
        pltpu.make_async_copy(source, target, done.at[index])
        for index, (source, target) in enumerate(
            ((features, planes), (conv, taps), (skip, skips), (lengths, valid))
        )
    ]
    for move in moves:
        move.start()
    for move in moves:
        move.wait()
    count, channels = taps.shape[0], planes.shape[-1]
    span = lax.axis_index(TM)
    pick = lax.broadcasted_iota(jnp.int32, (count, SPANS, OUT), 1) == span
    rows[...] = jnp.zeros_like(rows)
    rows[0:count, :] = jnp.sum(jnp.where(pick, taps[...].astype(jnp.float32), 0.0), axis=1)
    pick = lax.broadcasted_iota(jnp.int32, (SPANS, OUT), 0) == span
    rows[count : count + 1, :] = jnp.sum(
        jnp.where(pick, skips[...].astype(jnp.float32), 0.0), axis=0, keepdims=True
    )
    group = lax.broadcasted_iota(jnp.int32, (channels, 128), 0) // (channels // GROUPS)
    lane = lax.broadcasted_iota(jnp.int32, (channels, 128), 1)
    sums = jnp.zeros((1, 128), jnp.float32)
    for video in range(VIDEOS):
        linear = jnp.zeros((1, channels), jnp.float32)
        square = jnp.zeros((1, channels), jnp.float32)
        for frame in range(FRAMES):
            block = planes[video * FRAMES + frame].astype(jnp.float32)
            shown = (span * FRAMES + frame < valid[video]).astype(jnp.float32)
            linear += jnp.sum(block, axis=0, keepdims=True) * shown
            square += jnp.sum(block * block, axis=0, keepdims=True) * shown
        for which, value in ((video, linear), (VIDEOS + video, square)):
            chosen = (lane == group + which * GROUPS).astype(jnp.float32)
            sums += jnp.dot(
                value, chosen, precision=lax.Precision.HIGHEST, preferred_element_type=jnp.float32
            )
    high = sums.astype(jnp.bfloat16).astype(jnp.float32)
    middle = (sums - high).astype(jnp.bfloat16).astype(jnp.float32)
    rows[count + 1 : count + 2, 0:128] = high
    rows[count + 1 : count + 2, 128:256] = middle
    rows[count + 2 : count + 3, 0:128] = sums - high - middle
    value = rows[...].astype(jnp.bfloat16)
    for index in range(copies.shape[0]):
        copies[index] = value


def member_kernel(features, shares, tails):
    voxels, channels = features.shape[0] * COLS, features.shape[-1]
    column = lax.broadcasted_iota(jnp.int32, (channels, channels), 1)
    place = column % PART
    source = place % SHARE * SPANS + column // PART * 2 + place // SHARE
    match = lax.broadcasted_iota(jnp.int32, (channels, channels), 0) == source
    chosen = jnp.where(match, 1.0, 0.0).astype(jnp.bfloat16)
    for row in range(2):
        block = features[:, row * COLS : (row + 1) * COLS].reshape(voxels, channels)
        flat = jnp.dot(block, chosen, preferred_element_type=jnp.float32).astype(jnp.bfloat16)
        flat = flat.reshape(VIDEOS, FRAMES, COLS, channels)
        lanes = slice(row * PART, (row + 1) * PART)
        for chip in range(CHIPS):
            part = flat[..., chip * PART : (chip + 1) * PART]
            shares[chip, :, :, :, lanes] = part
            tails[chip, :, :, :, lanes] = part[:, FRAMES - 2 :]


def norm_kernel(
    lengths, totals, gain, bias, signal, above, below, shifted, raw, factor, moments,
    *, cells, tiles, tap_bound, skip_bound
):
    chip, core = lax.axis_index("x"), lax.axis_index("core")
    tile = lax.axis_index(TILE)
    summed = [totals[0:1, :]]
    for span in range(1, SPANS):
        summed.append(summed[-1] + totals[span : span + 1, :])
    summed = jnp.concatenate(summed, axis=0)
    entry = lax.broadcasted_iota(jnp.int32, (128, PART), 0)
    group = lax.broadcasted_iota(jnp.int32, (128, PART), 1) % SHARE // 2
    ends = (lax.broadcasted_iota(jnp.int32, (SPANS, PART), 0) + 1) * FRAMES

    def spread(which):
        chosen = (entry == group + which * GROUPS).astype(jnp.float32)
        return jnp.dot(
            summed, chosen, precision=lax.Precision.HIGHEST, preferred_element_type=jnp.float32
        )

    ratio = jnp.zeros((SPANS, PART), jnp.float32)
    largest = jnp.zeros((SPANS, PART), jnp.float32)
    for video in range(VIDEOS):
        seen = jnp.minimum(ends, lengths[video]).astype(jnp.float32) * cells
        square = spread(VIDEOS + video)
        centre = spread(video) / seen
        inverse = lax.rsqrt(square / seen - centre * centre + EPS)
        moments[2 * video] = centre
        moments[2 * video + 1] = inverse * gain[...]
        size = jnp.sqrt(square)
        ratio = jnp.maximum(ratio, size * inverse)
        largest = jnp.maximum(largest, size)
    bound = tap_bound * (3.0 * jnp.max(ratio, keepdims=True) + 3.0)
    bound = bound + skip_bound * jnp.max(largest, keepdims=True)
    factor[...] = jnp.broadcast_to(jnp.exp2(14.0 - jnp.floor(jnp.log2(bound))), factor.shape)

    offset = bias[...].reshape(1, 1, PART)

    def normed(value, video, span, first):
        centre = moments[2 * video, pl.ds(span, 1)].reshape(1, 1, PART)
        scale = moments[2 * video + 1, pl.ds(span, 1)].reshape(1, 1, PART)
        shown = lax.broadcasted_iota(jnp.int32, value.shape, 0) + first < lengths[video]
        value = (value.astype(jnp.float32) - centre) * scale + offset
        value = value / (1.0 + jnp.exp(-value))
        return jnp.where(shown, value, 0.0)

    for step in range(CHIPS):
        span = lax.rem(chip - step + CHIPS, CHIPS) * 2 + core
        before = jnp.maximum(span - 1, 0)
        behind = lax.rem(step + 1 - core, CHIPS)
        for video in range(VIDEOS):
            raw[step, video] = signal[step, video, :FRAMES]
            for row in range(ROWS):
                if row == 0:
                    now, past, lanes, edge = above, above, slice(0, PART), tile == 0
                elif row == ROWS - 1:
                    now, past, lanes, edge = below, below, slice(0, PART), tile == tiles - 1
                else:
                    now, past, lanes, edge = signal, signal, slice((row - 1) * PART, row * PART), None
                value = now[step, video, :FRAMES, :, lanes]
                old = past[behind, video, FRAMES:, :, lanes]
                if edge is not None:
                    same = slice(0, PART) if row == 0 else slice(PART, 2 * PART)
                    value = jnp.where(edge, signal[step, video, :FRAMES, :, same], value)
                    old = jnp.where(edge, signal[behind, video, FRAMES:, :, same], old)
                value = normed(value, video, span, span * FRAMES)
                old = normed(old, video, before, span * FRAMES - 2)
                old = jnp.where(span == 0, jnp.broadcast_to(value[:1], old.shape), old)
                value = jnp.concatenate([old, value], axis=0)
                left = jnp.concatenate([value[:, :1], value[:, :-1]], axis=1)
                right = jnp.concatenate([value[:, 1:], value[:, -1:]], axis=1)
                lanes = slice(row * PART, (row + 1) * PART)
                for side, part in enumerate((left, value, right)):
                    shifted[side, step, video, :, :, lanes] = part.astype(jnp.bfloat16)


def taps_kernel(shifted, raw, factor, mine, theirs, out, weights):
    chip, core = lax.axis_index("x"), lax.axis_index("core")
    count = mine.shape[0]
    for tap in range(count):
        weights[tap, pl.ds(pl.multiple_of(core * SHARE, SHARE), SHARE)] = mine[tap]
        weights[tap, pl.ds(pl.multiple_of((1 - core) * SHARE, SHARE), SHARE)] = theirs[tap]
    for row in range(2):
        total = None
        for pair in range(count // 2):
            blocks = []
            for tap in (2 * pair, 2 * pair + 1):
                if tap < count - 1:
                    at = (row + tap // 3 % 3) * PART
                    first = tap // 9
                    block = shifted[tap % 3, :, :, first : first + FRAMES, :, at : at + PART]
                else:
                    block = raw[..., row * PART : (row + 1) * PART]
                blocks.append(block.reshape(-1, PART))
            term = jnp.dot(
                jnp.concatenate(blocks, axis=1),
                weights[2 * pair : 2 * pair + 2].reshape(2 * PART, OUT),
                preferred_element_type=jnp.float32,
            )
            total = term if total is None else total + term
        total = (total * factor[...]).astype(out.dtype)
        total = total.reshape(CHIPS, -1, COLS, OUT)
        for step in range(CHIPS):
            owner = lax.rem(chip - step + CHIPS, CHIPS)
            out[owner, :, row * COLS : (row + 1) * COLS, :] = total[step]


def per_device(features, lengths, gain_in, bias_in, conv_in, skip_weight):
    videos, frames, row_count, col_count, wide_in = features.shape
    span, chip = lax.axis_index(TM), lax.axis_index("x")
    tiles, chips = lax.axis_size(TILE), lax.axis_size("x")
    taps = conv_in.shape[1]
    on_chip = pl.BlockSpec(memory_space=pltpu.VMEM)
    anywhere = pl.BlockSpec(memory_space=pl.ANY)
    scalar = pl.BlockSpec(memory_space=pltpu.SMEM)
    params = pltpu.CompilerParams(vmem_limit_bytes=20 * 1024 * 1024)

    planes = features.reshape(videos * frames, row_count * col_count, wide_in)
    copies = pl.pallas_call(
        payload_kernel,
        out_shape=jax.ShapeDtypeStruct((tiles, 32, OUT), jnp.bfloat16),
        in_specs=[anywhere] * 4,
        out_specs=on_chip,
        scratch_shapes=[
            pltpu.VMEM(planes.shape, jnp.bfloat16),
            pltpu.VMEM((taps, SPANS, OUT), jnp.bfloat16),
            pltpu.VMEM((SPANS, OUT), jnp.bfloat16),
            pltpu.SMEM((videos,), jnp.int32),
            pltpu.VMEM((32, OUT), jnp.float32),
            pltpu.SemaphoreType.DMA((4,)),
        ],
        compiler_params=pltpu.CompilerParams(vmem_limit_bytes=63 * 1024 * 1024),
        name="payload",
    )(planes, conv_in.transpose(1, 0, 2), skip_weight, lengths)
    arrived = lax.all_to_all(copies, TILE, 0, 0, tiled=True)

    shape = (chips, videos, frames, col_count, 2 * PART)
    shares, tails = pl.pallas_call(
        member_kernel,
        out_shape=(
            jax.ShapeDtypeStruct(shape, jnp.bfloat16),
            jax.ShapeDtypeStruct(shape[:2] + (2,) + shape[3:], jnp.bfloat16),
        ),
        in_specs=[on_chip],
        out_specs=(on_chip, on_chip),
        compiler_params=params,
        name="member_shares",
    )(planes)
    swap = [(0, 1), (1, 0)]
    shares = jnp.concatenate([shares, lax.ppermute(tails, "core", swap)], axis=2)
    signal = []
    for step in range(chips):
        block = lax.dynamic_index_in_dim(shares, lax.rem(chip + step, chips), 0, False)
        if step:
            block = lax.ppermute(block, "x", [(i, (i + step) % chips) for i in range(chips)])
        signal.append(block)
    signal = jnp.stack(signal)
    upper, lower = signal[..., PART:], signal[..., :PART]
    above = lax.ppermute(upper, TILE, [(i, i + 1) for i in range(tiles - 1)])
    below = lax.ppermute(lower, TILE, [(i + 1, i) for i in range(tiles - 1)])

    def lanes(vector):
        own = lax.dynamic_slice_in_dim(vector.reshape(SHARE, SPANS), 2 * chip, 2, axis=1)
        return own.T.reshape(1, PART)

    parts = jnp.sum(arrived[:, taps + 1 : taps + 3].astype(jnp.float32), axis=0)
    sums = parts[:1, :128] + parts[:1, 128:] + parts[1:, :128]
    gain, bias = lanes(gain_in), lanes(bias_in)
    sums, upper, lower, gain, bias = lax.optimization_barrier((sums, upper, lower, gain, bias))
    copies = jnp.broadcast_to(sums[None], (SPANS,) + sums.shape)
    totals = lax.all_to_all(copies, TM, 0, 0, tiled=True).reshape(SPANS, -1)
    mine = arrived[:, : taps + 1].transpose(1, 0, 2)
    theirs = lax.ppermute(mine, "core", swap)

    shifted, raw, factor = pl.pallas_call(
        functools.partial(
            norm_kernel,
            cells=float(row_count * tiles * col_count * (wide_in // GROUPS)),
            tiles=tiles,
            tap_bound=float(taps * PART) * 0.0546875,
            skip_bound=float(PART) * 0.25,
        ),
        out_shape=(
            jax.ShapeDtypeStruct(
                (3, chips, videos, frames + 2, col_count, ROWS * PART), jnp.bfloat16
            ),
            jax.ShapeDtypeStruct((chips, videos, frames, col_count, 2 * PART), jnp.bfloat16),
            jax.ShapeDtypeStruct((1, OUT), jnp.float32),
        ),
        in_specs=[scalar] + [on_chip] * 6,
        out_specs=(on_chip, on_chip, on_chip),
        scratch_shapes=[pltpu.VMEM((2 * videos, SPANS, PART), jnp.float32)],
        compiler_params=params,
        cost_estimate=pl.CostEstimate(flops=1 << 34, bytes_accessed=1 << 26, transcendentals=1 << 24),
        name="norm",
    )(lengths, totals, gain, bias, signal, above, below)
    total = pl.pallas_call(
        taps_kernel,
        out_shape=jax.ShapeDtypeStruct((chips, videos * frames, row_count * col_count, OUT), jnp.float32),
        in_specs=[on_chip] * 5,
        out_specs=on_chip,
        scratch_shapes=[pltpu.VMEM((taps + 1, PART, OUT), jnp.bfloat16)],
        compiler_params=params,
        cost_estimate=pl.CostEstimate(
            flops=2 * 28 * 1024 * 128 * 256, bytes_accessed=6 << 20, transcendentals=0
        ),
        name="taps",
    )(shifted, raw, factor, mine, theirs)

    total = total.astype(jnp.float16)
    total = lax.all_to_all(total, "x", 0, 0, tiled=True)
    total = jnp.sum(total.astype(jnp.float32), axis=0) / factor
    total = total.reshape(videos, frames, row_count, col_count, OUT)
    stamps = span * frames + jnp.arange(frames, dtype=jnp.int32)
    present = stamps[None, :] < lengths[:, None]
    return jnp.where(present[:, :, None, None, None], total, 0.0).astype(jnp.bfloat16)


def solution(mesh):
    spans, tiles = mesh.devices.shape
    fine = Mesh(mesh.devices.reshape(spans // 2, 2, 8, tiles // 8), TM + TILE)
    placed = (
        P(None, TM, TILE, None, None),
        P(),
        P(),
        P(),
        P(TILE, None, None),
        P(TILE, None),
    )
    return jax.shard_map(
        per_device,
        mesh=fine,
        in_specs=placed,
        out_specs=P(None, TM, TILE, None, None),
        check_vma=False,
    )
```

time: 88 us -> 81.3 us (0.924)
  waiting for transfers between devices: 21.6 us -> 17.5 us
  local copies, waits for them, and re-layouts: 5 us -> 3.05 us
  starting transfers between devices: 50.1 us -> 48.8 us
    all_to_all x1, waiting for transfers between devices: 3.63 us -> 0.81 us  [per_device(): totals = lax.all_to_all(copies, TM, 0, 0, tiled=True).reshape(SPANS, -1)]
    ppermute x3, waiting for transfers between devices: 1.66 us -> 4.19 us  [per_device(): lax.ppermute(block, 'x', [(i, (i + step) % chips) for i in range(chips)])]
    ppermute x4, waiting for transfers between devices: 3.2 us -> 0.7 us  [the longest x1 0.69 us: per_device(): lax.ppermute(tails, 'core', swap)]
    unnamed x18 -> x10, local copies, waits for them, and re-layouts: 3.73 us -> 1.77 us
    ppermute x3, starting transfers between devices: 10.5 us -> 9.33 us  [per_device(): lax.ppermute(block, 'x', [(i, (i + step) % chips) for i in range(chips)])]
    all_to_all x1, waiting for transfers between devices: 4.04 us -> 2.91 us  [per_device(): arrived = lax.all_to_all(copies, TILE, 0, 0, tiled=True)]
    reduce_sum x1, other arithmetic: 0.12 us -> 1.07 us  [per_device(): parts = jnp.sum(arrived[:, taps + 1:taps + 3].astype(jnp.float32), axis=0)]
    pallas_call x2 -> x3, Pallas kernels: 4.97 us -> 4.46 us  [the longest x1 2.1 us: per_device(): pl.pallas_call(taps_kernel, out_shape=jax.ShapeDtypeStruct((chips, videos...]
  transfers between devices with their start and end apart: 10 -> 10, of which waited for: 6 -> 6; matrix products, arithmetic and copies ran while one was open for 3% -> 5% of each run, Pallas kernels for 1% -> 3%
where the time goes in v4:
time: 81.3 us; the launch traced here: 79.8 us
  starting transfers between devices  48.8 us (60%)
  waiting for transfers between devices  17.5 us (22%)
  Pallas kernels  7.33 us (9%)
  local copies, waits for them, and re-layouts  3.05 us (4%)
  other arithmetic  2.95 us (4%)
    all_to_all x1, starting transfers between devices, per_device(): arrived = lax.all_to_all(copies, TILE, 0, 0, tiled=True)  17.4 us
    ppermute x3, starting transfers between devices, per_device(): lax.ppermute(block, 'x', [(i, (i + step) % chips) for i in range(chips)])  9.33 us
    all_to_all x1, waiting for transfers between devices, per_device(): total = lax.all_to_all(total, 'x', 0, 0, tiled=True)  8.88 us
    all_to_all x1, starting transfers between devices, per_device(): totals = lax.all_to_all(copies, TM, 0, 0, tiled=True).reshape(SPANS, -1)  8.19 us
    ppermute x3, waiting for transfers between devices, per_device(): lax.ppermute(block, 'x', [(i, (i + step) % chips) for i in range(chips)])  4.19 us
    ppermute x1, starting transfers between devices, per_device(): above = lax.ppermute(upper, TILE, [(i, i + 1) for i in range(tiles - 1)])  4 us
    all_to_all x1, starting transfers between devices, per_device(): total = lax.all_to_all(total, 'x', 0, 0, tiled=True)  3.75 us
    all_to_all x1, waiting for transfers between devices, per_device(): arrived = lax.all_to_all(copies, TILE, 0, 0, tiled=True)  2.91 us
  transfers between devices with their start and end apart: 10, of which 6 were waited for; matrix products, arithmetic and copies ran while one was open for 5% of the time, Pallas kernels for 3%

profile of v4, /device:TPU:1, one launch (start us, length us, event | category | flops | bytes accessed | tf_op | source)
XLA Modules:
  0.0 79.8 jit_solution(4514280675498870822)
XLA Ops:
  0.0 2.9 %payload.1 = bf16[64,32,256]{2,1,0:T(8,128)(2,1)} custom-call(bf16[8,32,512]{2,1,0:T(8,128)(2,1)} %bitcast.23, bf16[27,8,256]{2,1,0:T(8,128)(2,1)} %bitcast.30, bf16[8,256]{1,0:T(8,128)(2,1)} %skip.1, s32[2]{0:T(128)} %lengths.3), custom_call_target="tpu_custom_call" | custom-call | tf_op jit(solution)/shard_map/payload/pallas_call | solution.py:214
  2.9 17.4 %all-to-all-start = ((bf16[64,32,256]{2,1,0:T(8,128)(2,1)}), bf16[64,32,256]{2,1,0:T(8,128)(2,1)}, u32[]{:S(2)}, u32[]{:S(2)}) async-start(bf16[64,32,256]{2,1,0:T(8,128)(2,1)} %payload.1), calls=%async_computation | async-start | bytes 2097152 | tf_op jit(solution)/shard_map/all_to_all | solution.py:230
  20.3 0.4 member_shares.1
  20.7 2.9 %collective-permute-start = (bf16[4,2,2,16,256]{4,3,2,1,0:T(8,128)(2,1)S(1)}, bf16[4,2,2,16,256]{4,3,2,1,0:T(8,128)(2,1)S(1)}, u32[]{:S(2)}, u32[]{:S(2)}) collective-permute-start(bf16[4,2,2,16,256]{4,3,2,1,0:T(8,128)(2,1)S(1)} %get-tuple-element.14), channel_id=1, source_target_pairs={{0,64},{64,0},{1,65},{65,1},{2,66},{66,2},{3,67},{67,3},{4,68},{68... | collective-permute-start | bytes 393224 | tf_op jit(solution)/shard_map/ppermute | solution.py:245
  23.6 0.1 reshape.57
  23.7 0.1 reshape.59
  23.8 0.7 collective-permute-done
  24.6 4.4 %collective-permute-start.3 = (bf16[2,6,16,256]{3,2,1,0:T(8,128)(2,1)S(1)}, bf16[2,6,16,256]{3,2,1,0:T(8,128)(2,1)S(1)}, u32[]{:S(2)}, u32[]{:S(2)}) collective-permute-start(bf16[2,6,16,256]{3,2,1,0:T(8,128)(2,1)S(1)} %get-tuple-element.24), channel_id=1, source_target_pairs={{0,384},{128,0},{256,128},{384,256},{1,385},{129,1},{257,129},{385... | collective-permute-start | bytes 294920 | tf_op jit(solution)/shard_map/ppermute | solution.py:250
  29.0 2.4 %collective-permute-start.2 = (bf16[2,6,16,256]{3,2,1,0:T(8,128)(2,1)S(1)}, bf16[2,6,16,256]{3,2,1,0:T(8,128)(2,1)S(1)}, u32[]{:S(2)}, u32[]{:S(2)}) collective-permute-start(bf16[2,6,16,256]{3,2,1,0:T(8,128)(2,1)S(1)} %get-tuple-element.25), channel_id=1, source_target_pairs={{0,256},{128,384},{256,0},{384,128},{1,257},{129,385},{257,1},{385... | collective-permute-start | bytes 294920 | tf_op jit(solution)/shard_map/ppermute | solution.py:250
  31.4 2.5 %collective-permute-start.1 = (bf16[2,6,16,256]{3,2,1,0:T(8,128)(2,1)S(1)}, bf16[2,6,16,256]{3,2,1,0:T(8,128)(2,1)S(1)}, u32[]{:S(2)}, u32[]{:S(2)}) collective-permute-start(bf16[2,6,16,256]{3,2,1,0:T(8,128)(2,1)S(1)} %get-tuple-element.26), channel_id=1, source_target_pairs={{0,128},{128,256},{256,384},{384,0},{1,129},{129,257},{257,385},{3... | collective-permute-start | bytes 294920 | tf_op jit(solution)/shard_map/ppermute | solution.py:250
  33.9 0.1 dynamic-slice_bitcast_fusion.3
  34.1 0.1 reshape.60.bias
  34.3 0.1 reshape.58.gain
  34.3 1.9 %collective-permute-done.2 = bf16[2,6,16,256]{3,2,1,0:T(8,128)(2,1)S(1)} collective-permute-done((bf16[2,6,16,256]{3,2,1,0:T(8,128)(2,1)S(1)}, bf16[2,6,16,256]{3,2,1,0:T(8,128)(2,1)S(1)}, u32[]{:S(2)}, u32[]{:S(2)}) %collective-permute-start.2) | collective-permute-done | bytes 98336 | tf_op jit(solution)/shard_map/ppermute | solution.py:250
  36.3 2.3 %collective-permute-done.1 = bf16[2,6,16,256]{3,2,1,0:T(8,128)(2,1)S(1)} collective-permute-done((bf16[2,6,16,256]{3,2,1,0:T(8,128)(2,1)S(1)}, bf16[2,6,16,256]{3,2,1,0:T(8,128)(2,1)S(1)}, u32[]{:S(2)}, u32[]{:S(2)}) %collective-permute-start.1) | collective-permute-done | bytes 98336 | tf_op jit(solution)/shard_map/ppermute | solution.py:250
  38.7 1.3 %collective-permute-start.5 = (bf16[4,2,6,16,128]{4,3,2,1,0:T(8,128)(2,1)S(1)}, bf16[4,2,6,16,128]{4,3,2,1,0:T(8,128)(2,1)S(1)}, u32[]{:S(2)}, u32[]{:S(2)}) collective-permute-start(bf16[4,2,6,16,128]{4,3,2,1,0:T(8,128)(2,1)S(1)} %get-tuple-element.21), channel_id=1, source_target_pairs={{1,0},{2,1},{3,2},{4,3},{5,4},{6,5},{7,6},{8,7},{9,8},{10,9},{11,1... | collective-permute-start | bytes 589832 | tf_op jit(solution)/shard_map/ppermute | solution.py:255
  40.0 4.0 %collective-permute-start.4 = (bf16[4,2,6,16,128]{4,3,2,1,0:T(8,128)(2,1)S(1)}, bf16[4,2,6,16,128]{4,3,2,1,0:T(8,128)(2,1)S(1)}, u32[]{:S(2)}, u32[]{:S(2)}) collective-permute-start(bf16[4,2,6,16,128]{4,3,2,1,0:T(8,128)(2,1)S(1)} %get-tuple-element.22), channel_id=1, source_target_pairs={{0,1},{1,2},{2,3},{3,4},{4,5},{5,6},{6,7},{7,8},{8,9},{9,10},{10,1... | collective-permute-start | bytes 589832 | tf_op jit(solution)/shard_map/ppermute | solution.py:254
  44.0 2.9 %all-to-all-done = bf16[64,32,256]{2,1,0:T(8,128)(2,1)} async-done(((bf16[64,32,256]{2,1,0:T(8,128)(2,1)}), bf16[64,32,256]{2,1,0:T(8,128)(2,1)}, u32[]{:S(2)}, u32[]{:S(2)}) %all-to-all-start) | async-done | bytes 1048608 | tf_op jit(solution)/shard_map/all_to_all | solution.py:230
  46.9 1.1 %convert_reduce_fusion.1 = f32[2,256]{1,0:T(2,128)S(1)} fusion(bf16[64,32,256]{2,1,0:T(8,128)(2,1)} %all-to-all-done), kind=kLoop, calls=%fused_computation.4 | loop fusion | flops 65024 | bytes 67584 | tf_op jit(solution)/shard_map/reduce_sum | solution.py:261
  47.9 0.6 broadcast_in_dim.26
  48.5 8.2 %all-to-all-start.1 = ((f32[8,1,128]{2,1,0:T(1,128)}), f32[8,1,128]{2,1,0:T(1,128)S(1)}, u32[]{:S(2)}, u32[]{:S(2)}) async-start(f32[8,1,128]{2,1,0:T(1,128)} %broadcast_in_dim.26), calls=%async_computation.1 | async-start | bytes 8192 | tf_op jit(solution)/shard_map/all_to_all | solution.py:266
  56.7 1.7 %copy.16 = bf16[64,28,256]{2,0,1:T(8,128)(2,1)S(1)} copy(bf16[64,28,256]{2,1,0:T(8,128)(2,1)} %bitcast.22) | data formatting | bytes 1835008
  58.5 1.9 %collective-permute-start.6 = (bf16[28,64,256]{2,1,0:T(8,128)(2,1)S(1)}, bf16[28,64,256]{2,1,0:T(8,128)(2,1)S(1)}, u32[]{:S(2)}, u32[]{:S(2)}) collective-permute-start(bf16[28,64,256]{2,1,0:T(8,128)(2,1)S(1)} %bitcast.25), channel_id=1, source_target_pairs={{0,64},{64,0},{1,65},{65,1},{2,66},{66,2},{3,67},{67,3},{4,68},{68... | collective-permute-start | bytes 2752520 | tf_op jit(solution)/shard_map/ppermute | solution.py:268
  60.4 0.8 %all-to-all-done.1 = f32[8,1,128]{2,1,0:T(1,128)S(1)} async-done(((f32[8,1,128]{2,1,0:T(1,128)}), f32[8,1,128]{2,1,0:T(1,128)S(1)}, u32[]{:S(2)}, u32[]{:S(2)}) %all-to-all-start.1) | async-done | bytes 4128 | tf_op jit(solution)/shard_map/all_to_all | solution.py:266
  61.2 2.0 %norm.1 = (bf16[3,4,2,6,16,512]{5,4,3,2,1,0:T(8,128)(2,1)S(1)}, bf16[4,2,4,16,256]{4,3,2,1,0:T(8,128)(2,1)S(1)}, f32[1,256]{1,0:T(1,128)S(1)}) custom-call(s32[2]{0:T(128)S(1)} %copy-done.1, f32[8,128]{1,0:T(8,128)S(1)} %bitcast.27, f32[1,128]{1,0:T(1,128)S(1)} %reshape.58.gain, f32[1,128]{1,0:T(1,128)S(1)} %reshape.60.bias, ...), custom_call_target="tpu_custom_call" | custom-call | flops 17179869184 | bytes 67108864 | tf_op jit(solution)/shard_map/norm/pallas_call | solution.py:270
  63.3 2.1 %taps.1 = f32[4,8,32,256]{3,2,1,0:T(8,128)S(1)} custom-call(bf16[3,4,2,6,16,512]{5,4,3,2,1,0:T(8,128)(2,1)S(1)} %get-tuple-element.18.shifted, bf16[4,2,4,16,256]{4,3,2,1,0:T(8,128)(2,1)S(1)} %get-tuple-element.19.raw, f32[1,256]{1,0:T(1,128)S(1)} %get-tuple-element.20.factor, bf16[28,64,256]{2,1,0:T(8,128)(2,1)S(1)} %bitcast.26, ...), custom_call_target="tpu_custom_call" | custom-call | flops 1879048192 | bytes 6291456 | tf_op jit(solution)/shard_map/taps/pallas_call | solution.py:292
  65.4 0.9 %convert_element_type.13 = f16[4,8,32,256]{3,2,1,0:T(8,128)(2,1)} convert(f32[4,8,32,256]{3,2,1,0:T(8,128)S(1)} %taps.1) | non-fusion elementwise | flops 262144 | bytes 1572864 | tf_op jit(solution)/shard_map/convert_element_type | solution.py:305
  66.3 3.7 %all-to-all-start.2 = ((f16[4,8,32,256]{3,2,1,0:T(8,128)(2,1)}), f16[4,8,32,256]{3,2,1,0:T(8,128)(2,1)S(1)}, u32[]{:S(2)}, u32[]{:S(2)}) async-start(f16[4,8,32,256]{3,2,1,0:T(8,128)(2,1)} %convert_element_type.13), calls=%async_computation.2 | async-start | bytes 1048576 | tf_op jit(solution)/shard_map/all_to_all | solution.py:306
  70.0 0.1 broadcast_compare_fusion
  70.1 8.9 %all-to-all-done.2 = f16[4,8,32,256]{3,2,1,0:T(8,128)(2,1)S(1)} async-done(((f16[4,8,32,256]{3,2,1,0:T(8,128)(2,1)}), f16[4,8,32,256]{3,2,1,0:T(8,128)(2,1)S(1)}, u32[]{:S(2)}, u32[]{:S(2)}) %all-to-all-start.2) | async-done | bytes 524320 | tf_op jit(solution)/shard_map/all_to_all | solution.py:306
  79.0 0.1 convert_reduce_fusion
  79.1 0.7 select_convert_fusion
  (21 shorter events, 0.4 us)
Async XLA Ops:
  0.0 20.3 %copy-start = (bf16[2,4,2,16,512]{4,3,2,1,0:T(8,128)(2,1)S(1)}, bf16[2,4,2,16,512]{4,3,2,1,0:T(8,128)(2,1)}, u32[]{:S(2)}) copy-start(bf16[2,4,2,16,512]{4,3,2,1,0:T(8,128)(2,1)} %param.6) | copy-start | bytes 786436
  0.0 23.6 %copy-start.2 = (f32[512]{0:T(512)S(1)}, f32[512]{0:T(512)}, u32[]{:S(2)}) copy-start(f32[512]{0:T(512)} %param.8) | copy-start | bytes 6148
  0.0 23.7 %copy-start.3 = (f32[512]{0:T(512)S(1)}, f32[512]{0:T(512)}, u32[]{:S(2)}) copy-start(f32[512]{0:T(512)} %param.9) | copy-start | bytes 6148
  2.9 44.0 %all-to-all-start = ((bf16[64,32,256]{2,1,0:T(8,128)(2,1)}), bf16[64,32,256]{2,1,0:T(8,128)(2,1)}, u32[]{:S(2)}, u32[]{:S(2)}) async-start(bf16[64,32,256]{2,1,0:T(8,128)(2,1)} %payload.1), calls=%async_computation | async-start | bytes 2097152 | tf_op jit(solution)/shard_map/all_to_all | solution.py:230
  20.7 3.8 %collective-permute-start = (bf16[4,2,2,16,256]{4,3,2,1,0:T(8,128)(2,1)S(1)}, bf16[4,2,2,16,256]{4,3,2,1,0:T(8,128)(2,1)S(1)}, u32[]{:S(2)}, u32[]{:S(2)}) collective-permute-start(bf16[4,2,2,16,256]{4,3,2,1,0:T(8,128)(2,1)S(1)} %get-tuple-element.14), channel_id=1, source_target_pairs={{0,64},{64,0},{1,65},{65,1},{2,66},{66,2},{3,67},{67,3},{4,68},{68... | collective-permute-start | bytes 393224 | tf_op jit(solution)/shard_map/ppermute | solution.py:245
  24.5 36.7 %copy-start.1 = (s32[2]{0:T(128)S(1)}, s32[2]{0:T(128)}, u32[]{:S(2)}) copy-start(s32[2]{0:T(128)} %lengths.3) | copy-start | bytes 28
  24.6 9.8 %collective-permute-start.3 = (bf16[2,6,16,256]{3,2,1,0:T(8,128)(2,1)S(1)}, bf16[2,6,16,256]{3,2,1,0:T(8,128)(2,1)S(1)}, u32[]{:S(2)}, u32[]{:S(2)}) collective-permute-start(bf16[2,6,16,256]{3,2,1,0:T(8,128)(2,1)S(1)} %get-tuple-element.24), channel_id=1, source_target_pairs={{0,384},{128,0},{256,128},{384,256},{1,385},{129,1},{257,129},{385... | collective-permute-start | bytes 294920 | tf_op jit(solution)/shard_map/ppermute | solution.py:250
  29.0 7.3 %collective-permute-start.2 = (bf16[2,6,16,256]{3,2,1,0:T(8,128)(2,1)S(1)}, bf16[2,6,16,256]{3,2,1,0:T(8,128)(2,1)S(1)}, u32[]{:S(2)}, u32[]{:S(2)}) collective-permute-start(bf16[2,6,16,256]{3,2,1,0:T(8,128)(2,1)S(1)} %get-tuple-element.25), channel_id=1, source_target_pairs={{0,256},{128,384},{256,0},{384,128},{1,257},{129,385},{257,1},{385... | collective-permute-start | bytes 294920 | tf_op jit(solution)/shard_map/ppermute | solution.py:250
  31.4 7.1 %collective-permute-start.1 = (bf16[2,6,16,256]{3,2,1,0:T(8,128)(2,1)S(1)}, bf16[2,6,16,256]{3,2,1,0:T(8,128)(2,1)S(1)}, u32[]{:S(2)}, u32[]{:S(2)}) collective-permute-start(bf16[2,6,16,256]{3,2,1,0:T(8,128)(2,1)S(1)} %get-tuple-element.26), channel_id=1, source_target_pairs={{0,128},{128,256},{256,384},{384,0},{1,129},{129,257},{257,385},{3... | collective-permute-start | bytes 294920 | tf_op jit(solution)/shard_map/ppermute | solution.py:250
  38.7 21.7 %collective-permute-start.5 = (bf16[4,2,6,16,128]{4,3,2,1,0:T(8,128)(2,1)S(1)}, bf16[4,2,6,16,128]{4,3,2,1,0:T(8,128)(2,1)S(1)}, u32[]{:S(2)}, u32[]{:S(2)}) collective-permute-start(bf16[4,2,6,16,128]{4,3,2,1,0:T(8,128)(2,1)S(1)} %get-tuple-element.21), channel_id=1, source_target_pairs={{1,0},{2,1},{3,2},{4,3},{5,4},{6,5},{7,6},{8,7},{9,8},{10,9},{11,1... | collective-permute-start | bytes 589832 | tf_op jit(solution)/shard_map/ppermute | solution.py:255
  40.0 20.5 %collective-permute-start.4 = (bf16[4,2,6,16,128]{4,3,2,1,0:T(8,128)(2,1)S(1)}, bf16[4,2,6,16,128]{4,3,2,1,0:T(8,128)(2,1)S(1)}, u32[]{:S(2)}, u32[]{:S(2)}) collective-permute-start(bf16[4,2,6,16,128]{4,3,2,1,0:T(8,128)(2,1)S(1)} %get-tuple-element.22), channel_id=1, source_target_pairs={{0,1},{1,2},{2,3},{3,4},{4,5},{5,6},{6,7},{7,8},{8,9},{9,10},{10,1... | collective-permute-start | bytes 589832 | tf_op jit(solution)/shard_map/ppermute | solution.py:254
  48.5 12.7 %all-to-all-start.1 = ((f32[8,1,128]{2,1,0:T(1,128)}), f32[8,1,128]{2,1,0:T(1,128)S(1)}, u32[]{:S(2)}, u32[]{:S(2)}) async-start(f32[8,1,128]{2,1,0:T(1,128)} %broadcast_in_dim.26), calls=%async_computation.1 | async-start | bytes 8192 | tf_op jit(solution)/shard_map/all_to_all | solution.py:266
  58.5 4.8 %collective-permute-start.6 = (bf16[28,64,256]{2,1,0:T(8,128)(2,1)S(1)}, bf16[28,64,256]{2,1,0:T(8,128)(2,1)S(1)}, u32[]{:S(2)}, u32[]{:S(2)}) collective-permute-start(bf16[28,64,256]{2,1,0:T(8,128)(2,1)S(1)} %bitcast.25), channel_id=1, source_target_pairs={{0,64},{64,0},{1,65},{65,1},{2,66},{66,2},{3,67},{67,3},{4,68},{68... | collective-permute-start | bytes 2752520 | tf_op jit(solution)/shard_map/ppermute | solution.py:268
  66.3 12.7 %all-to-all-start.2 = ((f16[4,8,32,256]{3,2,1,0:T(8,128)(2,1)}), f16[4,8,32,256]{3,2,1,0:T(8,128)(2,1)S(1)}, u32[]{:S(2)}, u32[]{:S(2)}) async-start(f16[4,8,32,256]{3,2,1,0:T(8,128)(2,1)} %convert_element_type.13), calls=%async_computation.2 | async-start | bytes 1048576 | tf_op jit(solution)/shard_map/all_to_all | solution.py:306

commit v5 on v4

--- a/solution.py
+++ b/solution.py
@@ -27,6 +27,16 @@
     count = lax.axis_size(axis)
     copies = jnp.broadcast_to(block[None], (count,) + block.shape)
     return lax.all_to_all(copies, axis, 0, 0, tiled=True)
+
+
+def exact_dot(value, chosen):
+    high = value.astype(jnp.bfloat16)
+    rest = value - high.astype(jnp.float32)
+    middle = rest.astype(jnp.bfloat16)
+    low = (rest - middle.astype(jnp.float32)).astype(jnp.bfloat16)
+    total = jnp.dot(low, chosen, preferred_element_type=jnp.float32)
+    total = total + jnp.dot(middle, chosen, preferred_element_type=jnp.float32)
+    return total + jnp.dot(high, chosen, preferred_element_type=jnp.float32)
 
 
 def payload_kernel(features, conv, skip, lengths, copies, planes, taps, skips, valid, rows, done):
@@ -49,9 +59,7 @@
     rows[count : count + 1, :] = jnp.sum(
         jnp.where(pick, skips[...].astype(jnp.float32), 0.0), axis=0, keepdims=True
     )
-    group = lax.broadcasted_iota(jnp.int32, (channels, 128), 0) // (channels // GROUPS)
-    lane = lax.broadcasted_iota(jnp.int32, (channels, 128), 1)
-    sums = jnp.zeros((1, 128), jnp.float32)
+    lines = []
     for video in range(VIDEOS):
         linear = jnp.zeros((1, channels), jnp.float32)
         square = jnp.zeros((1, channels), jnp.float32)
@@ -60,11 +68,14 @@
             shown = (span * FRAMES + frame < valid[video]).astype(jnp.float32)
             linear += jnp.sum(block, axis=0, keepdims=True) * shown
             square += jnp.sum(block * block, axis=0, keepdims=True) * shown
-        for which, value in ((video, linear), (VIDEOS + video, square)):
-            chosen = (lane == group + which * GROUPS).astype(jnp.float32)
-            sums += jnp.dot(
-                value, chosen, precision=lax.Precision.HIGHEST, preferred_element_type=jnp.float32
-            )
+        lines += [(video, linear), (VIDEOS + video, square)]
+    lines = jnp.concatenate([line for _, line in sorted(lines, key=lambda pair: pair[0])], axis=0)
+    group = lax.broadcasted_iota(jnp.int32, (channels, 128), 0) // (channels // GROUPS)
+    lane = lax.broadcasted_iota(jnp.int32, (channels, 128), 1)
+    spots = exact_dot(lines, (lane % GROUPS == group).astype(jnp.bfloat16))
+    line = lax.broadcasted_iota(jnp.int32, spots.shape, 0)
+    lane = lax.broadcasted_iota(jnp.int32, spots.shape, 1)
+    sums = jnp.sum(jnp.where(lane // GROUPS == line, spots, 0.0), axis=0, keepdims=True)
     high = sums.astype(jnp.bfloat16).astype(jnp.float32)
     middle = (sums - high).astype(jnp.bfloat16).astype(jnp.float32)
     rows[count + 1 : count + 2, 0:128] = high
@@ -73,6 +84,14 @@
     value = rows[...].astype(jnp.bfloat16)
     for index in range(copies.shape[0]):
         copies[index] = value
+
+
+def sums_kernel(arrived, copies, *, first):
+    at = first // 16 * 16
+    rows = jnp.sum(arrived[:, at : at + 16, :].astype(jnp.float32), axis=0)
+    rows = rows[first - at : first - at + 2]
+    total = rows[1:2, 0:128] + rows[0:1, 128:256] + rows[0:1, 0:128]
+    copies[...] = jnp.broadcast_to(total[None], copies.shape)
 
 
 def member_kernel(features, shares, tails):
@@ -103,25 +122,21 @@
     for span in range(1, SPANS):
         summed.append(summed[-1] + totals[span : span + 1, :])
     summed = jnp.concatenate(summed, axis=0)
-    entry = lax.broadcasted_iota(jnp.int32, (128, PART), 0)
-    group = lax.broadcasted_iota(jnp.int32, (128, PART), 1) % SHARE // 2
+    entry = lax.broadcasted_iota(jnp.int32, (128, 4 * PART), 0)
+    lane = lax.broadcasted_iota(jnp.int32, (128, 4 * PART), 1)
+    wanted = lane // PART * GROUPS + lane % SHARE // 2
+    spread = exact_dot(summed, (entry == wanted).astype(jnp.bfloat16))
     ends = (lax.broadcasted_iota(jnp.int32, (SPANS, PART), 0) + 1) * FRAMES
-
-    def spread(which):
-        chosen = (entry == group + which * GROUPS).astype(jnp.float32)
-        return jnp.dot(
-            summed, chosen, precision=lax.Precision.HIGHEST, preferred_element_type=jnp.float32
-        )
 
     ratio = jnp.zeros((SPANS, PART), jnp.float32)
     largest = jnp.zeros((SPANS, PART), jnp.float32)
     for video in range(VIDEOS):
         seen = jnp.minimum(ends, lengths[video]).astype(jnp.float32) * cells
-        square = spread(VIDEOS + video)
-        centre = spread(video) / seen
+        square = spread[:, (VIDEOS + video) * PART : (VIDEOS + video + 1) * PART]
+        centre = spread[:, video * PART : (video + 1) * PART] / seen
         inverse = lax.rsqrt(square / seen - centre * centre + EPS)
         moments[2 * video] = centre
-        moments[2 * video + 1] = inverse * gain[...]
+        moments[2 * video + 1] = 0.5 * inverse * gain[...]
         size = jnp.sqrt(square)
         ratio = jnp.maximum(ratio, size * inverse)
         largest = jnp.maximum(largest, size)
@@ -129,15 +144,14 @@
     bound = bound + skip_bound * jnp.max(largest, keepdims=True)
     factor[...] = jnp.broadcast_to(jnp.exp2(14.0 - jnp.floor(jnp.log2(bound))), factor.shape)
 
-    offset = bias[...].reshape(1, 1, PART)
-
     def normed(value, video, span, first):
+        frame = lax.broadcasted_iota(jnp.int32, (value.shape[0], 1, PART), 0) + first
+        shown = frame < lengths[video]
         centre = moments[2 * video, pl.ds(span, 1)].reshape(1, 1, PART)
-        scale = moments[2 * video + 1, pl.ds(span, 1)].reshape(1, 1, PART)
-        shown = lax.broadcasted_iota(jnp.int32, value.shape, 0) + first < lengths[video]
+        scale = jnp.where(shown, moments[2 * video + 1, pl.ds(span, 1)].reshape(1, 1, PART), 0.0)
+        offset = jnp.where(shown, 0.5 * bias[...].reshape(1, 1, PART), 0.0)
         value = (value.astype(jnp.float32) - centre) * scale + offset
-        value = value / (1.0 + jnp.exp(-value))
-        return jnp.where(shown, value, 0.0)
+        return value + value * jnp.tanh(value)
 
     for step in range(CHIPS):
         span = lax.rem(chip - step + CHIPS, CHIPS) * 2 + core
@@ -206,7 +220,7 @@
     tiles, chips = lax.axis_size(TILE), lax.axis_size("x")
     taps = conv_in.shape[1]
     on_chip = pl.BlockSpec(memory_space=pltpu.VMEM)
-    anywhere = pl.BlockSpec(memory_space=pl.ANY)
+    outside = pl.BlockSpec(memory_space=pl.ANY)
     scalar = pl.BlockSpec(memory_space=pltpu.SMEM)
     params = pltpu.CompilerParams(vmem_limit_bytes=20 * 1024 * 1024)
 
@@ -214,7 +228,7 @@
     copies = pl.pallas_call(
         payload_kernel,
         out_shape=jax.ShapeDtypeStruct((tiles, 32, OUT), jnp.bfloat16),
-        in_specs=[anywhere] * 4,
+        in_specs=[outside] * 4,
         out_specs=on_chip,
         scratch_shapes=[
             pltpu.VMEM(planes.shape, jnp.bfloat16),
@@ -224,9 +238,14 @@
             pltpu.VMEM((32, OUT), jnp.float32),
             pltpu.SemaphoreType.DMA((4,)),
         ],
-        compiler_params=pltpu.CompilerParams(vmem_limit_bytes=63 * 1024 * 1024),
+        compiler_params=params,
         name="payload",
-    )(planes, conv_in.transpose(1, 0, 2), skip_weight, lengths)
+    )(
+        *[
+            pltpu.with_memory_space_constraint(value, pltpu.HBM)
+            for value in (planes, conv_in.transpose(1, 0, 2), skip_weight, lengths)
+        ]
+    )
     arrived = lax.all_to_all(copies, TILE, 0, 0, tiled=True)
 
     shape = (chips, videos, frames, col_count, 2 * PART)
@@ -258,11 +277,16 @@
         own = lax.dynamic_slice_in_dim(vector.reshape(SHARE, SPANS), 2 * chip, 2, axis=1)
         return own.T.reshape(1, PART)
 
-    parts = jnp.sum(arrived[:, taps + 1 : taps + 3].astype(jnp.float32), axis=0)
-    sums = parts[:1, :128] + parts[:1, 128:] + parts[1:, :128]
     gain, bias = lanes(gain_in), lanes(bias_in)
-    sums, upper, lower, gain, bias = lax.optimization_barrier((sums, upper, lower, gain, bias))
-    copies = jnp.broadcast_to(sums[None], (SPANS,) + sums.shape)
+    held, upper, lower, gain, bias = lax.optimization_barrier((arrived, upper, lower, gain, bias))
+    copies = pl.pallas_call(
+        functools.partial(sums_kernel, first=taps + 1),
+        out_shape=jax.ShapeDtypeStruct((SPANS, 1, 128), jnp.float32),
+        in_specs=[on_chip],
+        out_specs=on_chip,
+        compiler_params=params,
+        name="sums",
+    )(pltpu.with_memory_space_constraint(held, pltpu.VMEM))
     totals = lax.all_to_all(copies, TM, 0, 0, tiled=True).reshape(SPANS, -1)
     mine = arrived[:, : taps + 1].transpose(1, 0, 2)
     theirs = lax.ppermute(mine, "core", swap)

time: 81.3 us -> 79 us (0.972)
  local copies, waits for them, and re-layouts: 3.05 us -> 1.23 us
  waiting for transfers between devices: 17.5 us -> 18.8 us
  other arithmetic: 2.95 us -> 1.89 us
    all_to_all x1, waiting for transfers between devices: 0.81 us -> 2.04 us  [per_device(): totals = lax.all_to_all(copies, TM, 0, 0, tiled=True).reshape(SPANS, -1)]
    unnamed x10, local copies, waits for them, and re-layouts: 1.77 us -> 0.55 us
    reduce_sum x1 -> x0, other arithmetic: 1.07 us -> none  [per_device(): parts = jnp.sum(arrived[:, taps + 1:taps + 3].astype(jnp.float32), axis=0)]
  transfers between devices with their start and end apart: 10 -> 10, of which waited for: 6 -> 6; matrix products, arithmetic and copies ran while one was open for 5% -> 2% of each run, Pallas kernels for 3% -> 3%
where the time goes in v5:
time: 79 us; the launch traced here: 77.6 us
  starting transfers between devices  48.2 us (61%)
  waiting for transfers between devices  18.8 us (24%)
  Pallas kernels  7.22 us (9%)
  other arithmetic  1.89 us (2%)
  local copies, waits for them, and re-layouts  1.23 us (2%)
    all_to_all x1, starting transfers between devices, per_device(): arrived = lax.all_to_all(copies, TILE, 0, 0, tiled=True)  17.1 us
    ppermute x3, starting transfers between devices, per_device(): lax.ppermute(block, 'x', [(i, (i + step) % chips) for i in range(chips)])  9.33 us
    all_to_all x1, waiting for transfers between devices, per_device(): total = lax.all_to_all(total, 'x', 0, 0, tiled=True)  8.77 us
    all_to_all x1, starting transfers between devices, per_device(): totals = lax.all_to_all(copies, TM, 0, 0, tiled=True).reshape(SPANS, -1)  8.18 us
    ppermute x3, waiting for transfers between devices, per_device(): lax.ppermute(block, 'x', [(i, (i + step) % chips) for i in range(chips)])  4.47 us
    ppermute x1, starting transfers between devices, per_device(): above = lax.ppermute(upper, TILE, [(i, i + 1) for i in range(tiles - 1)])  4 us
    all_to_all x1, starting transfers between devices, per_device(): total = lax.all_to_all(total, 'x', 0, 0, tiled=True)  3.47 us
    ppermute x1, starting transfers between devices, per_device(): lax.ppermute(tails, 'core', swap)  2.87 us
  transfers between devices with their start and end apart: 10, of which 6 were waited for; matrix products, arithmetic and copies ran while one was open for 2% of the time, Pallas kernels for 3%

profile of v5, /device:TPU:1, one launch (start us, length us, event | category | flops | bytes accessed | tf_op | source)
XLA Modules:
  0.0 77.6 jit_solution(9800463642559598216)
XLA Ops:
  0.0 2.5 %payload.1 = bf16[64,32,256]{2,1,0:T(8,128)(2,1)} custom-call(bf16[8,32,512]{2,1,0:T(8,128)(2,1)} %bitcast.23, bf16[27,8,256]{2,1,0:T(8,128)(2,1)} %bitcast.30, bf16[8,256]{1,0:T(8,128)(2,1)} %skip.1, s32[2]{0:T(128)} %lengths.3), custom_call_target="tpu_custom_call" | custom-call | tf_op jit(solution)/shard_map/payload/pallas_call | solution.py:228
  2.5 17.1 %all-to-all-start = ((bf16[64,32,256]{2,1,0:T(8,128)(2,1)}), bf16[64,32,256]{2,1,0:T(8,128)(2,1)S(1)}, u32[]{:S(2)}, u32[]{:S(2)}) async-start(bf16[64,32,256]{2,1,0:T(8,128)(2,1)} %payload.1), calls=%async_computation | async-start | bytes 2097152 | tf_op jit(solution)/shard_map/all_to_all | solution.py:249
  19.7 0.4 member_shares.1
  20.0 2.9 %collective-permute-start = (bf16[4,2,2,16,256]{4,3,2,1,0:T(8,128)(2,1)S(1)}, bf16[4,2,2,16,256]{4,3,2,1,0:T(8,128)(2,1)S(1)}, u32[]{:S(2)}, u32[]{:S(2)}) collective-permute-start(bf16[4,2,2,16,256]{4,3,2,1,0:T(8,128)(2,1)S(1)} %get-tuple-element.14), channel_id=1, source_target_pairs={{0,64},{64,0},{1,65},{65,1},{2,66},{66,2},{3,67},{67,3},{4,68},{68... | collective-permute-start | bytes 393224 | tf_op jit(solution)/shard_map/ppermute | solution.py:264
  22.9 0.9 %collective-permute-done = bf16[4,2,2,16,256]{4,3,2,1,0:T(8,128)(2,1)S(1)} collective-permute-done((bf16[4,2,2,16,256]{4,3,2,1,0:T(8,128)(2,1)S(1)}, bf16[4,2,2,16,256]{4,3,2,1,0:T(8,128)(2,1)S(1)}, u32[]{:S(2)}, u32[]{:S(2)}) %collective-permute-start) | collective-permute-done | bytes 131104 | tf_op jit(solution)/shard_map/ppermute | solution.py:264
  23.9 4.4 %collective-permute-start.3 = (bf16[2,6,16,256]{3,2,1,0:T(8,128)(2,1)S(1)}, bf16[2,6,16,256]{3,2,1,0:T(8,128)(2,1)S(1)}, u32[]{:S(2)}, u32[]{:S(2)}) collective-permute-start(bf16[2,6,16,256]{3,2,1,0:T(8,128)(2,1)S(1)} %get-tuple-element.24), channel_id=1, source_target_pairs={{0,384},{128,0},{256,128},{384,256},{1,385},{129,1},{257,129},{385... | collective-permute-start | bytes 294920 | tf_op jit(solution)/shard_map/ppermute | solution.py:269
  28.3 2.4 %collective-permute-start.2 = (bf16[2,6,16,256]{3,2,1,0:T(8,128)(2,1)S(1)}, bf16[2,6,16,256]{3,2,1,0:T(8,128)(2,1)S(1)}, u32[]{:S(2)}, u32[]{:S(2)}) collective-permute-start(bf16[2,6,16,256]{3,2,1,0:T(8,128)(2,1)S(1)} %get-tuple-element.25), channel_id=1, source_target_pairs={{0,256},{128,384},{256,0},{384,128},{1,257},{129,385},{257,1},{385... | collective-permute-start | bytes 294920 | tf_op jit(solution)/shard_map/ppermute | solution.py:269
  30.7 2.5 %collective-permute-start.1 = (bf16[2,6,16,256]{3,2,1,0:T(8,128)(2,1)S(1)}, bf16[2,6,16,256]{3,2,1,0:T(8,128)(2,1)S(1)}, u32[]{:S(2)}, u32[]{:S(2)}) collective-permute-start(bf16[2,6,16,256]{3,2,1,0:T(8,128)(2,1)S(1)} %get-tuple-element.26), channel_id=1, source_target_pairs={{0,128},{128,256},{256,384},{384,0},{1,129},{129,257},{257,385},{3... | collective-permute-start | bytes 294920 | tf_op jit(solution)/shard_map/ppermute | solution.py:269
  33.3 2.2 %collective-permute-done.2 = bf16[2,6,16,256]{3,2,1,0:T(8,128)(2,1)S(1)} collective-permute-done((bf16[2,6,16,256]{3,2,1,0:T(8,128)(2,1)S(1)}, bf16[2,6,16,256]{3,2,1,0:T(8,128)(2,1)S(1)}, u32[]{:S(2)}, u32[]{:S(2)}) %collective-permute-start.2) | collective-permute-done | bytes 98336 | tf_op jit(solution)/shard_map/ppermute | solution.py:269
  35.5 2.3 %collective-permute-done.1 = bf16[2,6,16,256]{3,2,1,0:T(8,128)(2,1)S(1)} collective-permute-done((bf16[2,6,16,256]{3,2,1,0:T(8,128)(2,1)S(1)}, bf16[2,6,16,256]{3,2,1,0:T(8,128)(2,1)S(1)}, u32[]{:S(2)}, u32[]{:S(2)}) %collective-permute-start.1) | collective-permute-done | bytes 98336 | tf_op jit(solution)/shard_map/ppermute | solution.py:269
  37.9 1.3 %collective-permute-start.5 = (bf16[4,2,6,16,128]{4,3,2,1,0:T(8,128)(2,1)S(1)}, bf16[4,2,6,16,128]{4,3,2,1,0:T(8,128)(2,1)S(1)}, u32[]{:S(2)}, u32[]{:S(2)}) collective-permute-start(bf16[4,2,6,16,128]{4,3,2,1,0:T(8,128)(2,1)S(1)} %get-tuple-element.21), channel_id=1, source_target_pairs={{1,0},{2,1},{3,2},{4,3},{5,4},{6,5},{7,6},{8,7},{9,8},{10,9},{11,1... | collective-permute-start | bytes 589832 | tf_op jit(solution)/shard_map/ppermute | solution.py:274
  39.2 4.0 %collective-permute-start.4 = (bf16[4,2,6,16,128]{4,3,2,1,0:T(8,128)(2,1)S(1)}, bf16[4,2,6,16,128]{4,3,2,1,0:T(8,128)(2,1)S(1)}, u32[]{:S(2)}, u32[]{:S(2)}) collective-permute-start(bf16[4,2,6,16,128]{4,3,2,1,0:T(8,128)(2,1)S(1)} %get-tuple-element.22), channel_id=1, source_target_pairs={{0,1},{1,2},{2,3},{3,4},{4,5},{5,6},{6,7},{7,8},{8,9},{9,10},{10,1... | collective-permute-start | bytes 589832 | tf_op jit(solution)/shard_map/ppermute | solution.py:273
  43.2 0.1 reshape.54
  43.3 0.1 reshape.56
  43.4 0.1 dynamic-slice_bitcast_fusion.3
  43.5 0.1 copy.16
  43.5 0.1 reshape.57.bias
  43.7 0.1 reshape.55.gain
  43.8 2.6 %all-to-all-done.arrived = bf16[64,32,256]{2,1,0:T(8,128)(2,1)S(1)} async-done(((bf16[64,32,256]{2,1,0:T(8,128)(2,1)}), bf16[64,32,256]{2,1,0:T(8,128)(2,1)S(1)}, u32[]{:S(2)}, u32[]{:S(2)}) %all-to-all-start) | async-done | bytes 1048608 | tf_op jit(solution)/shard_map/all_to_all | solution.py:249
  46.4 0.7 sums.1
  47.0 8.2 %all-to-all-start.1 = ((f32[8,1,128]{2,1,0:T(1,128)}), f32[8,1,128]{2,1,0:T(1,128)S(1)}, u32[]{:S(2)}, u32[]{:S(2)}) async-start(f32[8,1,128]{2,1,0:T(1,128)} %sums.1), calls=%async_computation.1 | async-start | bytes 8192 | tf_op jit(solution)/shard_map/all_to_all | solution.py:290
  55.2 0.5 copy.20
  55.7 1.9 %collective-permute-start.6 = (bf16[28,64,256]{2,1,0:T(8,128)(2,1)S(1)}, bf16[28,64,256]{2,1,0:T(8,128)(2,1)S(1)}, u32[]{:S(2)}, u32[]{:S(2)}) collective-permute-start(bf16[28,64,256]{2,1,0:T(8,128)(2,1)S(1)} %bitcast.25), channel_id=1, source_target_pairs={{0,64},{64,0},{1,65},{65,1},{2,66},{66,2},{3,67},{67,3},{4,68},{68... | collective-permute-start | bytes 2752520 | tf_op jit(solution)/shard_map/ppermute | solution.py:292
  57.7 2.0 %all-to-all-done.1 = f32[8,1,128]{2,1,0:T(1,128)S(1)} async-done(((f32[8,1,128]{2,1,0:T(1,128)}), f32[8,1,128]{2,1,0:T(1,128)S(1)}, u32[]{:S(2)}, u32[]{:S(2)}) %all-to-all-start.1) | async-done | bytes 4128 | tf_op jit(solution)/shard_map/all_to_all | solution.py:290
  59.7 1.6 %norm.1 = (bf16[3,4,2,6,16,512]{5,4,3,2,1,0:T(8,128)(2,1)S(1)}, bf16[4,2,4,16,256]{4,3,2,1,0:T(8,128)(2,1)S(1)}, f32[1,256]{1,0:T(1,128)S(1)}) custom-call(s32[2]{0:T(128)S(1)} %copy-done.1, f32[8,128]{1,0:T(8,128)S(1)} %bitcast.27, f32[1,128]{1,0:T(1,128)S(1)} %reshape.55.gain, f32[1,128]{1,0:T(1,128)S(1)} %reshape.57.bias, ...), custom_call_target="tpu_custom_call" | custom-call | flops 17179869184 | bytes 67108864 | tf_op jit(solution)/shard_map/norm/pallas_call | solution.py:294
  61.4 2.1 %taps.1 = f32[4,8,32,256]{3,2,1,0:T(8,128)S(1)} custom-call(bf16[3,4,2,6,16,512]{5,4,3,2,1,0:T(8,128)(2,1)S(1)} %get-tuple-element.18.shifted, bf16[4,2,4,16,256]{4,3,2,1,0:T(8,128)(2,1)S(1)} %get-tuple-element.19.raw, f32[1,256]{1,0:T(1,128)S(1)} %get-tuple-element.20.factor, bf16[28,64,256]{2,1,0:T(8,128)(2,1)S(1)} %bitcast.26, ...), custom_call_target="tpu_custom_call" | custom-call | flops 1879048192 | bytes 6291456 | tf_op jit(solution)/shard_map/taps/pallas_call | solution.py:316
  63.5 0.9 %convert_element_type.9 = f16[4,8,32,256]{3,2,1,0:T(8,128)(2,1)} convert(f32[4,8,32,256]{3,2,1,0:T(8,128)S(1)} %taps.1) | non-fusion elementwise | flops 262144 | bytes 1572864 | tf_op jit(solution)/shard_map/convert_element_type | solution.py:329
  64.4 3.5 %all-to-all-start.2 = ((f16[4,8,32,256]{3,2,1,0:T(8,128)(2,1)}), f16[4,8,32,256]{3,2,1,0:T(8,128)(2,1)S(1)}, u32[]{:S(2)}, u32[]{:S(2)}) async-start(f16[4,8,32,256]{3,2,1,0:T(8,128)(2,1)} %convert_element_type.9), calls=%async_computation.2 | async-start | bytes 1048576 | tf_op jit(solution)/shard_map/all_to_all | solution.py:330
  67.9 0.1 broadcast_compare_fusion
  68.0 8.8 %all-to-all-done.2 = f16[4,8,32,256]{3,2,1,0:T(8,128)(2,1)S(1)} async-done(((f16[4,8,32,256]{3,2,1,0:T(8,128)(2,1)}), f16[4,8,32,256]{3,2,1,0:T(8,128)(2,1)S(1)}, u32[]{:S(2)}, u32[]{:S(2)}) %all-to-all-start.2) | async-done | bytes 524320 | tf_op jit(solution)/shard_map/all_to_all | solution.py:330
  76.7 0.1 convert_reduce_fusion
  76.8 0.7 select_convert_fusion
  (19 shorter events, 0.3 us)
Async XLA Ops:
  0.0 19.6 %copy-start = (bf16[2,4,2,16,512]{4,3,2,1,0:T(8,128)(2,1)S(1)}, bf16[2,4,2,16,512]{4,3,2,1,0:T(8,128)(2,1)}, u32[]{:S(2)}) copy-start(bf16[2,4,2,16,512]{4,3,2,1,0:T(8,128)(2,1)} %param.6) | copy-start | bytes 786436
  2.5 40.7 %copy-start.2 = (f32[512]{0:T(512)S(1)}, f32[512]{0:T(512)}, u32[]{:S(2)}) copy-start(f32[512]{0:T(512)} %param.8) | copy-start | bytes 6148
  2.5 40.8 %copy-start.3 = (f32[512]{0:T(512)S(1)}, f32[512]{0:T(512)}, u32[]{:S(2)}) copy-start(f32[512]{0:T(512)} %param.9) | copy-start | bytes 6148
  2.5 43.9 %all-to-all-start = ((bf16[64,32,256]{2,1,0:T(8,128)(2,1)}), bf16[64,32,256]{2,1,0:T(8,128)(2,1)S(1)}, u32[]{:S(2)}, u32[]{:S(2)}) async-start(bf16[64,32,256]{2,1,0:T(8,128)(2,1)} %payload.1), calls=%async_computation | async-start | bytes 2097152 | tf_op jit(solution)/shard_map/all_to_all | solution.py:249
  20.0 3.8 %collective-permute-start = (bf16[4,2,2,16,256]{4,3,2,1,0:T(8,128)(2,1)S(1)}, bf16[4,2,2,16,256]{4,3,2,1,0:T(8,128)(2,1)S(1)}, u32[]{:S(2)}, u32[]{:S(2)}) collective-permute-start(bf16[4,2,2,16,256]{4,3,2,1,0:T(8,128)(2,1)S(1)} %get-tuple-element.14), channel_id=1, source_target_pairs={{0,64},{64,0},{1,65},{65,1},{2,66},{66,2},{3,67},{67,3},{4,68},{68... | collective-permute-start | bytes 393224 | tf_op jit(solution)/shard_map/ppermute | solution.py:264
  23.9 9.4 %collective-permute-start.3 = (bf16[2,6,16,256]{3,2,1,0:T(8,128)(2,1)S(1)}, bf16[2,6,16,256]{3,2,1,0:T(8,128)(2,1)S(1)}, u32[]{:S(2)}, u32[]{:S(2)}) collective-permute-start(bf16[2,6,16,256]{3,2,1,0:T(8,128)(2,1)S(1)} %get-tuple-element.24), channel_id=1, source_target_pairs={{0,384},{128,0},{256,128},{384,256},{1,385},{129,1},{257,129},{385... | collective-permute-start | bytes 294920 | tf_op jit(solution)/shard_map/ppermute | solution.py:269
  28.3 7.2 %collective-permute-start.2 = (bf16[2,6,16,256]{3,2,1,0:T(8,128)(2,1)S(1)}, bf16[2,6,16,256]{3,2,1,0:T(8,128)(2,1)S(1)}, u32[]{:S(2)}, u32[]{:S(2)}) collective-permute-start(bf16[2,6,16,256]{3,2,1,0:T(8,128)(2,1)S(1)} %get-tuple-element.25), channel_id=1, source_target_pairs={{0,256},{128,384},{256,0},{384,128},{1,257},{129,385},{257,1},{385... | collective-permute-start | bytes 294920 | tf_op jit(solution)/shard_map/ppermute | solution.py:269
  30.7 7.0 %collective-permute-start.1 = (bf16[2,6,16,256]{3,2,1,0:T(8,128)(2,1)S(1)}, bf16[2,6,16,256]{3,2,1,0:T(8,128)(2,1)S(1)}, u32[]{:S(2)}, u32[]{:S(2)}) collective-permute-start(bf16[2,6,16,256]{3,2,1,0:T(8,128)(2,1)S(1)} %get-tuple-element.26), channel_id=1, source_target_pairs={{0,128},{128,256},{256,384},{384,0},{1,129},{129,257},{257,385},{3... | collective-permute-start | bytes 294920 | tf_op jit(solution)/shard_map/ppermute | solution.py:269
  37.7 22.0 %copy-start.1 = (s32[2]{0:T(128)S(1)}, s32[2]{0:T(128)}, u32[]{:S(2)}) copy-start(s32[2]{0:T(128)} %lengths.3) | copy-start | bytes 28
  37.9 19.8 %collective-permute-start.5 = (bf16[4,2,6,16,128]{4,3,2,1,0:T(8,128)(2,1)S(1)}, bf16[4,2,6,16,128]{4,3,2,1,0:T(8,128)(2,1)S(1)}, u32[]{:S(2)}, u32[]{:S(2)}) collective-permute-start(bf16[4,2,6,16,128]{4,3,2,1,0:T(8,128)(2,1)S(1)} %get-tuple-element.21), channel_id=1, source_target_pairs={{1,0},{2,1},{3,2},{4,3},{5,4},{6,5},{7,6},{8,7},{9,8},{10,9},{11,1... | collective-permute-start | bytes 589832 | tf_op jit(solution)/shard_map/ppermute | solution.py:274
  39.2 18.5 %collective-permute-start.4 = (bf16[4,2,6,16,128]{4,3,2,1,0:T(8,128)(2,1)S(1)}, bf16[4,2,6,16,128]{4,3,2,1,0:T(8,128)(2,1)S(1)}, u32[]{:S(2)}, u32[]{:S(2)}) collective-permute-start(bf16[4,2,6,16,128]{4,3,2,1,0:T(8,128)(2,1)S(1)} %get-tuple-element.22), channel_id=1, source_target_pairs={{0,1},{1,2},{2,3},{3,4},{4,5},{5,6},{6,7},{7,8},{8,9},{9,10},{10,1... | collective-permute-start | bytes 589832 | tf_op jit(solution)/shard_map/ppermute | solution.py:273
  47.0 12.7 %all-to-all-start.1 = ((f32[8,1,128]{2,1,0:T(1,128)}), f32[8,1,128]{2,1,0:T(1,128)S(1)}, u32[]{:S(2)}, u32[]{:S(2)}) async-start(f32[8,1,128]{2,1,0:T(1,128)} %sums.1), calls=%async_computation.1 | async-start | bytes 8192 | tf_op jit(solution)/shard_map/all_to_all | solution.py:290
  55.7 5.6 %collective-permute-start.6 = (bf16[28,64,256]{2,1,0:T(8,128)(2,1)S(1)}, bf16[28,64,256]{2,1,0:T(8,128)(2,1)S(1)}, u32[]{:S(2)}, u32[]{:S(2)}) collective-permute-start(bf16[28,64,256]{2,1,0:T(8,128)(2,1)S(1)} %bitcast.25), channel_id=1, source_target_pairs={{0,64},{64,0},{1,65},{65,1},{2,66},{66,2},{3,67},{67,3},{4,68},{68... | collective-permute-start | bytes 2752520 | tf_op jit(solution)/shard_map/ppermute | solution.py:292
  64.4 12.3 %all-to-all-start.2 = ((f16[4,8,32,256]{3,2,1,0:T(8,128)(2,1)}), f16[4,8,32,256]{3,2,1,0:T(8,128)(2,1)S(1)}, u32[]{:S(2)}, u32[]{:S(2)}) async-start(f16[4,8,32,256]{3,2,1,0:T(8,128)(2,1)} %convert_element_type.9), calls=%async_computation.2 | async-start | bytes 1048576 | tf_op jit(solution)/shard_map/all_to_all | solution.py:330

commit v6 on v5

v6 whole, which is shorter than its diff:
```python
import functools

import jax
import jax.numpy as jnp
from jax import lax
from jax.experimental import pallas as pl
from jax.experimental.pallas import tpu as pltpu
from jax.sharding import Mesh
from jax.sharding import PartitionSpec as P

GROUPS = 32
EPS = 1e-06
TM = ("x", "core")
TILE = ("y", "z")
SPANS = 8
VIDEOS = 2
FRAMES = 4
COLS = 16
SHARE = 64
CHIPS = 4
PART = 2 * SHARE
ROWS = 4
LINE = 15
OUT = 256


def to_all(block, axis):
    count = lax.axis_size(axis)
    copies = jnp.broadcast_to(block[None], (count,) + block.shape)
    return lax.all_to_all(copies, axis, 0, 0, tiled=True)


def exact_dot(value, chosen):
    high = value.astype(jnp.bfloat16)
    rest = value - high.astype(jnp.float32)
    middle = rest.astype(jnp.bfloat16)
    low = (rest - middle.astype(jnp.float32)).astype(jnp.bfloat16)
    total = jnp.dot(low, chosen, preferred_element_type=jnp.float32)
    total = total + jnp.dot(middle, chosen, preferred_element_type=jnp.float32)
    return total + jnp.dot(high, chosen, preferred_element_type=jnp.float32)


def payload_kernel(features, conv, skip, lengths, copies, planes, taps, skips, valid, rows, packed, few, done, left):
    moves = [
        pltpu.make_async_copy(source, target, done.at[index])
        for index, (source, target) in enumerate(
            ((features, planes), (conv, taps), (skip, skips), (lengths, valid))
        )
    ]
    for move in moves:
        move.start()
    for move in moves:
        move.wait()
    count, channels = taps.shape[0], planes.shape[-1]
    span = lax.axis_index(TM)
    pick = lax.broadcasted_iota(jnp.int32, (count, SPANS, OUT), 1) == span
    rows[...] = jnp.zeros_like(rows)
    rows[0:count, :] = jnp.sum(jnp.where(pick, taps[...].astype(jnp.float32), 0.0), axis=1)
    pick = lax.broadcasted_iota(jnp.int32, (SPANS, OUT), 0) == span
    rows[count : count + 1, :] = jnp.sum(
        jnp.where(pick, skips[...].astype(jnp.float32), 0.0), axis=0, keepdims=True
    )
    lines = []
    for video in range(VIDEOS):
        linear = jnp.zeros((1, channels), jnp.float32)
        square = jnp.zeros((1, channels), jnp.float32)
        for frame in range(FRAMES):
            block = planes[video * FRAMES + frame].astype(jnp.float32)
            shown = (span * FRAMES + frame < valid[video]).astype(jnp.float32)
            linear += jnp.sum(block, axis=0, keepdims=True) * shown
            square += jnp.sum(block * block, axis=0, keepdims=True) * shown
        lines += [(video, linear), (VIDEOS + video, square)]
    lines = jnp.concatenate([line for _, line in sorted(lines, key=lambda pair: pair[0])], axis=0)
    group = lax.broadcasted_iota(jnp.int32, (channels, 128), 0) // (channels // GROUPS)
    lane = lax.broadcasted_iota(jnp.int32, (channels, 128), 1)
    spots = exact_dot(lines, (lane % GROUPS == group).astype(jnp.bfloat16))
    line = lax.broadcasted_iota(jnp.int32, spots.shape, 0)
    lane = lax.broadcasted_iota(jnp.int32, spots.shape, 1)
    sums = jnp.sum(jnp.where(lane // GROUPS == line, spots, 0.0), axis=0, keepdims=True)
    high = sums.astype(jnp.bfloat16).astype(jnp.float32)
    middle = (sums - high).astype(jnp.bfloat16).astype(jnp.float32)
    rows[count + 1 : count + 2, 0:128] = high
    rows[count + 1 : count + 2, 128:256] = middle
    rows[count + 2 : count + 3, 0:128] = sums - high - middle
    for row in range(2 * LINE):
        at = row % LINE * OUT
        packed[row // LINE : row // LINE + 1, at : at + OUT] = rows[row : row + 1, :]
    value = packed[...].astype(jnp.bfloat16)
    some = few.shape[0]
    for index in range(some):
        few[index] = value
    moves = [
        pltpu.make_async_copy(few, copies.at[pl.ds(index * some, some)], left.at[index])
        for index in range(copies.shape[0] // some)
    ]
    for move in moves:
        move.start()
    for move in moves:
        move.wait()


def sums_kernel(arrived, copies, *, first):
    at = (first - LINE) * OUT
    line = jnp.sum(arrived[:, :, at : at + 2 * OUT].astype(jnp.float32), axis=0)[1:2]
    total = line[:, 256:384] + line[:, 128:256] + line[:, 0:128]
    copies[...] = jnp.broadcast_to(total[None], copies.shape)


def member_kernel(features, gain, bias, kept, sent, lanes):
    voxels, channels = features.shape[0] * COLS, features.shape[-1]
    column = lax.broadcasted_iota(jnp.int32, (channels, channels), 1)
    place = column % PART
    source = place % SHARE * SPANS + column // PART * 2 + place // SHARE
    match = lax.broadcasted_iota(jnp.int32, (channels, channels), 0) == source
    chosen = jnp.where(match, 1.0, 0.0).astype(jnp.bfloat16)
    even = lax.axis_index("core") == 0
    for row in range(2):
        block = features[:, row * COLS : (row + 1) * COLS].reshape(voxels, channels)
        flat = jnp.dot(block, chosen, preferred_element_type=jnp.float32).astype(jnp.bfloat16)
        flat = flat.reshape(VIDEOS, FRAMES, COLS, channels)
        mine, other = jnp.where(even, flat[0], flat[1]), jnp.where(even, flat[1], flat[0])
        at = slice(row * PART, (row + 1) * PART)
        for chip in range(CHIPS):
            kept[chip, :, :, at] = mine[..., chip * PART : (chip + 1) * PART]
            sent[chip, :, :, at] = other[..., chip * PART : (chip + 1) * PART]
    place = lax.broadcasted_iota(jnp.int32, (channels, PART), 1)
    source = place % SHARE * SPANS + lax.axis_index("x") * 2 + place // SHARE
    match = lax.broadcasted_iota(jnp.int32, (channels, PART), 0) == source
    pair = jnp.concatenate([gain[...], bias[...]], axis=0)
    lanes[...] = exact_dot(pair, jnp.where(match, 1.0, 0.0).astype(jnp.bfloat16))


def norm_kernel(
    lengths, totals, lanes, signal, above, below, shifted, raw, factor, moments,
    *, cells, tiles, tap_bound, skip_bound
):
    chip, core = lax.axis_index("x"), lax.axis_index("core")
    tile = lax.axis_index(TILE)
    summed = [totals[0:1, :]]
    for span in range(1, SPANS):
        summed.append(summed[-1] + totals[span : span + 1, :])
    summed = jnp.concatenate(summed, axis=0)
    entry = lax.broadcasted_iota(jnp.int32, (128, 4 * PART), 0)
    lane = lax.broadcasted_iota(jnp.int32, (128, 4 * PART), 1)
    wanted = lane // PART * GROUPS + lane % SHARE // 2
    spread = exact_dot(summed, jnp.where(entry == wanted, 1.0, 0.0).astype(jnp.bfloat16))
    ends = (lax.broadcasted_iota(jnp.int32, (SPANS, PART), 0) + 1) * FRAMES
    for video in range(VIDEOS):
        seen = jnp.minimum(ends, lengths[video]).astype(jnp.float32) * cells
        square = spread[:, (VIDEOS + video) * PART : (VIDEOS + video + 1) * PART]
        centre = spread[:, video * PART : (video + 1) * PART] / seen
        inverse = lax.rsqrt(square / seen - centre * centre + EPS)
        moments[2 * video] = centre
        moments[2 * video + 1] = 0.5 * inverse * lanes[0:1, :]
        size = jnp.sqrt(square)
        bound = tap_bound * (3.0 * jnp.max(size * inverse, keepdims=True) + 3.0)
        bound = bound + skip_bound * jnp.max(size, keepdims=True)
        bound = jnp.exp2(14.0 - jnp.floor(jnp.log2(bound)))
        factor[video : video + 1, :] = jnp.broadcast_to(bound, (1, OUT))
    half_bias = 0.5 * lanes[1:2, :]

    def normed(value, span):
        frame = lax.broadcasted_iota(jnp.int32, (FRAMES, 1, PART), 0) + span * FRAMES
        shown = frame < lengths[core]
        centre = moments[2 * core, pl.ds(span, 1)].reshape(1, 1, PART)
        scale = jnp.where(shown, moments[2 * core + 1, pl.ds(span, 1)].reshape(1, 1, PART), 0.0)
        offset = jnp.where(shown, half_bias.reshape(1, 1, PART), 0.0)
        value = (value.astype(jnp.float32) - centre) * scale + offset
        return value + value * jnp.tanh(value)

    for step in range(CHIPS):
        for other in range(2):
            span = lax.rem(chip - step + CHIPS, CHIPS) * 2 + lax.rem(core + other, 2)
            raw[pl.ds(span * FRAMES, FRAMES)] = signal[step, other]
            for row in range(ROWS):
                if row == 0:
                    value = jnp.where(tile == 0, signal[step, other, :, :, :PART], above[step, other])
                elif row == ROWS - 1:
                    value = jnp.where(
                        tile == tiles - 1, signal[step, other, :, :, PART:], below[step, other]
                    )
                else:
                    value = signal[step, other, :, :, (row - 1) * PART : row * PART]
                value = normed(value, span)
                left = jnp.concatenate([value[:, :1], value[:, :-1]], axis=1)
                right = jnp.concatenate([value[:, 1:], value[:, -1:]], axis=1)
                for side, part in enumerate((left, value, right)):
                    shifted[
                        side, pl.ds(2 + span * FRAMES, FRAMES), :, row * PART : (row + 1) * PART
                    ] = part.astype(jnp.bfloat16)
    for side in range(3):
        shifted[side, 0] = shifted[side, 2]
        shifted[side, 1] = shifted[side, 2]


def taps_kernel(shifted, raw, mine, theirs, factor, out, weights):
    core = lax.axis_index("core")
    count = mine.shape[0]
    for tap in range(count):
        weights[tap, pl.ds(pl.multiple_of(core * SHARE, SHARE), SHARE)] = mine[tap]
        weights[tap, pl.ds(pl.multiple_of((1 - core) * SHARE, SHARE), SHARE)] = theirs[tap]
    length = SPANS * FRAMES
    scale = jnp.where(core == 0, factor[0:1, :], factor[1:2, :])
    for row in range(2):
        total = None
        for pair in range(count // 2):
            blocks = []
            for tap in (2 * pair, 2 * pair + 1):
                if tap < count - 1:
                    at = (row + tap // 3 % 3) * PART
                    block = shifted[tap % 3, tap // 9 : tap // 9 + length, :, at : at + PART]
                else:
                    block = raw[..., row * PART : (row + 1) * PART]
                blocks.append(block.reshape(-1, PART))
            term = jnp.dot(
                jnp.concatenate(blocks, axis=1),
                weights[2 * pair : 2 * pair + 2].reshape(2 * PART, OUT),
                preferred_element_type=jnp.float32,
            )
            total = term if total is None else total + term
        total = (total * scale).reshape(SPANS, FRAMES, COLS, OUT)
        out[:, :, row * COLS : (row + 1) * COLS, :] = total


def per_device(features, lengths, gain_in, bias_in, conv_in, skip_weight):
    videos, frames, row_count, col_count, wide_in = features.shape
    span, chip = lax.axis_index(TM), lax.axis_index("x")
    tiles, chips = lax.axis_size(TILE), lax.axis_size("x")
    taps = conv_in.shape[1]
    on_chip = pl.BlockSpec(memory_space=pltpu.VMEM)
    outside = pl.BlockSpec(memory_space=pl.ANY)
    scalar = pl.BlockSpec(memory_space=pltpu.SMEM)
    params = pltpu.CompilerParams(vmem_limit_bytes=20 * 1024 * 1024)

    planes = features.reshape(videos * frames, row_count * col_count, wide_in)
    copies = pl.pallas_call(
        payload_kernel,
        out_shape=jax.ShapeDtypeStruct((tiles, 2, LINE * OUT), jnp.bfloat16),
        in_specs=[outside] * 4,
        out_specs=outside,
        scratch_shapes=[
            pltpu.VMEM(planes.shape, jnp.bfloat16),
            pltpu.VMEM((taps, SPANS, OUT), jnp.bfloat16),
            pltpu.VMEM((SPANS, OUT), jnp.bfloat16),
            pltpu.SMEM((videos,), jnp.int32),
            pltpu.VMEM((32, OUT), jnp.float32),
            pltpu.VMEM((2, LINE * OUT), jnp.float32),
            pltpu.VMEM((8, 2, LINE * OUT), jnp.bfloat16),
            pltpu.SemaphoreType.DMA((4,)),
            pltpu.SemaphoreType.DMA((tiles // 8,)),
        ],
        compiler_params=params,
        name="payload",
    )(
        *[
            pltpu.with_memory_space_constraint(value, pltpu.HBM)
            for value in (planes, conv_in.transpose(1, 0, 2), skip_weight, lengths)
        ]
    )
    arrived = lax.all_to_all(copies, TILE, 0, 0, tiled=True)

    shape = (chips, frames, col_count, 2 * PART)
    kept, sent, lanes = pl.pallas_call(
        member_kernel,
        out_shape=(
            jax.ShapeDtypeStruct(shape, jnp.bfloat16),
            jax.ShapeDtypeStruct(shape, jnp.bfloat16),
            jax.ShapeDtypeStruct((2, PART), jnp.float32),
        ),
        in_specs=[on_chip] * 3,
        out_specs=(on_chip, on_chip, on_chip),
        compiler_params=params,
        name="member_shares",
    )(planes, gain_in.reshape(1, -1), bias_in.reshape(1, -1))
    swap = [(0, 1), (1, 0)]
    shares = jnp.stack([kept, lax.ppermute(sent, "core", swap)], axis=1)
    signal = []
    for step in range(chips):
        block = lax.dynamic_index_in_dim(shares, lax.rem(chip + step, chips), 0, False)
        if step:
            block = lax.ppermute(block, "x", [(i, (i + step) % chips) for i in range(chips)])
        signal.append(block)
    signal = jnp.stack(signal)
    upper, lower = signal[..., PART:], signal[..., :PART]
    above = lax.ppermute(upper, TILE, [(i, i + 1) for i in range(tiles - 1)])
    below = lax.ppermute(lower, TILE, [(i + 1, i) for i in range(tiles - 1)])

    held, upper, lower = lax.optimization_barrier((arrived, upper, lower))
    copies = pl.pallas_call(
        functools.partial(sums_kernel, first=taps + 1),
        out_shape=jax.ShapeDtypeStruct((SPANS, 1, 128), jnp.float32),
        in_specs=[on_chip],
        out_specs=on_chip,
        compiler_params=params,
        name="sums",
    )(pltpu.with_memory_space_constraint(held, pltpu.VMEM))
    totals = lax.all_to_all(copies, TM, 0, 0, tiled=True).reshape(SPANS, -1)
    mine = arrived.reshape(tiles, 2 * LINE, OUT)[:, : taps + 1].transpose(1, 0, 2)
    theirs = lax.ppermute(mine, "core", swap)

    shifted, raw, factor = pl.pallas_call(
        functools.partial(
            norm_kernel,
            cells=float(row_count * tiles * col_count * (wide_in // GROUPS)),
            tiles=tiles,
            tap_bound=float(taps * PART) * 0.0546875,
            skip_bound=float(PART) * 0.25,
        ),
        out_shape=(
            jax.ShapeDtypeStruct((3, SPANS * frames + 2, col_count, ROWS * PART), jnp.bfloat16),
            jax.ShapeDtypeStruct((SPANS * frames, col_count, 2 * PART), jnp.bfloat16),
            jax.ShapeDtypeStruct((videos, OUT), jnp.float32),
        ),
        in_specs=[scalar] + [on_chip] * 5,
        out_specs=(on_chip, on_chip, on_chip),
        scratch_shapes=[pltpu.VMEM((2 * videos, SPANS, PART), jnp.float32)],
        compiler_params=params,
        cost_estimate=pl.CostEstimate(flops=1 << 34, bytes_accessed=1 << 26, transcendentals=1 << 24),
        name="norm",
    )(lengths, totals, lanes, signal, above, below)
    total = pl.pallas_call(
        taps_kernel,
        out_shape=jax.ShapeDtypeStruct((SPANS, frames, row_count * col_count, OUT), jnp.float32),
        in_specs=[on_chip] * 5,
        out_specs=on_chip,
        scratch_shapes=[pltpu.VMEM((taps + 1, PART, OUT), jnp.bfloat16)],
        compiler_params=params,
        cost_estimate=pl.CostEstimate(
            flops=2 * 28 * 1024 * 128 * 256, bytes_accessed=6 << 20, transcendentals=0
        ),
        name="taps",
    )(shifted, raw, mine, theirs, factor)

    total = total.astype(jnp.float16)
    total = lax.all_to_all(total, TM, 0, 0, tiled=True).astype(jnp.float32)
    total = jnp.sum(total.reshape((chips, videos) + total.shape[1:]), axis=0)
    total = total / factor[:, None, None, :]
    total = total.reshape(videos, frames, row_count, col_count, OUT)
    stamps = span * frames + jnp.arange(frames, dtype=jnp.int32)
    present = stamps[None, :] < lengths[:, None]
    return jnp.where(present[:, :, None, None, None], total, 0.0).astype(jnp.bfloat16)


def solution(mesh):
    spans, tiles = mesh.devices.shape
    fine = Mesh(mesh.devices.reshape(spans // 2, 2, 8, tiles // 8), TM + TILE)
    placed = (
        P(None, TM, TILE, None, None),
        P(),
        P(),
        P(),
        P(TILE, None, None),
        P(TILE, None),
    )
    return jax.shard_map(
        per_device,
        mesh=fine,
        in_specs=placed,
        out_specs=P(None, TM, TILE, None, None),
        check_vma=False,
    )
```

time: 79 us -> 78.1 us (0.989)
  waiting for transfers between devices: 18.8 us -> 16.2 us
  starting transfers between devices: 48.2 us -> 50.2 us
    ppermute x3, waiting for transfers between devices: 4.47 us -> 2.22 us  [per_device(): lax.ppermute(block, 'x', [(i, (i + step) % chips) for i in range(chips)])]
    ppermute x3, starting transfers between devices: 9.33 us -> 10.5 us  [per_device(): lax.ppermute(block, 'x', [(i, (i + step) % chips) for i in range(chips)])]
    all_to_all x1, starting transfers between devices: 3.47 us -> 4.32 us  [per_device(): total = lax.all_to_all(total, TM, 0, 0, tiled=True).astype(jnp.float32)]
  transfers between devices with their start and end apart: 10 -> 10, of which waited for: 6 -> 5; matrix products, arithmetic and copies ran while one was open for 2% -> 3% of each run, Pallas kernels for 3% -> 3%
where the time goes in v6:
time: 78.1 us; the launch traced here: 77.5 us
  starting transfers between devices  50.2 us (64%)
  waiting for transfers between devices  16.2 us (21%)
  Pallas kernels  7.03 us (9%)
  local copies, waits for them, and re-layouts  1.92 us (2%)
  other arithmetic  1.9 us (2%)
    all_to_all x1, starting transfers between devices, per_device(): arrived = lax.all_to_all(copies, TILE, 0, 0, tiled=True)  17.1 us
    ppermute x3, starting transfers between devices, per_device(): lax.ppermute(block, 'x', [(i, (i + step) % chips) for i in range(chips)])  10.5 us
    all_to_all x1, waiting for transfers between devices, per_device(): total = lax.all_to_all(total, TM, 0, 0, tiled=True).astype(jnp.float32)  9.4 us
    all_to_all x1, starting transfers between devices, per_device(): totals = lax.all_to_all(copies, TM, 0, 0, tiled=True).reshape(SPANS, -1)  8.15 us
    all_to_all x1, starting transfers between devices, per_device(): total = lax.all_to_all(total, TM, 0, 0, tiled=True).astype(jnp.float32)  4.32 us
    ppermute x1, starting transfers between devices, per_device(): above = lax.ppermute(upper, TILE, [(i, i + 1) for i in range(tiles - 1)])  3.99 us
    ppermute x1, starting transfers between devices, per_device(): shares = jnp.stack([kept, lax.ppermute(sent, 'core', swap)], axis=1)  2.86 us
    pallas_call x1, Pallas kernels, per_device(): pl.pallas_call(payload_kernel, out_shape=jax.ShapeDtypeStruct((tiles, 2,...  2.45 us
  transfers between devices with their start and end apart: 10, of which 5 were waited for; matrix products, arithmetic and copies ran while one was open for 3% of the time, Pallas kernels for 3%

profile of v6, /device:TPU:1, one launch (start us, length us, event | category | flops | bytes accessed | tf_op | source)
XLA Modules:
  0.0 77.5 jit_solution(11288420511683479591)
XLA Ops:
  0.0 2.5 %payload.1 = bf16[64,2,3840]{2,1,0:T(2,128)(2,1)} custom-call(bf16[8,32,512]{2,1,0:T(8,128)(2,1)} %bitcast.23, bf16[27,8,256]{2,1,0:T(8,128)(2,1)} %bitcast.35, bf16[8,256]{1,0:T(8,128)(2,1)} %skip.1, s32[2]{0:T(128)} %lengths.3), custom_call_target="tpu_custom_call" | custom-call | tf_op jit(solution)/shard_map/payload/pallas_call | solution.py:236
  2.5 17.1 %all-to-all-start = ((bf16[64,2,3840]{2,1,0:T(2,128)(2,1)}), bf16[64,2,3840]{2,1,0:T(2,128)(2,1)S(1)}, u32[]{:S(2)}, u32[]{:S(2)}) async-start(bf16[64,2,3840]{2,1,0:T(2,128)(2,1)} %payload.1), calls=%async_computation | async-start | bytes 1966080 | tf_op jit(solution)/shard_map/all_to_all | solution.py:260
  19.7 0.4 member_shares.1
  20.0 2.9 %collective-permute-start = (bf16[4,4,16,256]{3,2,1,0:T(8,128)(2,1)S(1)}, bf16[4,4,16,256]{3,2,1,0:T(8,128)(2,1)S(1)}, u32[]{:S(2)}, u32[]{:S(2)}) collective-permute-start(bf16[4,4,16,256]{3,2,1,0:T(8,128)(2,1)S(1)} %get-tuple-element.13), channel_id=1, source_target_pairs={{0,64},{64,0},{1,65},{65,1},{2,66},{66,2},{3,67},{67,3},{4,68},{68... | collective-permute-start | bytes 393224 | tf_op jit(solution)/shard_map/ppermute | solution.py:276
  22.9 0.9 %collective-permute-done = bf16[4,4,16,256]{3,2,1,0:T(8,128)(2,1)S(1)} collective-permute-done((bf16[4,4,16,256]{3,2,1,0:T(8,128)(2,1)S(1)}, bf16[4,4,16,256]{3,2,1,0:T(8,128)(2,1)S(1)}, u32[]{:S(2)}, u32[]{:S(2)}) %collective-permute-start) | collective-permute-done | bytes 131104 | tf_op jit(solution)/shard_map/ppermute | solution.py:276
  23.9 3.1 %collective-permute-start.1 = (bf16[2,4,16,256]{3,2,1,0:T(8,128)(2,1)S(1)}, bf16[2,4,16,256]{3,2,1,0:T(8,128)(2,1)S(1)}, u32[]{:S(2)}, u32[]{:S(2)}) collective-permute-start(bf16[2,4,16,256]{3,2,1,0:T(8,128)(2,1)S(1)} %get-tuple-element.22), channel_id=1, source_target_pairs={{0,128},{128,256},{256,384},{384,0},{1,129},{129,257},{257,385},{3... | collective-permute-start | bytes 196616 | tf_op jit(solution)/shard_map/ppermute | solution.py:281
  27.0 4.4 %collective-permute-start.2 = (bf16[2,4,16,256]{3,2,1,0:T(8,128)(2,1)S(1)}, bf16[2,4,16,256]{3,2,1,0:T(8,128)(2,1)S(1)}, u32[]{:S(2)}, u32[]{:S(2)}) collective-permute-start(bf16[2,4,16,256]{3,2,1,0:T(8,128)(2,1)S(1)} %get-tuple-element.23), channel_id=1, source_target_pairs={{0,256},{128,384},{256,0},{384,128},{1,257},{129,385},{257,1},{385... | collective-permute-start | bytes 196616 | tf_op jit(solution)/shard_map/ppermute | solution.py:281
  31.4 3.1 %collective-permute-start.3 = (bf16[2,4,16,256]{3,2,1,0:T(8,128)(2,1)S(1)}, bf16[2,4,16,256]{3,2,1,0:T(8,128)(2,1)S(1)}, u32[]{:S(2)}, u32[]{:S(2)}) collective-permute-start(bf16[2,4,16,256]{3,2,1,0:T(8,128)(2,1)S(1)} %get-tuple-element.24), channel_id=1, source_target_pairs={{0,384},{128,0},{256,128},{384,256},{1,385},{129,1},{257,129},{385... | collective-permute-start | bytes 196616 | tf_op jit(solution)/shard_map/ppermute | solution.py:281
  34.5 0.0 collective-permute-done.1
  34.5 0.0 collective-permute-done.2
  34.5 2.2 %collective-permute-done.3 = bf16[2,4,16,256]{3,2,1,0:T(8,128)(2,1)S(1)} collective-permute-done((bf16[2,4,16,256]{3,2,1,0:T(8,128)(2,1)S(1)}, bf16[2,4,16,256]{3,2,1,0:T(8,128)(2,1)S(1)}, u32[]{:S(2)}, u32[]{:S(2)}) %collective-permute-start.3) | collective-permute-done | bytes 65568 | tf_op jit(solution)/shard_map/ppermute | solution.py:281
  36.7 0.8 fusion.7
  37.5 1.3 %collective-permute-start.5 = (bf16[4,2,4,16,128]{4,3,2,1,0:T(8,128)(2,1)}, bf16[4,2,4,16,128]{4,3,2,1,0:T(8,128)(2,1)S(1)}, u32[]{:S(2)}, u32[]{:S(2)}) collective-permute-start(bf16[4,2,4,16,128]{4,3,2,1,0:T(8,128)(2,1)} %get-tuple-element.19), channel_id=1, source_target_pairs={{1,0},{2,1},{3,2},{4,3},{5,4},{6,5},{7,6},{8,7},{9,8},{10,9},{11,1... | collective-permute-start | bytes 393224 | tf_op jit(solution)/shard_map/ppermute | solution.py:286
  38.8 4.0 %collective-permute-start.4 = (bf16[4,2,4,16,128]{4,3,2,1,0:T(8,128)(2,1)}, bf16[4,2,4,16,128]{4,3,2,1,0:T(8,128)(2,1)S(1)}, u32[]{:S(2)}, u32[]{:S(2)}) collective-permute-start(bf16[4,2,4,16,128]{4,3,2,1,0:T(8,128)(2,1)} %get-tuple-element.20), channel_id=1, source_target_pairs={{0,1},{1,2},{2,3},{3,4},{4,5},{5,6},{6,7},{7,8},{8,9},{9,10},{10,1... | collective-permute-start | bytes 393224 | tf_op jit(solution)/shard_map/ppermute | solution.py:285
  42.8 2.2 %all-to-all-done.arrived = bf16[64,2,3840]{2,1,0:T(2,128)(2,1)S(1)} async-done(((bf16[64,2,3840]{2,1,0:T(2,128)(2,1)}), bf16[64,2,3840]{2,1,0:T(2,128)(2,1)S(1)}, u32[]{:S(2)}, u32[]{:S(2)}) %all-to-all-start) | async-done | bytes 983072 | tf_op jit(solution)/shard_map/all_to_all | solution.py:260
  45.0 0.7 sums.1
  45.7 8.1 %all-to-all-start.1 = ((f32[8,1,128]{2,1,0:T(1,128)}), f32[8,1,128]{2,1,0:T(1,128)S(1)}, u32[]{:S(2)}, u32[]{:S(2)}) async-start(f32[8,1,128]{2,1,0:T(1,128)} %sums.1), calls=%async_computation.1 | async-start | bytes 8192 | tf_op jit(solution)/shard_map/all_to_all | solution.py:297
  53.8 0.6 reshape.60
  54.4 0.5 copy.13
  55.0 1.9 %collective-permute-start.6 = (bf16[28,64,256]{2,1,0:T(8,128)(2,1)S(1)}, bf16[28,64,256]{2,1,0:T(8,128)(2,1)S(1)}, u32[]{:S(2)}, u32[]{:S(2)}) collective-permute-start(bf16[28,64,256]{2,1,0:T(8,128)(2,1)S(1)} %bitcast.25), channel_id=1, source_target_pairs={{0,64},{64,0},{1,65},{65,1},{2,66},{66,2},{3,67},{67,3},{4,68},{68... | collective-permute-start | bytes 2752520 | tf_op jit(solution)/shard_map/ppermute | solution.py:299
  56.9 0.0 collective-permute-done.5.below
  56.9 0.0 collective-permute-done.4.above
  56.9 1.5 %all-to-all-done.1 = f32[8,1,128]{2,1,0:T(1,128)S(1)} async-done(((f32[8,1,128]{2,1,0:T(1,128)}), f32[8,1,128]{2,1,0:T(1,128)S(1)}, u32[]{:S(2)}, u32[]{:S(2)}) %all-to-all-start.1) | async-done | bytes 4128 | tf_op jit(solution)/shard_map/all_to_all | solution.py:297
  58.4 1.4 %norm.1 = (bf16[3,34,16,512]{3,2,1,0:T(8,128)(2,1)S(1)}, bf16[32,16,256]{2,1,0:T(8,128)(2,1)S(1)}, f32[2,256]{1,0:T(2,128)S(1)}) custom-call(s32[2]{0:T(128)S(1)} %copy-done.3, f32[8,128]{1,0:T(8,128)S(1)} %bitcast.28, f32[2,128]{1,0:T(2,128)S(1)} %get-tuple-element.15.lanes, bf16[4,2,4,16,256]{4,3,2,1,0:T(8,128)(2,1)S(1)} %pad_maximum_fusion.signal, ...), custom_call_target="tpu_custom_call" | custom-call | flops 17179869184 | bytes 67108864 | tf_op jit(solution)/shard_map/norm/pallas_call | solution.py:301
  59.8 0.0 collective-permute-done.6.theirs
  59.8 2.1 %taps.1 = f32[8,4,32,256]{3,2,1,0:T(8,128)S(1)} custom-call(bf16[3,34,16,512]{3,2,1,0:T(8,128)(2,1)S(1)} %get-tuple-element.16.shifted, bf16[32,16,256]{2,1,0:T(8,128)(2,1)S(1)} %get-tuple-element.17.raw, bf16[28,64,256]{2,1,0:T(8,128)(2,1)S(1)} %bitcast.26, bf16[28,64,256]{2,1,0:T(8,128)(2,1)S(1)} %collective-permute-done.6.theirs, ...), custom_call_target="tpu_custom_call" | custom-call | flops 1879048192 | bytes 6291456 | tf_op jit(solution)/shard_map/taps/pallas_call | solution.py:321
  61.9 0.9 %convert_element_type.7 = f16[8,4,32,256]{3,2,1,0:T(8,128)(2,1)} convert(f32[8,4,32,256]{3,2,1,0:T(8,128)S(1)} %taps.1) | non-fusion elementwise | flops 262144 | bytes 1572864 | tf_op jit(solution)/shard_map/convert_element_type | solution.py:334
  62.8 4.3 %all-to-all-start.2 = ((f16[8,4,32,256]{3,2,1,0:T(8,128)(2,1)}), f16[8,4,32,256]{3,2,1,0:T(8,128)(2,1)S(1)}, u32[]{:S(2)}, u32[]{:S(2)}) async-start(f16[8,4,32,256]{3,2,1,0:T(8,128)(2,1)} %convert_element_type.7), calls=%async_computation.2 | async-start | bytes 1048576 | tf_op jit(solution)/shard_map/all_to_all | solution.py:335
  67.2 0.1 broadcast_compare_fusion
  67.2 9.4 %all-to-all-done.2 = f16[8,4,32,256]{3,2,1,0:T(8,128)(2,1)S(1)} async-done(((f16[8,4,32,256]{3,2,1,0:T(8,128)(2,1)}), f16[8,4,32,256]{3,2,1,0:T(8,128)(2,1)S(1)}, u32[]{:S(2)}, u32[]{:S(2)}) %all-to-all-start.2) | async-done | bytes 524320 | tf_op jit(solution)/shard_map/all_to_all | solution.py:335
  76.6 0.1 convert_reduce_fusion
  76.7 0.7 select_convert_fusion
  (11 shorter events, 0.1 us)
Async XLA Ops:
  0.0 19.6 %copy-start = (bf16[2,4,2,16,512]{4,3,2,1,0:T(8,128)(2,1)S(1)}, bf16[2,4,2,16,512]{4,3,2,1,0:T(8,128)(2,1)}, u32[]{:S(2)}) copy-start(bf16[2,4,2,16,512]{4,3,2,1,0:T(8,128)(2,1)} %param.6) | copy-start | bytes 786436
  0.0 19.6 %copy-start.2 = (f32[512]{0:T(512)S(1)}, f32[512]{0:T(512)}, u32[]{:S(2)}) copy-start(f32[512]{0:T(512)} %param.9) | copy-start | bytes 6148
  0.0 19.6 %copy-start.1 = (f32[512]{0:T(512)S(1)}, f32[512]{0:T(512)}, u32[]{:S(2)}) copy-start(f32[512]{0:T(512)} %param.8) | copy-start | bytes 6148
  2.5 42.5 %all-to-all-start = ((bf16[64,2,3840]{2,1,0:T(2,128)(2,1)}), bf16[64,2,3840]{2,1,0:T(2,128)(2,1)S(1)}, u32[]{:S(2)}, u32[]{:S(2)}) async-start(bf16[64,2,3840]{2,1,0:T(2,128)(2,1)} %payload.1), calls=%async_computation | async-start | bytes 1966080 | tf_op jit(solution)/shard_map/all_to_all | solution.py:260
  20.0 3.8 %collective-permute-start = (bf16[4,4,16,256]{3,2,1,0:T(8,128)(2,1)S(1)}, bf16[4,4,16,256]{3,2,1,0:T(8,128)(2,1)S(1)}, u32[]{:S(2)}, u32[]{:S(2)}) collective-permute-start(bf16[4,4,16,256]{3,2,1,0:T(8,128)(2,1)S(1)} %get-tuple-element.13), channel_id=1, source_target_pairs={{0,64},{64,0},{1,65},{65,1},{2,66},{66,2},{3,67},{67,3},{4,68},{68... | collective-permute-start | bytes 393224 | tf_op jit(solution)/shard_map/ppermute | solution.py:276
  23.9 10.6 %collective-permute-start.1 = (bf16[2,4,16,256]{3,2,1,0:T(8,128)(2,1)S(1)}, bf16[2,4,16,256]{3,2,1,0:T(8,128)(2,1)S(1)}, u32[]{:S(2)}, u32[]{:S(2)}) collective-permute-start(bf16[2,4,16,256]{3,2,1,0:T(8,128)(2,1)S(1)} %get-tuple-element.22), channel_id=1, source_target_pairs={{0,128},{128,256},{256,384},{384,0},{1,129},{129,257},{257,385},{3... | collective-permute-start | bytes 196616 | tf_op jit(solution)/shard_map/ppermute | solution.py:281
  27.0 7.4 %collective-permute-start.2 = (bf16[2,4,16,256]{3,2,1,0:T(8,128)(2,1)S(1)}, bf16[2,4,16,256]{3,2,1,0:T(8,128)(2,1)S(1)}, u32[]{:S(2)}, u32[]{:S(2)}) collective-permute-start(bf16[2,4,16,256]{3,2,1,0:T(8,128)(2,1)S(1)} %get-tuple-element.23), channel_id=1, source_target_pairs={{0,256},{128,384},{256,0},{384,128},{1,257},{129,385},{257,1},{385... | collective-permute-start | bytes 196616 | tf_op jit(solution)/shard_map/ppermute | solution.py:281
  31.4 5.3 %collective-permute-start.3 = (bf16[2,4,16,256]{3,2,1,0:T(8,128)(2,1)S(1)}, bf16[2,4,16,256]{3,2,1,0:T(8,128)(2,1)S(1)}, u32[]{:S(2)}, u32[]{:S(2)}) collective-permute-start(bf16[2,4,16,256]{3,2,1,0:T(8,128)(2,1)S(1)} %get-tuple-element.24), channel_id=1, source_target_pairs={{0,384},{128,0},{256,128},{384,256},{1,385},{129,1},{257,129},{385... | collective-permute-start | bytes 196616 | tf_op jit(solution)/shard_map/ppermute | solution.py:281
  37.5 19.4 %collective-permute-start.5 = (bf16[4,2,4,16,128]{4,3,2,1,0:T(8,128)(2,1)}, bf16[4,2,4,16,128]{4,3,2,1,0:T(8,128)(2,1)S(1)}, u32[]{:S(2)}, u32[]{:S(2)}) collective-permute-start(bf16[4,2,4,16,128]{4,3,2,1,0:T(8,128)(2,1)} %get-tuple-element.19), channel_id=1, source_target_pairs={{1,0},{2,1},{3,2},{4,3},{5,4},{6,5},{7,6},{8,7},{9,8},{10,9},{11,1... | collective-permute-start | bytes 393224 | tf_op jit(solution)/shard_map/ppermute | solution.py:286
  38.8 18.1 %collective-permute-start.4 = (bf16[4,2,4,16,128]{4,3,2,1,0:T(8,128)(2,1)}, bf16[4,2,4,16,128]{4,3,2,1,0:T(8,128)(2,1)S(1)}, u32[]{:S(2)}, u32[]{:S(2)}) collective-permute-start(bf16[4,2,4,16,128]{4,3,2,1,0:T(8,128)(2,1)} %get-tuple-element.20), channel_id=1, source_target_pairs={{0,1},{1,2},{2,3},{3,4},{4,5},{5,6},{6,7},{7,8},{8,9},{9,10},{10,1... | collective-permute-start | bytes 393224 | tf_op jit(solution)/shard_map/ppermute | solution.py:285
  45.7 12.7 %all-to-all-start.1 = ((f32[8,1,128]{2,1,0:T(1,128)}), f32[8,1,128]{2,1,0:T(1,128)S(1)}, u32[]{:S(2)}, u32[]{:S(2)}) async-start(f32[8,1,128]{2,1,0:T(1,128)} %sums.1), calls=%async_computation.1 | async-start | bytes 8192 | tf_op jit(solution)/shard_map/all_to_all | solution.py:297
  53.8 4.6 %copy-start.3 = (s32[2]{0:T(128)S(1)}, s32[2]{0:T(128)}, u32[]{:S(2)}) copy-start(s32[2]{0:T(128)} %lengths.3) | copy-start | bytes 28
  55.0 4.8 %collective-permute-start.6 = (bf16[28,64,256]{2,1,0:T(8,128)(2,1)S(1)}, bf16[28,64,256]{2,1,0:T(8,128)(2,1)S(1)}, u32[]{:S(2)}, u32[]{:S(2)}) collective-permute-start(bf16[28,64,256]{2,1,0:T(8,128)(2,1)S(1)} %bitcast.25), channel_id=1, source_target_pairs={{0,64},{64,0},{1,65},{65,1},{2,66},{66,2},{3,67},{67,3},{4,68},{68... | collective-permute-start | bytes 2752520 | tf_op jit(solution)/shard_map/ppermute | solution.py:299
  62.8 13.8 %all-to-all-start.2 = ((f16[8,4,32,256]{3,2,1,0:T(8,128)(2,1)}), f16[8,4,32,256]{3,2,1,0:T(8,128)(2,1)S(1)}, u32[]{:S(2)}, u32[]{:S(2)}) async-start(f16[8,4,32,256]{3,2,1,0:T(8,128)(2,1)} %convert_element_type.7), calls=%async_computation.2 | async-start | bytes 1048576 | tf_op jit(solution)/shard_map/all_to_all | solution.py:335

commit v7 on v6

--- a/solution.py
+++ b/solution.py
@@ -130,6 +130,15 @@
     lanes[...] = exact_dot(pair, jnp.where(match, 1.0, 0.0).astype(jnp.bfloat16))
 
 
+def edges_kernel(*refs):
+    signal, upper, lower = refs[-3:]
+    for step, block in enumerate(refs[:-3]):
+        value = block[...]
+        signal[step] = value
+        upper[step] = value[..., PART:]
+        lower[step] = value[..., :PART]
+
+
 def norm_kernel(
     lengths, totals, lanes, signal, above, below, shifted, raw, factor, moments,
     *, cells, tiles, tap_bound, skip_bound
@@ -195,10 +204,12 @@
 
 def taps_kernel(shifted, raw, mine, theirs, factor, out, weights):
     core = lax.axis_index("core")
-    count = mine.shape[0]
+    count = weights.shape[0]
     for tap in range(count):
-        weights[tap, pl.ds(pl.multiple_of(core * SHARE, SHARE), SHARE)] = mine[tap]
-        weights[tap, pl.ds(pl.multiple_of((1 - core) * SHARE, SHARE), SHARE)] = theirs[tap]
+        line, at = tap // LINE, tap % LINE * OUT
+        for place, half in ((core, mine), (1 - core, theirs)):
+            rows = pl.ds(pl.multiple_of(place * SHARE, SHARE), SHARE)
+            weights[tap, rows] = half[line, :, at : at + OUT]
     length = SPANS * FRAMES
     scale = jnp.where(core == 0, factor[0:1, :], factor[1:2, :])
     for row in range(2):
@@ -280,8 +291,16 @@
         if step:
             block = lax.ppermute(block, "x", [(i, (i + step) % chips) for i in range(chips)])
         signal.append(block)
-    signal = jnp.stack(signal)
-    upper, lower = signal[..., PART:], signal[..., :PART]
+    whole = (chips,) + signal[0].shape
+    edge = whole[:-1] + (PART,)
+    signal, upper, lower = pl.pallas_call(
+        edges_kernel,
+        out_shape=tuple(pltpu.VMEM(shape, jnp.bfloat16) for shape in (whole, edge, edge)),
+        in_specs=[on_chip] * chips,
+        out_specs=(on_chip, on_chip, on_chip),
+        compiler_params=params,
+        name="edges",
+    )(*signal)
     above = lax.ppermute(upper, TILE, [(i, i + 1) for i in range(tiles - 1)])
     below = lax.ppermute(lower, TILE, [(i + 1, i) for i in range(tiles - 1)])
 
@@ -295,7 +314,7 @@
         name="sums",
     )(pltpu.with_memory_space_constraint(held, pltpu.VMEM))
     totals = lax.all_to_all(copies, TM, 0, 0, tiled=True).reshape(SPANS, -1)
-    mine = arrived.reshape(tiles, 2 * LINE, OUT)[:, : taps + 1].transpose(1, 0, 2)
+    mine = arrived.transpose(1, 0, 2)
     theirs = lax.ppermute(mine, "core", swap)
 
     shifted, raw, factor = pl.pallas_call(

time: 78.1 us -> 77.8 us (level)
  waiting for transfers between devices: 16.2 us -> 18.7 us
  local copies, waits for them, and re-layouts: 1.92 us -> 0.12 us
  starting transfers between devices: 50.2 us -> 48.5 us
    all_to_all x1, waiting for transfers between devices: 1.47 us -> 2.52 us  [per_device(): totals = lax.all_to_all(copies, TM, 0, 0, tiled=True).reshape(SPANS, -1)]
    ppermute x3, waiting for transfers between devices: 2.22 us -> 3.16 us  [per_device(): lax.ppermute(block, 'x', [(i, (i + step) % chips) for i in range(chips)])]
    ppermute x1, starting transfers between devices: 3.99 us -> 3.19 us  [per_device(): above = lax.ppermute(upper, TILE, [(i, i + 1) for i in range(tiles - 1)])]
  transfers between devices with their start and end apart: 10 -> 10, of which waited for: 5 -> 6; matrix products, arithmetic and copies ran while one was open for 3% -> 0% of each run, Pallas kernels for 3% -> 4%
where the time goes in v7:
time: 77.8 us; the launch traced here: 77.2 us
  starting transfers between devices  48.5 us (62%)
  waiting for transfers between devices  18.7 us (24%)
  Pallas kernels  7.79 us (10%)
  other arithmetic  1.87 us (2%)
    all_to_all x1, starting transfers between devices, per_device(): arrived = lax.all_to_all(copies, TILE, 0, 0, tiled=True)  17.1 us
    ppermute x3, starting transfers between devices, per_device(): lax.ppermute(block, 'x', [(i, (i + step) % chips) for i in range(chips)])  9.94 us
    all_to_all x1, waiting for transfers between devices, per_device(): total = lax.all_to_all(total, TM, 0, 0, tiled=True).astype(jnp.float32)  9.42 us
    all_to_all x1, starting transfers between devices, per_device(): totals = lax.all_to_all(copies, TM, 0, 0, tiled=True).reshape(SPANS, -1)  8.11 us
    all_to_all x1, starting transfers between devices, per_device(): total = lax.all_to_all(total, TM, 0, 0, tiled=True).astype(jnp.float32)  4.07 us
    ppermute x1, starting transfers between devices, per_device(): above = lax.ppermute(upper, TILE, [(i, i + 1) for i in range(tiles - 1)])  3.19 us
    ppermute x3, waiting for transfers between devices, per_device(): lax.ppermute(block, 'x', [(i, (i + step) % chips) for i in range(chips)])  3.16 us
    ppermute x1, starting transfers between devices, per_device(): shares = jnp.stack([kept, lax.ppermute(sent, 'core', swap)], axis=1)  2.86 us
  transfers between devices with their start and end apart: 10, of which 6 were waited for; matrix products, arithmetic and copies ran while one was open for 0% of the time, Pallas kernels for 4%

profile of v7, /device:TPU:1, one launch (start us, length us, event | category | flops | bytes accessed | tf_op | source)
XLA Modules:
  0.0 77.2 jit_solution(9069358107488770193)
XLA Ops:
  0.0 2.5 %payload.1 = bf16[64,2,3840]{2,1,0:T(2,128)(2,1)} custom-call(bf16[8,32,512]{2,1,0:T(8,128)(2,1)} %bitcast.21, bf16[27,8,256]{2,1,0:T(8,128)(2,1)} %bitcast.32, bf16[8,256]{1,0:T(8,128)(2,1)} %skip.1, s32[2]{0:T(128)} %lengths.3), custom_call_target="tpu_custom_call" | custom-call | tf_op jit(solution)/shard_map/payload/pallas_call | solution.py:247
  2.5 17.1 %all-to-all-start = ((bf16[64,2,3840]{2,1,0:T(2,128)(2,1)}), bf16[64,2,3840]{2,1,0:T(2,128)(2,1)S(1)}, u32[]{:S(2)}, u32[]{:S(2)}) async-start(bf16[64,2,3840]{2,1,0:T(2,128)(2,1)} %payload.1), calls=%async_computation | async-start | bytes 1966080 | tf_op jit(solution)/shard_map/all_to_all | solution.py:271
  19.7 0.4 member_shares.1
  20.0 2.9 %collective-permute-start = (bf16[4,4,16,256]{3,2,1,0:T(8,128)(2,1)S(1)}, bf16[4,4,16,256]{3,2,1,0:T(8,128)(2,1)S(1)}, u32[]{:S(2)}, u32[]{:S(2)}) collective-permute-start(bf16[4,4,16,256]{3,2,1,0:T(8,128)(2,1)S(1)} %get-tuple-element.16), channel_id=1, source_target_pairs={{0,64},{64,0},{1,65},{65,1},{2,66},{66,2},{3,67},{67,3},{4,68},{68... | collective-permute-start | bytes 393224 | tf_op jit(solution)/shard_map/ppermute | solution.py:287
  22.9 0.9 %collective-permute-done = bf16[4,4,16,256]{3,2,1,0:T(8,128)(2,1)S(1)} collective-permute-done((bf16[4,4,16,256]{3,2,1,0:T(8,128)(2,1)S(1)}, bf16[4,4,16,256]{3,2,1,0:T(8,128)(2,1)S(1)}, u32[]{:S(2)}, u32[]{:S(2)}) %collective-permute-start) | collective-permute-done | bytes 131104 | tf_op jit(solution)/shard_map/ppermute | solution.py:287
  23.9 0.0 copy-start.3
  23.9 4.4 %collective-permute-start.3 = (bf16[2,4,16,256]{3,2,1,0:T(8,128)(2,1)S(1)}, bf16[2,4,16,256]{3,2,1,0:T(8,128)(2,1)S(1)}, u32[]{:S(2)}, u32[]{:S(2)}) collective-permute-start(bf16[2,4,16,256]{3,2,1,0:T(8,128)(2,1)S(1)} %get-tuple-element.25), channel_id=1, source_target_pairs={{0,384},{128,0},{256,128},{384,256},{1,385},{129,1},{257,129},{385... | collective-permute-start | bytes 196616 | tf_op jit(solution)/shard_map/ppermute | solution.py:292
  28.3 1.9 %collective-permute-start.1 = (bf16[2,4,16,256]{3,2,1,0:T(8,128)(2,1)S(1)}, bf16[2,4,16,256]{3,2,1,0:T(8,128)(2,1)S(1)}, u32[]{:S(2)}, u32[]{:S(2)}) collective-permute-start(bf16[2,4,16,256]{3,2,1,0:T(8,128)(2,1)S(1)} %get-tuple-element.27), channel_id=1, source_target_pairs={{0,128},{128,256},{256,384},{384,0},{1,129},{129,257},{257,385},{3... | collective-permute-start | bytes 196616 | tf_op jit(solution)/shard_map/ppermute | solution.py:292
  30.2 3.6 %collective-permute-start.2 = (bf16[2,4,16,256]{3,2,1,0:T(8,128)(2,1)S(1)}, bf16[2,4,16,256]{3,2,1,0:T(8,128)(2,1)S(1)}, u32[]{:S(2)}, u32[]{:S(2)}) collective-permute-start(bf16[2,4,16,256]{3,2,1,0:T(8,128)(2,1)S(1)} %get-tuple-element.28), channel_id=1, source_target_pairs={{0,256},{128,384},{256,0},{384,128},{1,257},{129,385},{257,1},{385... | collective-permute-start | bytes 196616 | tf_op jit(solution)/shard_map/ppermute | solution.py:292
  33.9 0.0 collective-permute-done.3.refs_3_
  33.9 0.9 %collective-permute-done.1.refs_1_ = bf16[2,4,16,256]{3,2,1,0:T(8,128)(2,1)S(1)} collective-permute-done((bf16[2,4,16,256]{3,2,1,0:T(8,128)(2,1)S(1)}, bf16[2,4,16,256]{3,2,1,0:T(8,128)(2,1)S(1)}, u32[]{:S(2)}, u32[]{:S(2)}) %collective-permute-start.1) | collective-permute-done | bytes 65568 | tf_op jit(solution)/shard_map/ppermute | solution.py:292
  34.8 2.2 %collective-permute-done.2.refs_2_ = bf16[2,4,16,256]{3,2,1,0:T(8,128)(2,1)S(1)} collective-permute-done((bf16[2,4,16,256]{3,2,1,0:T(8,128)(2,1)S(1)}, bf16[2,4,16,256]{3,2,1,0:T(8,128)(2,1)S(1)}, u32[]{:S(2)}, u32[]{:S(2)}) %collective-permute-start.2) | collective-permute-done | bytes 65568 | tf_op jit(solution)/shard_map/ppermute | solution.py:292
  37.1 0.8 edges.1
  37.8 3.2 %collective-permute-start.4 = (bf16[4,2,4,16,128]{4,3,2,1,0:T(8,128)(2,1)}, bf16[4,2,4,16,128]{4,3,2,1,0:T(8,128)(2,1)S(1)}, u32[]{:S(2)}, u32[]{:S(2)}) collective-permute-start(bf16[4,2,4,16,128]{4,3,2,1,0:T(8,128)(2,1)} %get-tuple-element.17), channel_id=1, source_target_pairs={{0,1},{1,2},{2,3},{3,4},{4,5},{5,6},{6,7},{7,8},{8,9},{9,10},{10,1... | collective-permute-start | bytes 393224 | tf_op jit(solution)/shard_map/ppermute | solution.py:304
  41.0 1.3 %collective-permute-start.5 = (bf16[4,2,4,16,128]{4,3,2,1,0:T(8,128)(2,1)}, bf16[4,2,4,16,128]{4,3,2,1,0:T(8,128)(2,1)S(1)}, u32[]{:S(2)}, u32[]{:S(2)}) collective-permute-start(bf16[4,2,4,16,128]{4,3,2,1,0:T(8,128)(2,1)} %get-tuple-element.18), channel_id=1, source_target_pairs={{1,0},{2,1},{3,2},{4,3},{5,4},{6,5},{7,6},{8,7},{9,8},{10,9},{11,1... | collective-permute-start | bytes 393224 | tf_op jit(solution)/shard_map/ppermute | solution.py:305
  42.3 2.7 %all-to-all-done.arrived = bf16[64,2,3840]{2,1,0:T(2,128)(2,1)S(1)} async-done(((bf16[64,2,3840]{2,1,0:T(2,128)(2,1)}), bf16[64,2,3840]{2,1,0:T(2,128)(2,1)S(1)}, u32[]{:S(2)}, u32[]{:S(2)}) %all-to-all-start) | async-done | bytes 983072 | tf_op jit(solution)/shard_map/all_to_all | solution.py:271
  45.0 0.7 sums.1
  45.7 8.1 %all-to-all-start.1 = ((f32[8,1,128]{2,1,0:T(1,128)}), f32[8,1,128]{2,1,0:T(1,128)S(1)}, u32[]{:S(2)}, u32[]{:S(2)}) async-start(f32[8,1,128]{2,1,0:T(1,128)} %sums.1), calls=%async_computation.1 | async-start | bytes 8192 | tf_op jit(solution)/shard_map/all_to_all | solution.py:316
  53.8 0.1 copy.12
  53.9 1.9 %collective-permute-start.6 = (bf16[2,64,3840]{2,1,0:T(8,128)(2,1)S(1)}, bf16[2,64,3840]{2,1,0:T(8,128)(2,1)S(1)}, u32[]{:S(2)}, u32[]{:S(2)}) collective-permute-start(bf16[2,64,3840]{2,1,0:T(8,128)(2,1)S(1)} %bitcast.23), channel_id=1, source_target_pairs={{0,64},{64,0},{1,65},{65,1},{2,66},{66,2},{3,67},{67,3},{4,68},{68... | collective-permute-start | bytes 2949128 | tf_op jit(solution)/shard_map/ppermute | solution.py:318
  55.8 0.0 collective-permute-done.4.above
  55.8 0.0 collective-permute-done.5.below
  55.8 2.5 %all-to-all-done.1 = f32[8,1,128]{2,1,0:T(1,128)S(1)} async-done(((f32[8,1,128]{2,1,0:T(1,128)}), f32[8,1,128]{2,1,0:T(1,128)S(1)}, u32[]{:S(2)}, u32[]{:S(2)}) %all-to-all-start.1) | async-done | bytes 4128 | tf_op jit(solution)/shard_map/all_to_all | solution.py:316
  58.3 1.4 %norm.1 = (bf16[3,34,16,512]{3,2,1,0:T(8,128)(2,1)S(1)}, bf16[32,16,256]{2,1,0:T(8,128)(2,1)S(1)}, f32[2,256]{1,0:T(2,128)S(1)}) custom-call(s32[2]{0:T(128)S(1)} %copy-done.3, f32[8,128]{1,0:T(8,128)S(1)} %bitcast.26, f32[2,128]{1,0:T(2,128)S(1)} %get-tuple-element.20.lanes, bf16[4,2,4,16,256]{4,3,2,1,0:T(8,128)(2,1)S(1)} %get-tuple-element.21.signal, ...), custom_call_target="tpu_custom_call" | custom-call | flops 17179869184 | bytes 67108864 | tf_op jit(solution)/shard_map/norm/pallas_call | solution.py:320
  59.7 0.0 collective-permute-done.6.theirs
  59.8 2.1 %taps.1 = f32[8,4,32,256]{3,2,1,0:T(8,128)S(1)} custom-call(bf16[3,34,16,512]{3,2,1,0:T(8,128)(2,1)S(1)} %get-tuple-element.22.shifted, bf16[32,16,256]{2,1,0:T(8,128)(2,1)S(1)} %get-tuple-element.23.raw, bf16[2,64,3840]{2,1,0:T(8,128)(2,1)S(1)} %bitcast.24, bf16[2,64,3840]{2,1,0:T(8,128)(2,1)S(1)} %collective-permute-done.6.theirs, ...), custom_call_target="tpu_custom_call" | custom-call | flops 1879048192 | bytes 6291456 | tf_op jit(solution)/shard_map/taps/pallas_call | solution.py:340
  61.9 0.9 %convert_element_type.7 = f16[8,4,32,256]{3,2,1,0:T(8,128)(2,1)} convert(f32[8,4,32,256]{3,2,1,0:T(8,128)S(1)} %taps.1) | non-fusion elementwise | flops 262144 | bytes 1572864 | tf_op jit(solution)/shard_map/convert_element_type | solution.py:353
  62.8 4.1 %all-to-all-start.2 = ((f16[8,4,32,256]{3,2,1,0:T(8,128)(2,1)}), f16[8,4,32,256]{3,2,1,0:T(8,128)(2,1)S(1)}, u32[]{:S(2)}, u32[]{:S(2)}) async-start(f16[8,4,32,256]{3,2,1,0:T(8,128)(2,1)} %convert_element_type.7), calls=%async_computation.2 | async-start | bytes 1048576 | tf_op jit(solution)/shard_map/all_to_all | solution.py:354
  66.9 0.1 broadcast_compare_fusion
  66.9 9.4 %all-to-all-done.2 = f16[8,4,32,256]{3,2,1,0:T(8,128)(2,1)S(1)} async-done(((f16[8,4,32,256]{3,2,1,0:T(8,128)(2,1)}), f16[8,4,32,256]{3,2,1,0:T(8,128)(2,1)S(1)}, u32[]{:S(2)}, u32[]{:S(2)}) %all-to-all-start.2) | async-done | bytes 524320 | tf_op jit(solution)/shard_map/all_to_all | solution.py:354
  76.4 0.1 convert_reduce_fusion
  76.5 0.7 select_convert_fusion
  (9 shorter events, 0.0 us)
Async XLA Ops:
  0.0 19.6 %copy-start = (bf16[2,4,2,16,512]{4,3,2,1,0:T(8,128)(2,1)S(1)}, bf16[2,4,2,16,512]{4,3,2,1,0:T(8,128)(2,1)}, u32[]{:S(2)}) copy-start(bf16[2,4,2,16,512]{4,3,2,1,0:T(8,128)(2,1)} %param.6) | copy-start | bytes 786436
  0.0 19.6 %copy-start.2 = (f32[512]{0:T(512)S(1)}, f32[512]{0:T(512)}, u32[]{:S(2)}) copy-start(f32[512]{0:T(512)} %param.9) | copy-start | bytes 6148
  0.0 19.6 %copy-start.1 = (f32[512]{0:T(512)S(1)}, f32[512]{0:T(512)}, u32[]{:S(2)}) copy-start(f32[512]{0:T(512)} %param.8) | copy-start | bytes 6148
  2.5 42.5 %all-to-all-start = ((bf16[64,2,3840]{2,1,0:T(2,128)(2,1)}), bf16[64,2,3840]{2,1,0:T(2,128)(2,1)S(1)}, u32[]{:S(2)}, u32[]{:S(2)}) async-start(bf16[64,2,3840]{2,1,0:T(2,128)(2,1)} %payload.1), calls=%async_computation | async-start | bytes 1966080 | tf_op jit(solution)/shard_map/all_to_all | solution.py:271
  20.0 3.8 %collective-permute-start = (bf16[4,4,16,256]{3,2,1,0:T(8,128)(2,1)S(1)}, bf16[4,4,16,256]{3,2,1,0:T(8,128)(2,1)S(1)}, u32[]{:S(2)}, u32[]{:S(2)}) collective-permute-start(bf16[4,4,16,256]{3,2,1,0:T(8,128)(2,1)S(1)} %get-tuple-element.16), channel_id=1, source_target_pairs={{0,64},{64,0},{1,65},{65,1},{2,66},{66,2},{3,67},{67,3},{4,68},{68... | collective-permute-start | bytes 393224 | tf_op jit(solution)/shard_map/ppermute | solution.py:287
  23.9 34.4 %copy-start.3 = (s32[2]{0:T(128)S(1)}, s32[2]{0:T(128)}, u32[]{:S(2)}) copy-start(s32[2]{0:T(128)} %lengths.3) | copy-start | bytes 28
  23.9 10.0 %collective-permute-start.3 = (bf16[2,4,16,256]{3,2,1,0:T(8,128)(2,1)S(1)}, bf16[2,4,16,256]{3,2,1,0:T(8,128)(2,1)S(1)}, u32[]{:S(2)}, u32[]{:S(2)}) collective-permute-start(bf16[2,4,16,256]{3,2,1,0:T(8,128)(2,1)S(1)} %get-tuple-element.25), channel_id=1, source_target_pairs={{0,384},{128,0},{256,128},{384,256},{1,385},{129,1},{257,129},{385... | collective-permute-start | bytes 196616 | tf_op jit(solution)/shard_map/ppermute | solution.py:292
  28.3 6.5 %collective-permute-start.1 = (bf16[2,4,16,256]{3,2,1,0:T(8,128)(2,1)S(1)}, bf16[2,4,16,256]{3,2,1,0:T(8,128)(2,1)S(1)}, u32[]{:S(2)}, u32[]{:S(2)}) collective-permute-start(bf16[2,4,16,256]{3,2,1,0:T(8,128)(2,1)S(1)} %get-tuple-element.27), channel_id=1, source_target_pairs={{0,128},{128,256},{256,384},{384,0},{1,129},{129,257},{257,385},{3... | collective-permute-start | bytes 196616 | tf_op jit(solution)/shard_map/ppermute | solution.py:292
  30.2 6.8 %collective-permute-start.2 = (bf16[2,4,16,256]{3,2,1,0:T(8,128)(2,1)S(1)}, bf16[2,4,16,256]{3,2,1,0:T(8,128)(2,1)S(1)}, u32[]{:S(2)}, u32[]{:S(2)}) collective-permute-start(bf16[2,4,16,256]{3,2,1,0:T(8,128)(2,1)S(1)} %get-tuple-element.28), channel_id=1, source_target_pairs={{0,256},{128,384},{256,0},{384,128},{1,257},{129,385},{257,1},{385... | collective-permute-start | bytes 196616 | tf_op jit(solution)/shard_map/ppermute | solution.py:292
  37.8 18.0 %collective-permute-start.4 = (bf16[4,2,4,16,128]{4,3,2,1,0:T(8,128)(2,1)}, bf16[4,2,4,16,128]{4,3,2,1,0:T(8,128)(2,1)S(1)}, u32[]{:S(2)}, u32[]{:S(2)}) collective-permute-start(bf16[4,2,4,16,128]{4,3,2,1,0:T(8,128)(2,1)} %get-tuple-element.17), channel_id=1, source_target_pairs={{0,1},{1,2},{2,3},{3,4},{4,5},{5,6},{6,7},{7,8},{8,9},{9,10},{10,1... | collective-permute-start | bytes 393224 | tf_op jit(solution)/shard_map/ppermute | solution.py:304
  41.0 14.8 %collective-permute-start.5 = (bf16[4,2,4,16,128]{4,3,2,1,0:T(8,128)(2,1)}, bf16[4,2,4,16,128]{4,3,2,1,0:T(8,128)(2,1)S(1)}, u32[]{:S(2)}, u32[]{:S(2)}) collective-permute-start(bf16[4,2,4,16,128]{4,3,2,1,0:T(8,128)(2,1)} %get-tuple-element.18), channel_id=1, source_target_pairs={{1,0},{2,1},{3,2},{4,3},{5,4},{6,5},{7,6},{8,7},{9,8},{10,9},{11,1... | collective-permute-start | bytes 393224 | tf_op jit(solution)/shard_map/ppermute | solution.py:305
  45.7 12.7 %all-to-all-start.1 = ((f32[8,1,128]{2,1,0:T(1,128)}), f32[8,1,128]{2,1,0:T(1,128)S(1)}, u32[]{:S(2)}, u32[]{:S(2)}) async-start(f32[8,1,128]{2,1,0:T(1,128)} %sums.1), calls=%async_computation.1 | async-start | bytes 8192 | tf_op jit(solution)/shard_map/all_to_all | solution.py:316
  53.9 5.9 %collective-permute-start.6 = (bf16[2,64,3840]{2,1,0:T(8,128)(2,1)S(1)}, bf16[2,64,3840]{2,1,0:T(8,128)(2,1)S(1)}, u32[]{:S(2)}, u32[]{:S(2)}) collective-permute-start(bf16[2,64,3840]{2,1,0:T(8,128)(2,1)S(1)} %bitcast.23), channel_id=1, source_target_pairs={{0,64},{64,0},{1,65},{65,1},{2,66},{66,2},{3,67},{67,3},{4,68},{68... | collective-permute-start | bytes 2949128 | tf_op jit(solution)/shard_map/ppermute | solution.py:318
  62.8 13.6 %all-to-all-start.2 = ((f16[8,4,32,256]{3,2,1,0:T(8,128)(2,1)}), f16[8,4,32,256]{3,2,1,0:T(8,128)(2,1)S(1)}, u32[]{:S(2)}, u32[]{:S(2)}) async-start(f16[8,4,32,256]{3,2,1,0:T(8,128)(2,1)} %convert_element_type.7), calls=%async_computation.2 | async-start | bytes 1048576 | tf_op jit(solution)/shard_map/all_to_all | solution.py:354

commit v8 on v7

--- a/solution.py
+++ b/solution.py
@@ -49,7 +49,7 @@
     ]
     for move in moves:
         move.start()
-    for move in moves:
+    for move in moves[1:]:
         move.wait()
     count, channels = taps.shape[0], planes.shape[-1]
     span = lax.axis_index(TM)
@@ -60,6 +60,7 @@
     rows[count : count + 1, :] = jnp.sum(
         jnp.where(pick, skips[...].astype(jnp.float32), 0.0), axis=0, keepdims=True
     )
+    moves[0].wait()
     lines = []
     for video in range(VIDEOS):
         linear = jnp.zeros((1, channels), jnp.float32)
@@ -85,7 +86,7 @@
     for row in range(2 * LINE):
         at = row % LINE * OUT
         packed[row // LINE : row // LINE + 1, at : at + OUT] = rows[row : row + 1, :]
-    value = packed[...].astype(jnp.bfloat16)
+    value = packed[0:2, :].astype(jnp.bfloat16)
     some = few.shape[0]
     for index in range(some):
         few[index] = value
@@ -162,7 +163,9 @@
         moments[2 * video] = centre
         moments[2 * video + 1] = 0.5 * inverse * lanes[0:1, :]
         size = jnp.sqrt(square)
-        bound = tap_bound * (3.0 * jnp.max(size * inverse, keepdims=True) + 3.0)
+        ratio = size * inverse
+        ratio = jnp.where(ratio < 1e30, ratio, 0.0)
+        bound = tap_bound * (3.0 * jnp.max(ratio, keepdims=True) + 3.0)
         bound = bound + skip_bound * jnp.max(size, keepdims=True)
         bound = jnp.exp2(14.0 - jnp.floor(jnp.log2(bound)))
         factor[video : video + 1, :] = jnp.broadcast_to(bound, (1, OUT))
@@ -255,7 +258,7 @@
             pltpu.VMEM((SPANS, OUT), jnp.bfloat16),
             pltpu.SMEM((videos,), jnp.int32),
             pltpu.VMEM((32, OUT), jnp.float32),
-            pltpu.VMEM((2, LINE * OUT), jnp.float32),
+            pltpu.VMEM((8, LINE * OUT), jnp.float32),
             pltpu.VMEM((8, 2, LINE * OUT), jnp.bfloat16),
             pltpu.SemaphoreType.DMA((4,)),
             pltpu.SemaphoreType.DMA((tiles // 8,)),
@@ -332,7 +335,7 @@
         ),
         in_specs=[scalar] + [on_chip] * 5,
         out_specs=(on_chip, on_chip, on_chip),
-        scratch_shapes=[pltpu.VMEM((2 * videos, SPANS, PART), jnp.float32)],
+        scratch_shapes=[pltpu.VMEM((2 * videos + 1, SPANS, PART), jnp.float32)],
         compiler_params=params,
         cost_estimate=pl.CostEstimate(flops=1 << 34, bytes_accessed=1 << 26, transcendentals=1 << 24),
         name="norm",

time: 77.8 us -> 77.9 us (level)
  no operation moved by 1% of the time
where the time goes in v8:
time: 77.9 us; the launch traced here: 77.3 us
  starting transfers between devices  48.5 us (62%)
  waiting for transfers between devices  18.7 us (24%)
  Pallas kernels  7.85 us (10%)
  other arithmetic  1.87 us (2%)
    all_to_all x1, starting transfers between devices, per_device(): arrived = lax.all_to_all(copies, TILE, 0, 0, tiled=True)  17.1 us
    ppermute x3, starting transfers between devices, per_device(): lax.ppermute(block, 'x', [(i, (i + step) % chips) for i in range(chips)])  9.93 us
    all_to_all x1, waiting for transfers between devices, per_device(): total = lax.all_to_all(total, TM, 0, 0, tiled=True).astype(jnp.float32)  9.42 us
    all_to_all x1, starting transfers between devices, per_device(): totals = lax.all_to_all(copies, TM, 0, 0, tiled=True).reshape(SPANS, -1)  8.11 us
    all_to_all x1, starting transfers between devices, per_device(): total = lax.all_to_all(total, TM, 0, 0, tiled=True).astype(jnp.float32)  4.07 us
    ppermute x1, starting transfers between devices, per_device(): above = lax.ppermute(upper, TILE, [(i, i + 1) for i in range(tiles - 1)])  3.19 us
    ppermute x3, waiting for transfers between devices, per_device(): lax.ppermute(block, 'x', [(i, (i + step) % chips) for i in range(chips)])  3.17 us
    ppermute x1, starting transfers between devices, per_device(): shares = jnp.stack([kept, lax.ppermute(sent, 'core', swap)], axis=1)  2.86 us
  transfers between devices with their start and end apart: 10, of which 6 were waited for; matrix products, arithmetic and copies ran while one was open for 0% of the time, Pallas kernels for 4%

profile of v8, /device:TPU:1, one launch (start us, length us, event | category | flops | bytes accessed | tf_op | source)
XLA Modules:
  0.0 77.3 jit_solution(2748808357038299995)
XLA Ops:
  0.0 2.5 %payload.1 = bf16[64,2,3840]{2,1,0:T(2,128)(2,1)} custom-call(bf16[8,32,512]{2,1,0:T(8,128)(2,1)} %bitcast.21, bf16[27,8,256]{2,1,0:T(8,128)(2,1)} %bitcast.32, bf16[8,256]{1,0:T(8,128)(2,1)} %skip.1, s32[2]{0:T(128)} %lengths.3), custom_call_target="tpu_custom_call" | custom-call | tf_op jit(solution)/shard_map/payload/pallas_call | solution.py:250
  2.5 17.1 %all-to-all-start = ((bf16[64,2,3840]{2,1,0:T(2,128)(2,1)}), bf16[64,2,3840]{2,1,0:T(2,128)(2,1)S(1)}, u32[]{:S(2)}, u32[]{:S(2)}) async-start(bf16[64,2,3840]{2,1,0:T(2,128)(2,1)} %payload.1), calls=%async_computation | async-start | bytes 1966080 | tf_op jit(solution)/shard_map/all_to_all | solution.py:274
  19.7 0.4 member_shares.1
  20.1 2.9 %collective-permute-start = (bf16[4,4,16,256]{3,2,1,0:T(8,128)(2,1)S(1)}, bf16[4,4,16,256]{3,2,1,0:T(8,128)(2,1)S(1)}, u32[]{:S(2)}, u32[]{:S(2)}) collective-permute-start(bf16[4,4,16,256]{3,2,1,0:T(8,128)(2,1)S(1)} %get-tuple-element.16), channel_id=1, source_target_pairs={{0,64},{64,0},{1,65},{65,1},{2,66},{66,2},{3,67},{67,3},{4,68},{68... | collective-permute-start | bytes 393224 | tf_op jit(solution)/shard_map/ppermute | solution.py:290
  23.0 0.9 %collective-permute-done = bf16[4,4,16,256]{3,2,1,0:T(8,128)(2,1)S(1)} collective-permute-done((bf16[4,4,16,256]{3,2,1,0:T(8,128)(2,1)S(1)}, bf16[4,4,16,256]{3,2,1,0:T(8,128)(2,1)S(1)}, u32[]{:S(2)}, u32[]{:S(2)}) %collective-permute-start) | collective-permute-done | bytes 131104 | tf_op jit(solution)/shard_map/ppermute | solution.py:290
  24.0 0.0 copy-start.3
  24.0 4.4 %collective-permute-start.3 = (bf16[2,4,16,256]{3,2,1,0:T(8,128)(2,1)S(1)}, bf16[2,4,16,256]{3,2,1,0:T(8,128)(2,1)S(1)}, u32[]{:S(2)}, u32[]{:S(2)}) collective-permute-start(bf16[2,4,16,256]{3,2,1,0:T(8,128)(2,1)S(1)} %get-tuple-element.25), channel_id=1, source_target_pairs={{0,384},{128,0},{256,128},{384,256},{1,385},{129,1},{257,129},{385... | collective-permute-start | bytes 196616 | tf_op jit(solution)/shard_map/ppermute | solution.py:295
  28.4 1.9 %collective-permute-start.1 = (bf16[2,4,16,256]{3,2,1,0:T(8,128)(2,1)S(1)}, bf16[2,4,16,256]{3,2,1,0:T(8,128)(2,1)S(1)}, u32[]{:S(2)}, u32[]{:S(2)}) collective-permute-start(bf16[2,4,16,256]{3,2,1,0:T(8,128)(2,1)S(1)} %get-tuple-element.27), channel_id=1, source_target_pairs={{0,128},{128,256},{256,384},{384,0},{1,129},{129,257},{257,385},{3... | collective-permute-start | bytes 196616 | tf_op jit(solution)/shard_map/ppermute | solution.py:295
  30.3 3.6 %collective-permute-start.2 = (bf16[2,4,16,256]{3,2,1,0:T(8,128)(2,1)S(1)}, bf16[2,4,16,256]{3,2,1,0:T(8,128)(2,1)S(1)}, u32[]{:S(2)}, u32[]{:S(2)}) collective-permute-start(bf16[2,4,16,256]{3,2,1,0:T(8,128)(2,1)S(1)} %get-tuple-element.28), channel_id=1, source_target_pairs={{0,256},{128,384},{256,0},{384,128},{1,257},{129,385},{257,1},{385... | collective-permute-start | bytes 196616 | tf_op jit(solution)/shard_map/ppermute | solution.py:295
  33.9 0.0 collective-permute-done.3.refs_3_
  34.0 0.9 %collective-permute-done.1.refs_1_ = bf16[2,4,16,256]{3,2,1,0:T(8,128)(2,1)S(1)} collective-permute-done((bf16[2,4,16,256]{3,2,1,0:T(8,128)(2,1)S(1)}, bf16[2,4,16,256]{3,2,1,0:T(8,128)(2,1)S(1)}, u32[]{:S(2)}, u32[]{:S(2)}) %collective-permute-start.1) | collective-permute-done | bytes 65568 | tf_op jit(solution)/shard_map/ppermute | solution.py:295
  34.9 2.2 %collective-permute-done.2.refs_2_ = bf16[2,4,16,256]{3,2,1,0:T(8,128)(2,1)S(1)} collective-permute-done((bf16[2,4,16,256]{3,2,1,0:T(8,128)(2,1)S(1)}, bf16[2,4,16,256]{3,2,1,0:T(8,128)(2,1)S(1)}, u32[]{:S(2)}, u32[]{:S(2)}) %collective-permute-start.2) | collective-permute-done | bytes 65568 | tf_op jit(solution)/shard_map/ppermute | solution.py:295
  37.1 0.8 edges.1
  37.9 3.2 %collective-permute-start.4 = (bf16[4,2,4,16,128]{4,3,2,1,0:T(8,128)(2,1)}, bf16[4,2,4,16,128]{4,3,2,1,0:T(8,128)(2,1)S(1)}, u32[]{:S(2)}, u32[]{:S(2)}) collective-permute-start(bf16[4,2,4,16,128]{4,3,2,1,0:T(8,128)(2,1)} %get-tuple-element.17), channel_id=1, source_target_pairs={{0,1},{1,2},{2,3},{3,4},{4,5},{5,6},{6,7},{7,8},{8,9},{9,10},{10,1... | collective-permute-start | bytes 393224 | tf_op jit(solution)/shard_map/ppermute | solution.py:307
  41.1 1.3 %collective-permute-start.5 = (bf16[4,2,4,16,128]{4,3,2,1,0:T(8,128)(2,1)}, bf16[4,2,4,16,128]{4,3,2,1,0:T(8,128)(2,1)S(1)}, u32[]{:S(2)}, u32[]{:S(2)}) collective-permute-start(bf16[4,2,4,16,128]{4,3,2,1,0:T(8,128)(2,1)} %get-tuple-element.18), channel_id=1, source_target_pairs={{1,0},{2,1},{3,2},{4,3},{5,4},{6,5},{7,6},{8,7},{9,8},{10,9},{11,1... | collective-permute-start | bytes 393224 | tf_op jit(solution)/shard_map/ppermute | solution.py:308
  42.4 2.7 %all-to-all-done.arrived = bf16[64,2,3840]{2,1,0:T(2,128)(2,1)S(1)} async-done(((bf16[64,2,3840]{2,1,0:T(2,128)(2,1)}), bf16[64,2,3840]{2,1,0:T(2,128)(2,1)S(1)}, u32[]{:S(2)}, u32[]{:S(2)}) %all-to-all-start) | async-done | bytes 983072 | tf_op jit(solution)/shard_map/all_to_all | solution.py:274
  45.0 0.7 sums.1
  45.7 8.1 %all-to-all-start.1 = ((f32[8,1,128]{2,1,0:T(1,128)}), f32[8,1,128]{2,1,0:T(1,128)S(1)}, u32[]{:S(2)}, u32[]{:S(2)}) async-start(f32[8,1,128]{2,1,0:T(1,128)} %sums.1), calls=%async_computation.1 | async-start | bytes 8192 | tf_op jit(solution)/shard_map/all_to_all | solution.py:319
  53.8 0.1 copy.12
  53.9 1.9 %collective-permute-start.6 = (bf16[2,64,3840]{2,1,0:T(8,128)(2,1)S(1)}, bf16[2,64,3840]{2,1,0:T(8,128)(2,1)S(1)}, u32[]{:S(2)}, u32[]{:S(2)}) collective-permute-start(bf16[2,64,3840]{2,1,0:T(8,128)(2,1)S(1)} %bitcast.23), channel_id=1, source_target_pairs={{0,64},{64,0},{1,65},{65,1},{2,66},{66,2},{3,67},{67,3},{4,68},{68... | collective-permute-start | bytes 2949128 | tf_op jit(solution)/shard_map/ppermute | solution.py:321
  55.9 0.0 collective-permute-done.4.above
  55.9 0.0 collective-permute-done.5.below
  55.9 2.5 %all-to-all-done.1 = f32[8,1,128]{2,1,0:T(1,128)S(1)} async-done(((f32[8,1,128]{2,1,0:T(1,128)}), f32[8,1,128]{2,1,0:T(1,128)S(1)}, u32[]{:S(2)}, u32[]{:S(2)}) %all-to-all-start.1) | async-done | bytes 4128 | tf_op jit(solution)/shard_map/all_to_all | solution.py:319
  58.4 1.4 %norm.1 = (bf16[3,34,16,512]{3,2,1,0:T(8,128)(2,1)S(1)}, bf16[32,16,256]{2,1,0:T(8,128)(2,1)S(1)}, f32[2,256]{1,0:T(2,128)S(1)}) custom-call(s32[2]{0:T(128)S(1)} %copy-done.3, f32[8,128]{1,0:T(8,128)S(1)} %bitcast.26, f32[2,128]{1,0:T(2,128)S(1)} %get-tuple-element.20.lanes, bf16[4,2,4,16,256]{4,3,2,1,0:T(8,128)(2,1)S(1)} %get-tuple-element.21.signal, ...), custom_call_target="tpu_custom_call" | custom-call | flops 17179869184 | bytes 67108864 | tf_op jit(solution)/shard_map/norm/pallas_call | solution.py:323
  59.8 0.0 collective-permute-done.6.theirs
  59.8 2.1 %taps.1 = f32[8,4,32,256]{3,2,1,0:T(8,128)S(1)} custom-call(bf16[3,34,16,512]{3,2,1,0:T(8,128)(2,1)S(1)} %get-tuple-element.22.shifted, bf16[32,16,256]{2,1,0:T(8,128)(2,1)S(1)} %get-tuple-element.23.raw, bf16[2,64,3840]{2,1,0:T(8,128)(2,1)S(1)} %bitcast.24, bf16[2,64,3840]{2,1,0:T(8,128)(2,1)S(1)} %collective-permute-done.6.theirs, ...), custom_call_target="tpu_custom_call" | custom-call | flops 1879048192 | bytes 6291456 | tf_op jit(solution)/shard_map/taps/pallas_call | solution.py:343
  61.9 0.9 %convert_element_type.7 = f16[8,4,32,256]{3,2,1,0:T(8,128)(2,1)} convert(f32[8,4,32,256]{3,2,1,0:T(8,128)S(1)} %taps.1) | non-fusion elementwise | flops 262144 | bytes 1572864 | tf_op jit(solution)/shard_map/convert_element_type | solution.py:356
  62.9 4.1 %all-to-all-start.2 = ((f16[8,4,32,256]{3,2,1,0:T(8,128)(2,1)}), f16[8,4,32,256]{3,2,1,0:T(8,128)(2,1)S(1)}, u32[]{:S(2)}, u32[]{:S(2)}) async-start(f16[8,4,32,256]{3,2,1,0:T(8,128)(2,1)} %convert_element_type.7), calls=%async_computation.2 | async-start | bytes 1048576 | tf_op jit(solution)/shard_map/all_to_all | solution.py:357
  66.9 0.1 broadcast_compare_fusion
  67.0 9.4 %all-to-all-done.2 = f16[8,4,32,256]{3,2,1,0:T(8,128)(2,1)S(1)} async-done(((f16[8,4,32,256]{3,2,1,0:T(8,128)(2,1)}), f16[8,4,32,256]{3,2,1,0:T(8,128)(2,1)S(1)}, u32[]{:S(2)}, u32[]{:S(2)}) %all-to-all-start.2) | async-done | bytes 524320 | tf_op jit(solution)/shard_map/all_to_all | solution.py:357
  76.4 0.1 convert_reduce_fusion
  76.5 0.7 select_convert_fusion
  (9 shorter events, 0.0 us)
Async XLA Ops:
  0.0 19.7 %copy-start = (bf16[2,4,2,16,512]{4,3,2,1,0:T(8,128)(2,1)S(1)}, bf16[2,4,2,16,512]{4,3,2,1,0:T(8,128)(2,1)}, u32[]{:S(2)}) copy-start(bf16[2,4,2,16,512]{4,3,2,1,0:T(8,128)(2,1)} %param.6) | copy-start | bytes 786436
  0.0 19.7 %copy-start.2 = (f32[512]{0:T(512)S(1)}, f32[512]{0:T(512)}, u32[]{:S(2)}) copy-start(f32[512]{0:T(512)} %param.9) | copy-start | bytes 6148
  0.0 19.7 %copy-start.1 = (f32[512]{0:T(512)S(1)}, f32[512]{0:T(512)}, u32[]{:S(2)}) copy-start(f32[512]{0:T(512)} %param.8) | copy-start | bytes 6148
  2.5 42.5 %all-to-all-start = ((bf16[64,2,3840]{2,1,0:T(2,128)(2,1)}), bf16[64,2,3840]{2,1,0:T(2,128)(2,1)S(1)}, u32[]{:S(2)}, u32[]{:S(2)}) async-start(bf16[64,2,3840]{2,1,0:T(2,128)(2,1)} %payload.1), calls=%async_computation | async-start | bytes 1966080 | tf_op jit(solution)/shard_map/all_to_all | solution.py:274
  20.1 3.8 %collective-permute-start = (bf16[4,4,16,256]{3,2,1,0:T(8,128)(2,1)S(1)}, bf16[4,4,16,256]{3,2,1,0:T(8,128)(2,1)S(1)}, u32[]{:S(2)}, u32[]{:S(2)}) collective-permute-start(bf16[4,4,16,256]{3,2,1,0:T(8,128)(2,1)S(1)} %get-tuple-element.16), channel_id=1, source_target_pairs={{0,64},{64,0},{1,65},{65,1},{2,66},{66,2},{3,67},{67,3},{4,68},{68... | collective-permute-start | bytes 393224 | tf_op jit(solution)/shard_map/ppermute | solution.py:290
  24.0 34.4 %copy-start.3 = (s32[2]{0:T(128)S(1)}, s32[2]{0:T(128)}, u32[]{:S(2)}) copy-start(s32[2]{0:T(128)} %lengths.3) | copy-start | bytes 28
  24.0 10.0 %collective-permute-start.3 = (bf16[2,4,16,256]{3,2,1,0:T(8,128)(2,1)S(1)}, bf16[2,4,16,256]{3,2,1,0:T(8,128)(2,1)S(1)}, u32[]{:S(2)}, u32[]{:S(2)}) collective-permute-start(bf16[2,4,16,256]{3,2,1,0:T(8,128)(2,1)S(1)} %get-tuple-element.25), channel_id=1, source_target_pairs={{0,384},{128,0},{256,128},{384,256},{1,385},{129,1},{257,129},{385... | collective-permute-start | bytes 196616 | tf_op jit(solution)/shard_map/ppermute | solution.py:295
  28.4 6.5 %collective-permute-start.1 = (bf16[2,4,16,256]{3,2,1,0:T(8,128)(2,1)S(1)}, bf16[2,4,16,256]{3,2,1,0:T(8,128)(2,1)S(1)}, u32[]{:S(2)}, u32[]{:S(2)}) collective-permute-start(bf16[2,4,16,256]{3,2,1,0:T(8,128)(2,1)S(1)} %get-tuple-element.27), channel_id=1, source_target_pairs={{0,128},{128,256},{256,384},{384,0},{1,129},{129,257},{257,385},{3... | collective-permute-start | bytes 196616 | tf_op jit(solution)/shard_map/ppermute | solution.py:295
  30.3 6.8 %collective-permute-start.2 = (bf16[2,4,16,256]{3,2,1,0:T(8,128)(2,1)S(1)}, bf16[2,4,16,256]{3,2,1,0:T(8,128)(2,1)S(1)}, u32[]{:S(2)}, u32[]{:S(2)}) collective-permute-start(bf16[2,4,16,256]{3,2,1,0:T(8,128)(2,1)S(1)} %get-tuple-element.28), channel_id=1, source_target_pairs={{0,256},{128,384},{256,0},{384,128},{1,257},{129,385},{257,1},{385... | collective-permute-start | bytes 196616 | tf_op jit(solution)/shard_map/ppermute | solution.py:295
  37.9 18.0 %collective-permute-start.4 = (bf16[4,2,4,16,128]{4,3,2,1,0:T(8,128)(2,1)}, bf16[4,2,4,16,128]{4,3,2,1,0:T(8,128)(2,1)S(1)}, u32[]{:S(2)}, u32[]{:S(2)}) collective-permute-start(bf16[4,2,4,16,128]{4,3,2,1,0:T(8,128)(2,1)} %get-tuple-element.17), channel_id=1, source_target_pairs={{0,1},{1,2},{2,3},{3,4},{4,5},{5,6},{6,7},{7,8},{8,9},{9,10},{10,1... | collective-permute-start | bytes 393224 | tf_op jit(solution)/shard_map/ppermute | solution.py:307
  41.1 14.8 %collective-permute-start.5 = (bf16[4,2,4,16,128]{4,3,2,1,0:T(8,128)(2,1)}, bf16[4,2,4,16,128]{4,3,2,1,0:T(8,128)(2,1)S(1)}, u32[]{:S(2)}, u32[]{:S(2)}) collective-permute-start(bf16[4,2,4,16,128]{4,3,2,1,0:T(8,128)(2,1)} %get-tuple-element.18), channel_id=1, source_target_pairs={{1,0},{2,1},{3,2},{4,3},{5,4},{6,5},{7,6},{8,7},{9,8},{10,9},{11,1... | collective-permute-start | bytes 393224 | tf_op jit(solution)/shard_map/ppermute | solution.py:308
  45.7 12.7 %all-to-all-start.1 = ((f32[8,1,128]{2,1,0:T(1,128)}), f32[8,1,128]{2,1,0:T(1,128)S(1)}, u32[]{:S(2)}, u32[]{:S(2)}) async-start(f32[8,1,128]{2,1,0:T(1,128)} %sums.1), calls=%async_computation.1 | async-start | bytes 8192 | tf_op jit(solution)/shard_map/all_to_all | solution.py:319
  53.9 5.9 %collective-permute-start.6 = (bf16[2,64,3840]{2,1,0:T(8,128)(2,1)S(1)}, bf16[2,64,3840]{2,1,0:T(8,128)(2,1)S(1)}, u32[]{:S(2)}, u32[]{:S(2)}) collective-permute-start(bf16[2,64,3840]{2,1,0:T(8,128)(2,1)S(1)} %bitcast.23), channel_id=1, source_target_pairs={{0,64},{64,0},{1,65},{65,1},{2,66},{66,2},{3,67},{67,3},{4,68},{68... | collective-permute-start | bytes 2949128 | tf_op jit(solution)/shard_map/ppermute | solution.py:321
  62.9 13.6 %all-to-all-start.2 = ((f16[8,4,32,256]{3,2,1,0:T(8,128)(2,1)}), f16[8,4,32,256]{3,2,1,0:T(8,128)(2,1)S(1)}, u32[]{:S(2)}, u32[]{:S(2)}) async-start(f16[8,4,32,256]{3,2,1,0:T(8,128)(2,1)} %convert_element_type.7), calls=%async_computation.2 | async-start | bytes 1048576 | tf_op jit(solution)/shard_map/all_to_all | solution.py:357

commit v9 on v8

--- a/solution.py
+++ b/solution.py
@@ -20,8 +20,9 @@
 CHIPS = 4
 PART = 2 * SHARE
 ROWS = 4
-LINE = 15
+LINE = 14
 OUT = 256
+WIDTH = LINE * OUT + 128
 
 
 def to_all(block, axis):
@@ -40,7 +41,21 @@
     return total + jnp.dot(high, chosen, preferred_element_type=jnp.float32)
 
 
-def payload_kernel(features, conv, skip, lengths, copies, planes, taps, skips, valid, rows, packed, few, done, left):
+def own_counts(lengths, span):
+    lane = lax.broadcasted_iota(jnp.int32, (1, 128), 1)
+    count = jnp.where(lane % (2 * GROUPS) < GROUPS, lengths[0], lengths[1]) - span * FRAMES
+    count = jnp.clip(count, 1, FRAMES).astype(jnp.float32)
+    return 1.0 / (count * float(2 * COLS * SPANS * SHARE // GROUPS))
+
+
+def own_square(value, inverse):
+    axis = value.ndim - 1
+    turned = pltpu.roll(value, 2 * GROUPS, axis)
+    upper = lax.broadcasted_iota(jnp.int32, (1,) * axis + (128,), axis) >= 2 * GROUPS
+    return jnp.where(upper, turned * turned * inverse, 0.0)
+
+
+def payload_kernel(features, conv, skip, lengths, copies, counts, planes, taps, skips, valid, rows, packed, few, done, left):
     moves = [
         pltpu.make_async_copy(source, target, done.at[index])
         for index, (source, target) in enumerate(
@@ -78,11 +93,17 @@
     line = lax.broadcasted_iota(jnp.int32, spots.shape, 0)
     lane = lax.broadcasted_iota(jnp.int32, spots.shape, 1)
     sums = jnp.sum(jnp.where(lane // GROUPS == line, spots, 0.0), axis=0, keepdims=True)
+    sums = jnp.broadcast_to(sums, (8, 128))
+    inverse = own_counts(valid, span)
+    sums = sums - own_square(sums, inverse)
+    counts[...] = jnp.concatenate(
+        [jnp.full((1, 128), valid[video]).astype(jnp.float32) for video in range(VIDEOS)]
+        + [inverse, jnp.zeros((5, 128), jnp.float32)],
+        axis=0,
+    )
     high = sums.astype(jnp.bfloat16).astype(jnp.float32)
-    middle = (sums - high).astype(jnp.bfloat16).astype(jnp.float32)
-    rows[count + 1 : count + 2, 0:128] = high
-    rows[count + 1 : count + 2, 128:256] = middle
-    rows[count + 2 : count + 3, 0:128] = sums - high - middle
+    for line, value in enumerate((high, sums - high)):
+        packed[line : line + 1, LINE * OUT : WIDTH] = value[0:1]
     for row in range(2 * LINE):
         at = row % LINE * OUT
         packed[row // LINE : row // LINE + 1, at : at + OUT] = rows[row : row + 1, :]
@@ -100,11 +121,12 @@
         move.wait()
 
 
-def sums_kernel(arrived, copies, *, first):
-    at = (first - LINE) * OUT
-    line = jnp.sum(arrived[:, :, at : at + 2 * OUT].astype(jnp.float32), axis=0)[1:2]
-    total = line[:, 256:384] + line[:, 128:256] + line[:, 0:128]
-    copies[...] = jnp.broadcast_to(total[None], copies.shape)
+def sums_kernel(counts, arrived, copies):
+    value = arrived[:, 0:1, LINE * OUT : WIDTH].astype(jnp.float32)
+    value = value + arrived[:, 1:2, LINE * OUT : WIDTH].astype(jnp.float32)
+    value = value + own_square(value, counts[2:3, :].reshape(1, 1, 128))
+    total = jnp.sum(value, axis=0, keepdims=True)
+    copies[...] = jnp.broadcast_to(total, copies.shape)
 
 
 def member_kernel(features, gain, bias, kept, sent, lanes):
@@ -141,7 +163,7 @@
 
 
 def norm_kernel(
-    lengths, totals, lanes, signal, above, below, shifted, raw, factor, moments,
+    totals, counts, lanes, signal, above, below, shifted, raw, factor, moments,
     *, cells, tiles, tap_bound, skip_bound
 ):
     chip, core = lax.axis_index("x"), lax.axis_index("core")
@@ -154,9 +176,9 @@
     lane = lax.broadcasted_iota(jnp.int32, (128, 4 * PART), 1)
     wanted = lane // PART * GROUPS + lane % SHARE // 2
     spread = exact_dot(summed, jnp.where(entry == wanted, 1.0, 0.0).astype(jnp.bfloat16))
-    ends = (lax.broadcasted_iota(jnp.int32, (SPANS, PART), 0) + 1) * FRAMES
+    ends = ((lax.broadcasted_iota(jnp.int32, (SPANS, PART), 0) + 1) * FRAMES).astype(jnp.float32)
     for video in range(VIDEOS):
-        seen = jnp.minimum(ends, lengths[video]).astype(jnp.float32) * cells
+        seen = jnp.minimum(ends, counts[video : video + 1, :]) * cells
         square = spread[:, (VIDEOS + video) * PART : (VIDEOS + video + 1) * PART]
         centre = spread[:, video * PART : (video + 1) * PART] / seen
         inverse = lax.rsqrt(square / seen - centre * centre + EPS)
@@ -170,10 +192,11 @@
         bound = jnp.exp2(14.0 - jnp.floor(jnp.log2(bound)))
         factor[video : video + 1, :] = jnp.broadcast_to(bound, (1, OUT))
     half_bias = 0.5 * lanes[1:2, :]
+    length = jnp.where(core == 0, counts[0:1, :], counts[1:2, :]).reshape(1, 1, PART)
 
     def normed(value, span):
         frame = lax.broadcasted_iota(jnp.int32, (FRAMES, 1, PART), 0) + span * FRAMES
-        shown = frame < lengths[core]
+        shown = frame.astype(jnp.float32) < length
         centre = moments[2 * core, pl.ds(span, 1)].reshape(1, 1, PART)
         scale = jnp.where(shown, moments[2 * core + 1, pl.ds(span, 1)].reshape(1, 1, PART), 0.0)
         offset = jnp.where(shown, half_bias.reshape(1, 1, PART), 0.0)
@@ -243,23 +266,25 @@
     taps = conv_in.shape[1]
     on_chip = pl.BlockSpec(memory_space=pltpu.VMEM)
     outside = pl.BlockSpec(memory_space=pl.ANY)
-    scalar = pl.BlockSpec(memory_space=pltpu.SMEM)
     params = pltpu.CompilerParams(vmem_limit_bytes=20 * 1024 * 1024)
 
     planes = features.reshape(videos * frames, row_count * col_count, wide_in)
-    copies = pl.pallas_call(
+    copies, counts = pl.pallas_call(
         payload_kernel,
-        out_shape=jax.ShapeDtypeStruct((tiles, 2, LINE * OUT), jnp.bfloat16),
+        out_shape=(
+            jax.ShapeDtypeStruct((tiles, 2, WIDTH), jnp.bfloat16),
+            jax.ShapeDtypeStruct((8, 128), jnp.float32),
+        ),
         in_specs=[outside] * 4,
-        out_specs=outside,
+        out_specs=(outside, on_chip),
         scratch_shapes=[
             pltpu.VMEM(planes.shape, jnp.bfloat16),
             pltpu.VMEM((taps, SPANS, OUT), jnp.bfloat16),
             pltpu.VMEM((SPANS, OUT), jnp.bfloat16),
             pltpu.SMEM((videos,), jnp.int32),
             pltpu.VMEM((32, OUT), jnp.float32),
-            pltpu.VMEM((8, LINE * OUT), jnp.float32),
-            pltpu.VMEM((8, 2, LINE * OUT), jnp.bfloat16),
+            pltpu.VMEM((8, WIDTH), jnp.float32),
+            pltpu.VMEM((8, 2, WIDTH), jnp.bfloat16),
             pltpu.SemaphoreType.DMA((4,)),
             pltpu.SemaphoreType.DMA((tiles // 8,)),
         ],
@@ -309,13 +334,13 @@
 
     held, upper, lower = lax.optimization_barrier((arrived, upper, lower))
     copies = pl.pallas_call(
-        functools.partial(sums_kernel, first=taps + 1),
+        sums_kernel,
         out_shape=jax.ShapeDtypeStruct((SPANS, 1, 128), jnp.float32),
-        in_specs=[on_chip],
+        in_specs=[on_chip, on_chip],
         out_specs=on_chip,
         compiler_params=params,
         name="sums",
-    )(pltpu.with_memory_space_constraint(held, pltpu.VMEM))
+    )(counts, pltpu.with_memory_space_constraint(held, pltpu.VMEM))
     totals = lax.all_to_all(copies, TM, 0, 0, tiled=True).reshape(SPANS, -1)
     mine = arrived.transpose(1, 0, 2)
     theirs = lax.ppermute(mine, "core", swap)
@@ -333,13 +358,13 @@
             jax.ShapeDtypeStruct((SPANS * frames, col_count, 2 * PART), jnp.bfloat16),
             jax.ShapeDtypeStruct((videos, OUT), jnp.float32),
         ),
-        in_specs=[scalar] + [on_chip] * 5,
+        in_specs=[on_chip] * 6,
         out_specs=(on_chip, on_chip, on_chip),
         scratch_shapes=[pltpu.VMEM((2 * videos + 1, SPANS, PART), jnp.float32)],
         compiler_params=params,
         cost_estimate=pl.CostEstimate(flops=1 << 34, bytes_accessed=1 << 26, transcendentals=1 << 24),
         name="norm",
-    )(lengths, totals, lanes, signal, above, below)
+    )(totals, counts, lanes, signal, above, below)
     total = pl.pallas_call(
         taps_kernel,
         out_shape=jax.ShapeDtypeStruct((SPANS, frames, row_count * col_count, OUT), jnp.float32),

time: 77.9 us -> 76.7 us (0.985)
  transfers between devices with their start and end apart: 10 -> 10, of which waited for: 6 -> 6; matrix products, arithmetic and copies ran while one was open for 0% -> 0% of each run, Pallas kernels for 4% -> 3%
where the time goes in v9:
time: 76.7 us; the launch traced here: 76.2 us
  starting transfers between devices  48.6 us (63%)
  waiting for transfers between devices  18.1 us (24%)
  Pallas kernels  7.27 us (9%)
  other arithmetic  1.86 us (2%)
    all_to_all x1, starting transfers between devices, per_device(): arrived = lax.all_to_all(copies, TILE, 0, 0, tiled=True)  17.1 us
    ppermute x3, starting transfers between devices, per_device(): lax.ppermute(block, 'x', [(i, (i + step) % chips) for i in range(chips)])  9.93 us
    all_to_all x1, waiting for transfers between devices, per_device(): total = lax.all_to_all(total, TM, 0, 0, tiled=True).astype(jnp.float32)  9.42 us
    all_to_all x1, starting transfers between devices, per_device(): totals = lax.all_to_all(copies, TM, 0, 0, tiled=True).reshape(SPANS, -1)  8.2 us
    all_to_all x1, starting transfers between devices, per_device(): total = lax.all_to_all(total, TM, 0, 0, tiled=True).astype(jnp.float32)  4.07 us
    ppermute x1, starting transfers between devices, per_device(): above = lax.ppermute(upper, TILE, [(i, i + 1) for i in range(tiles - 1)])  3.19 us
    ppermute x3, waiting for transfers between devices, per_device(): lax.ppermute(block, 'x', [(i, (i + step) % chips) for i in range(chips)])  3.16 us
    ppermute x1, starting transfers between devices, per_device(): shares = jnp.stack([kept, lax.ppermute(sent, 'core', swap)], axis=1)  2.86 us
  transfers between devices with their start and end apart: 10, of which 6 were waited for; matrix products, arithmetic and copies ran while one was open for 0% of the time, Pallas kernels for 3%

profile of v9, /device:TPU:1, one launch (start us, length us, event | category | flops | bytes accessed | tf_op | source)
XLA Modules:
  0.0 76.2 jit_solution(6937218663917591197)
XLA Ops:
  0.0 2.6 %payload.1 = (bf16[64,2,3712]{2,1,0:T(2,128)(2,1)}, f32[8,128]{1,0:T(8,128)S(1)}) custom-call(bf16[8,32,512]{2,1,0:T(8,128)(2,1)} %bitcast.21, bf16[27,8,256]{2,1,0:T(8,128)(2,1)} %bitcast.32, bf16[8,256]{1,0:T(8,128)(2,1)} %skip.1, s32[2]{0:T(128)} %lengths.1), custom_call_target="tpu_custom_call" | custom-call | tf_op jit(solution)/shard_map/payload/pallas_call | solution.py:272
  2.6 17.1 %all-to-all-start = ((bf16[64,2,3712]{2,1,0:T(2,128)(2,1)}), bf16[64,2,3712]{2,1,0:T(2,128)(2,1)S(1)}, u32[]{:S(2)}, u32[]{:S(2)}) async-start(bf16[64,2,3712]{2,1,0:T(2,128)(2,1)} %get-tuple-element.18), calls=%async_computation | async-start | bytes 1900544 | tf_op jit(solution)/shard_map/all_to_all | solution.py:299
  19.8 0.4 member_shares.1
  20.2 2.9 %collective-permute-start = (bf16[4,4,16,256]{3,2,1,0:T(8,128)(2,1)S(1)}, bf16[4,4,16,256]{3,2,1,0:T(8,128)(2,1)S(1)}, u32[]{:S(2)}, u32[]{:S(2)}) collective-permute-start(bf16[4,4,16,256]{3,2,1,0:T(8,128)(2,1)S(1)} %get-tuple-element.20), channel_id=1, source_target_pairs={{0,64},{64,0},{1,65},{65,1},{2,66},{66,2},{3,67},{67,3},{4,68},{68... | collective-permute-start | bytes 393224 | tf_op jit(solution)/shard_map/ppermute | solution.py:315
  23.1 0.9 %collective-permute-done = bf16[4,4,16,256]{3,2,1,0:T(8,128)(2,1)S(1)} collective-permute-done((bf16[4,4,16,256]{3,2,1,0:T(8,128)(2,1)S(1)}, bf16[4,4,16,256]{3,2,1,0:T(8,128)(2,1)S(1)}, u32[]{:S(2)}, u32[]{:S(2)}) %collective-permute-start) | collective-permute-done | bytes 131104 | tf_op jit(solution)/shard_map/ppermute | solution.py:315
  24.0 4.4 %collective-permute-start.3 = (bf16[2,4,16,256]{3,2,1,0:T(8,128)(2,1)S(1)}, bf16[2,4,16,256]{3,2,1,0:T(8,128)(2,1)S(1)}, u32[]{:S(2)}, u32[]{:S(2)}) collective-permute-start(bf16[2,4,16,256]{3,2,1,0:T(8,128)(2,1)S(1)} %get-tuple-element.29), channel_id=1, source_target_pairs={{0,384},{128,0},{256,128},{384,256},{1,385},{129,1},{257,129},{385... | collective-permute-start | bytes 196616 | tf_op jit(solution)/shard_map/ppermute | solution.py:320
  28.4 1.9 %collective-permute-start.1 = (bf16[2,4,16,256]{3,2,1,0:T(8,128)(2,1)S(1)}, bf16[2,4,16,256]{3,2,1,0:T(8,128)(2,1)S(1)}, u32[]{:S(2)}, u32[]{:S(2)}) collective-permute-start(bf16[2,4,16,256]{3,2,1,0:T(8,128)(2,1)S(1)} %get-tuple-element.31), channel_id=1, source_target_pairs={{0,128},{128,256},{256,384},{384,0},{1,129},{129,257},{257,385},{3... | collective-permute-start | bytes 196616 | tf_op jit(solution)/shard_map/ppermute | solution.py:320
  30.3 3.6 %collective-permute-start.2 = (bf16[2,4,16,256]{3,2,1,0:T(8,128)(2,1)S(1)}, bf16[2,4,16,256]{3,2,1,0:T(8,128)(2,1)S(1)}, u32[]{:S(2)}, u32[]{:S(2)}) collective-permute-start(bf16[2,4,16,256]{3,2,1,0:T(8,128)(2,1)S(1)} %get-tuple-element.32), channel_id=1, source_target_pairs={{0,256},{128,384},{256,0},{384,128},{1,257},{129,385},{257,1},{385... | collective-permute-start | bytes 196616 | tf_op jit(solution)/shard_map/ppermute | solution.py:320
  34.0 0.0 collective-permute-done.3.refs_3_
  34.0 0.9 %collective-permute-done.1.refs_1_ = bf16[2,4,16,256]{3,2,1,0:T(8,128)(2,1)S(1)} collective-permute-done((bf16[2,4,16,256]{3,2,1,0:T(8,128)(2,1)S(1)}, bf16[2,4,16,256]{3,2,1,0:T(8,128)(2,1)S(1)}, u32[]{:S(2)}, u32[]{:S(2)}) %collective-permute-start.1) | collective-permute-done | bytes 65568 | tf_op jit(solution)/shard_map/ppermute | solution.py:320
  34.9 2.2 %collective-permute-done.2.refs_2_ = bf16[2,4,16,256]{3,2,1,0:T(8,128)(2,1)S(1)} collective-permute-done((bf16[2,4,16,256]{3,2,1,0:T(8,128)(2,1)S(1)}, bf16[2,4,16,256]{3,2,1,0:T(8,128)(2,1)S(1)}, u32[]{:S(2)}, u32[]{:S(2)}) %collective-permute-start.2) | collective-permute-done | bytes 65568 | tf_op jit(solution)/shard_map/ppermute | solution.py:320
  37.2 0.7 edges.1
  37.9 3.2 %collective-permute-start.4 = (bf16[4,2,4,16,128]{4,3,2,1,0:T(8,128)(2,1)}, bf16[4,2,4,16,128]{4,3,2,1,0:T(8,128)(2,1)S(1)}, u32[]{:S(2)}, u32[]{:S(2)}) collective-permute-start(bf16[4,2,4,16,128]{4,3,2,1,0:T(8,128)(2,1)} %get-tuple-element.21), channel_id=1, source_target_pairs={{0,1},{1,2},{2,3},{3,4},{4,5},{5,6},{6,7},{7,8},{8,9},{9,10},{10,1... | collective-permute-start | bytes 393224 | tf_op jit(solution)/shard_map/ppermute | solution.py:332
  41.1 1.3 %collective-permute-start.5 = (bf16[4,2,4,16,128]{4,3,2,1,0:T(8,128)(2,1)S(1)}, bf16[4,2,4,16,128]{4,3,2,1,0:T(8,128)(2,1)S(1)}, u32[]{:S(2)}, u32[]{:S(2)}) collective-permute-start(bf16[4,2,4,16,128]{4,3,2,1,0:T(8,128)(2,1)S(1)} %get-tuple-element.22), channel_id=1, source_target_pairs={{1,0},{2,1},{3,2},{4,3},{5,4},{6,5},{7,6},{8,7},{9,8},{10,9},{11,1... | collective-permute-start | bytes 393224 | tf_op jit(solution)/shard_map/ppermute | solution.py:333
  42.4 2.1 %all-to-all-done.arrived = bf16[64,2,3712]{2,1,0:T(2,128)(2,1)S(1)} async-done(((bf16[64,2,3712]{2,1,0:T(2,128)(2,1)}), bf16[64,2,3712]{2,1,0:T(2,128)(2,1)S(1)}, u32[]{:S(2)}, u32[]{:S(2)}) %all-to-all-start) | async-done | bytes 950304 | tf_op jit(solution)/shard_map/all_to_all | solution.py:299
  44.4 0.7 sums.1
  45.2 8.2 %all-to-all-start.1 = ((f32[8,1,128]{2,1,0:T(1,128)}), f32[8,1,128]{2,1,0:T(1,128)S(1)}, u32[]{:S(2)}, u32[]{:S(2)}) async-start(f32[8,1,128]{2,1,0:T(1,128)} %sums.1), calls=%async_computation.1 | async-start | bytes 8192 | tf_op jit(solution)/shard_map/all_to_all | solution.py:344
  53.4 0.1 copy.12
  53.5 1.9 %collective-permute-start.6 = (bf16[2,64,3712]{2,1,0:T(8,128)(2,1)S(1)}, bf16[2,64,3712]{2,1,0:T(8,128)(2,1)S(1)}, u32[]{:S(2)}, u32[]{:S(2)}) collective-permute-start(bf16[2,64,3712]{2,1,0:T(8,128)(2,1)S(1)} %bitcast.23), channel_id=1, source_target_pairs={{0,64},{64,0},{1,65},{65,1},{2,66},{66,2},{3,67},{67,3},{4,68},{68... | collective-permute-start | bytes 2850824 | tf_op jit(solution)/shard_map/ppermute | solution.py:346
  55.4 0.0 collective-permute-done.4.above
  55.4 0.0 collective-permute-done.5.below
  55.4 2.5 %all-to-all-done.1 = f32[8,1,128]{2,1,0:T(1,128)S(1)} async-done(((f32[8,1,128]{2,1,0:T(1,128)}), f32[8,1,128]{2,1,0:T(1,128)S(1)}, u32[]{:S(2)}, u32[]{:S(2)}) %all-to-all-start.1) | async-done | bytes 4128 | tf_op jit(solution)/shard_map/all_to_all | solution.py:344
  57.9 0.8 %norm.1 = (bf16[3,34,16,512]{3,2,1,0:T(8,128)(2,1)S(1)}, bf16[32,16,256]{2,1,0:T(8,128)(2,1)S(1)}, f32[2,256]{1,0:T(2,128)S(1)}) custom-call(f32[8,128]{1,0:T(8,128)S(1)} %bitcast.26, f32[8,128]{1,0:T(8,128)S(1)} %get-tuple-element.17.counts, f32[2,128]{1,0:T(2,128)S(1)} %get-tuple-element.24.lanes, ...), custom_call_target="tpu_custom_call" | custom-call | flops 17179869184 | bytes 67108864 | tf_op jit(solution)/shard_map/norm/pallas_call | solution.py:348
  58.7 0.0 collective-permute-done.6.theirs
  58.7 2.1 %taps.1 = f32[8,4,32,256]{3,2,1,0:T(8,128)S(1)} custom-call(bf16[3,34,16,512]{3,2,1,0:T(8,128)(2,1)S(1)} %get-tuple-element.26.shifted, bf16[32,16,256]{2,1,0:T(8,128)(2,1)S(1)} %get-tuple-element.27.raw, bf16[2,64,3712]{2,1,0:T(8,128)(2,1)S(1)} %bitcast.24, bf16[2,64,3712]{2,1,0:T(8,128)(2,1)S(1)} %collective-permute-done.6.theirs, ...), custom_call_target="tpu_custom_call" | custom-call | flops 1879048192 | bytes 6291456 | tf_op jit(solution)/shard_map/taps/pallas_call | solution.py:368
  60.8 0.0 copy-start.3
  60.8 0.9 %convert_element_type.7 = f16[8,4,32,256]{3,2,1,0:T(8,128)(2,1)} convert(f32[8,4,32,256]{3,2,1,0:T(8,128)S(1)} %taps.1) | non-fusion elementwise | flops 262144 | bytes 1572864 | tf_op jit(solution)/shard_map/convert_element_type | solution.py:381
  61.7 4.1 %all-to-all-start.2 = ((f16[8,4,32,256]{3,2,1,0:T(8,128)(2,1)}), f16[8,4,32,256]{3,2,1,0:T(8,128)(2,1)S(1)}, u32[]{:S(2)}, u32[]{:S(2)}) async-start(f16[8,4,32,256]{3,2,1,0:T(8,128)(2,1)} %convert_element_type.7), calls=%async_computation.2 | async-start | bytes 1048576 | tf_op jit(solution)/shard_map/all_to_all | solution.py:382
  65.8 0.1 broadcast_compare_fusion
  65.9 9.4 %all-to-all-done.2 = f16[8,4,32,256]{3,2,1,0:T(8,128)(2,1)S(1)} async-done(((f16[8,4,32,256]{3,2,1,0:T(8,128)(2,1)}), f16[8,4,32,256]{3,2,1,0:T(8,128)(2,1)S(1)}, u32[]{:S(2)}, u32[]{:S(2)}) %all-to-all-start.2) | async-done | bytes 524320 | tf_op jit(solution)/shard_map/all_to_all | solution.py:382
  75.3 0.1 convert_reduce_fusion
  75.4 0.7 select_convert_fusion
  (9 shorter events, 0.0 us)
Async XLA Ops:
  0.0 19.7 %copy-start = (bf16[2,4,2,16,512]{4,3,2,1,0:T(8,128)(2,1)S(1)}, bf16[2,4,2,16,512]{4,3,2,1,0:T(8,128)(2,1)}, u32[]{:S(2)}) copy-start(bf16[2,4,2,16,512]{4,3,2,1,0:T(8,128)(2,1)} %param.6) | copy-start | bytes 786436
  0.0 19.7 %copy-start.2 = (f32[512]{0:T(512)S(1)}, f32[512]{0:T(512)}, u32[]{:S(2)}) copy-start(f32[512]{0:T(512)} %param.9) | copy-start | bytes 6148
  0.0 19.8 %copy-start.1 = (f32[512]{0:T(512)S(1)}, f32[512]{0:T(512)}, u32[]{:S(2)}) copy-start(f32[512]{0:T(512)} %param.8) | copy-start | bytes 6148
  2.6 41.8 %all-to-all-start = ((bf16[64,2,3712]{2,1,0:T(2,128)(2,1)}), bf16[64,2,3712]{2,1,0:T(2,128)(2,1)S(1)}, u32[]{:S(2)}, u32[]{:S(2)}) async-start(bf16[64,2,3712]{2,1,0:T(2,128)(2,1)} %get-tuple-element.18), calls=%async_computation | async-start | bytes 1900544 | tf_op jit(solution)/shard_map/all_to_all | solution.py:299
  20.2 3.8 %collective-permute-start = (bf16[4,4,16,256]{3,2,1,0:T(8,128)(2,1)S(1)}, bf16[4,4,16,256]{3,2,1,0:T(8,128)(2,1)S(1)}, u32[]{:S(2)}, u32[]{:S(2)}) collective-permute-start(bf16[4,4,16,256]{3,2,1,0:T(8,128)(2,1)S(1)} %get-tuple-element.20), channel_id=1, source_target_pairs={{0,64},{64,0},{1,65},{65,1},{2,66},{66,2},{3,67},{67,3},{4,68},{68... | collective-permute-start | bytes 393224 | tf_op jit(solution)/shard_map/ppermute | solution.py:315
  24.0 10.0 %collective-permute-start.3 = (bf16[2,4,16,256]{3,2,1,0:T(8,128)(2,1)S(1)}, bf16[2,4,16,256]{3,2,1,0:T(8,128)(2,1)S(1)}, u32[]{:S(2)}, u32[]{:S(2)}) collective-permute-start(bf16[2,4,16,256]{3,2,1,0:T(8,128)(2,1)S(1)} %get-tuple-element.29), channel_id=1, source_target_pairs={{0,384},{128,0},{256,128},{384,256},{1,385},{129,1},{257,129},{385... | collective-permute-start | bytes 196616 | tf_op jit(solution)/shard_map/ppermute | solution.py:320
  28.4 6.5 %collective-permute-start.1 = (bf16[2,4,16,256]{3,2,1,0:T(8,128)(2,1)S(1)}, bf16[2,4,16,256]{3,2,1,0:T(8,128)(2,1)S(1)}, u32[]{:S(2)}, u32[]{:S(2)}) collective-permute-start(bf16[2,4,16,256]{3,2,1,0:T(8,128)(2,1)S(1)} %get-tuple-element.31), channel_id=1, source_target_pairs={{0,128},{128,256},{256,384},{384,0},{1,129},{129,257},{257,385},{3... | collective-permute-start | bytes 196616 | tf_op jit(solution)/shard_map/ppermute | solution.py:320
  30.3 6.8 %collective-permute-start.2 = (bf16[2,4,16,256]{3,2,1,0:T(8,128)(2,1)S(1)}, bf16[2,4,16,256]{3,2,1,0:T(8,128)(2,1)S(1)}, u32[]{:S(2)}, u32[]{:S(2)}) collective-permute-start(bf16[2,4,16,256]{3,2,1,0:T(8,128)(2,1)S(1)} %get-tuple-element.32), channel_id=1, source_target_pairs={{0,256},{128,384},{256,0},{384,128},{1,257},{129,385},{257,1},{385... | collective-permute-start | bytes 196616 | tf_op jit(solution)/shard_map/ppermute | solution.py:320
  37.9 17.5 %collective-permute-start.4 = (bf16[4,2,4,16,128]{4,3,2,1,0:T(8,128)(2,1)}, bf16[4,2,4,16,128]{4,3,2,1,0:T(8,128)(2,1)S(1)}, u32[]{:S(2)}, u32[]{:S(2)}) collective-permute-start(bf16[4,2,4,16,128]{4,3,2,1,0:T(8,128)(2,1)} %get-tuple-element.21), channel_id=1, source_target_pairs={{0,1},{1,2},{2,3},{3,4},{4,5},{5,6},{6,7},{7,8},{8,9},{9,10},{10,1... | collective-permute-start | bytes 393224 | tf_op jit(solution)/shard_map/ppermute | solution.py:332
  41.1 14.3 %collective-permute-start.5 = (bf16[4,2,4,16,128]{4,3,2,1,0:T(8,128)(2,1)S(1)}, bf16[4,2,4,16,128]{4,3,2,1,0:T(8,128)(2,1)S(1)}, u32[]{:S(2)}, u32[]{:S(2)}) collective-permute-start(bf16[4,2,4,16,128]{4,3,2,1,0:T(8,128)(2,1)S(1)} %get-tuple-element.22), channel_id=1, source_target_pairs={{1,0},{2,1},{3,2},{4,3},{5,4},{6,5},{7,6},{8,7},{9,8},{10,9},{11,1... | collective-permute-start | bytes 393224 | tf_op jit(solution)/shard_map/ppermute | solution.py:333
  45.2 12.8 %all-to-all-start.1 = ((f32[8,1,128]{2,1,0:T(1,128)}), f32[8,1,128]{2,1,0:T(1,128)S(1)}, u32[]{:S(2)}, u32[]{:S(2)}) async-start(f32[8,1,128]{2,1,0:T(1,128)} %sums.1), calls=%async_computation.1 | async-start | bytes 8192 | tf_op jit(solution)/shard_map/all_to_all | solution.py:344
  53.5 5.2 %collective-permute-start.6 = (bf16[2,64,3712]{2,1,0:T(8,128)(2,1)S(1)}, bf16[2,64,3712]{2,1,0:T(8,128)(2,1)S(1)}, u32[]{:S(2)}, u32[]{:S(2)}) collective-permute-start(bf16[2,64,3712]{2,1,0:T(8,128)(2,1)S(1)} %bitcast.23), channel_id=1, source_target_pairs={{0,64},{64,0},{1,65},{65,1},{2,66},{66,2},{3,67},{67,3},{4,68},{68... | collective-permute-start | bytes 2850824 | tf_op jit(solution)/shard_map/ppermute | solution.py:346
  60.8 5.0 %copy-start.3 = (s32[2]{0:T(128)S(1)}, s32[2]{0:T(128)}, u32[]{:S(2)}) copy-start(s32[2]{0:T(128)} %lengths.1) | copy-start | bytes 28
  61.7 13.6 %all-to-all-start.2 = ((f16[8,4,32,256]{3,2,1,0:T(8,128)(2,1)}), f16[8,4,32,256]{3,2,1,0:T(8,128)(2,1)S(1)}, u32[]{:S(2)}, u32[]{:S(2)}) async-start(f16[8,4,32,256]{3,2,1,0:T(8,128)(2,1)} %convert_element_type.7), calls=%async_computation.2 | async-start | bytes 1048576 | tf_op jit(solution)/shard_map/all_to_all | solution.py:382

commit v10 on v9

--- a/solution.py
+++ b/solution.py
@@ -151,15 +151,6 @@
     match = lax.broadcasted_iota(jnp.int32, (channels, PART), 0) == source
     pair = jnp.concatenate([gain[...], bias[...]], axis=0)
     lanes[...] = exact_dot(pair, jnp.where(match, 1.0, 0.0).astype(jnp.bfloat16))
-
-
-def edges_kernel(*refs):
-    signal, upper, lower = refs[-3:]
-    for step, block in enumerate(refs[:-3]):
-        value = block[...]
-        signal[step] = value
-        upper[step] = value[..., PART:]
-        lower[step] = value[..., :PART]
 
 
 def norm_kernel(
@@ -319,16 +310,8 @@
         if step:
             block = lax.ppermute(block, "x", [(i, (i + step) % chips) for i in range(chips)])
         signal.append(block)
-    whole = (chips,) + signal[0].shape
-    edge = whole[:-1] + (PART,)
-    signal, upper, lower = pl.pallas_call(
-        edges_kernel,
-        out_shape=tuple(pltpu.VMEM(shape, jnp.bfloat16) for shape in (whole, edge, edge)),
-        in_specs=[on_chip] * chips,
-        out_specs=(on_chip, on_chip, on_chip),
-        compiler_params=params,
-        name="edges",
-    )(*signal)
+    signal = jnp.stack(signal)
+    upper, lower = signal[..., PART:], signal[..., :PART]
     above = lax.ppermute(upper, TILE, [(i, i + 1) for i in range(tiles - 1)])
     below = lax.ppermute(lower, TILE, [(i + 1, i) for i in range(tiles - 1)])
 

time: 76.7 us -> 76.7 us (level)
  waiting for transfers between devices: 18.1 us -> 16.7 us
  starting transfers between devices: 48.6 us -> 50 us
    ppermute x3, waiting for transfers between devices: 3.16 us -> 2.22 us  [per_device(): lax.ppermute(block, 'x', [(i, (i + step) % chips) for i in range(chips)])]
    ppermute x1, starting transfers between devices: 3.19 us -> 3.99 us  [per_device(): above = lax.ppermute(upper, TILE, [(i, i + 1) for i in range(tiles - 1)])]
  transfers between devices with their start and end apart: 10 -> 10, of which waited for: 6 -> 5; matrix products, arithmetic and copies ran while one was open for 0% -> 1% of each run, Pallas kernels for 3% -> 2%
where the time goes in v10:
time: 76.7 us; the launch traced here: 76.2 us
  starting transfers between devices  50 us (65%)
  waiting for transfers between devices  16.7 us (22%)
  Pallas kernels  6.57 us (9%)
  other arithmetic  1.9 us (2%)
  local copies, waits for them, and re-layouts  0.82 us (1%)
    all_to_all x1, starting transfers between devices, per_device(): arrived = lax.all_to_all(copies, TILE, 0, 0, tiled=True)  17.1 us
    ppermute x3, starting transfers between devices, per_device(): lax.ppermute(block, 'x', [(i, (i + step) % chips) for i in range(chips)])  10.5 us
    all_to_all x1, waiting for transfers between devices, per_device(): total = lax.all_to_all(total, TM, 0, 0, tiled=True).astype(jnp.float32)  9.42 us
    all_to_all x1, starting transfers between devices, per_device(): totals = lax.all_to_all(copies, TM, 0, 0, tiled=True).reshape(SPANS, -1)  8.21 us
    all_to_all x1, starting transfers between devices, per_device(): total = lax.all_to_all(total, TM, 0, 0, tiled=True).astype(jnp.float32)  4.06 us
    ppermute x1, starting transfers between devices, per_device(): above = lax.ppermute(upper, TILE, [(i, i + 1) for i in range(tiles - 1)])  3.99 us
    ppermute x1, starting transfers between devices, per_device(): shares = jnp.stack([kept, lax.ppermute(sent, 'core', swap)], axis=1)  2.86 us
    pallas_call x1, Pallas kernels, per_device(): pl.pallas_call(payload_kernel, out_shape=(jax.ShapeDtypeStruct((tiles, 2,...  2.56 us
  transfers between devices with their start and end apart: 10, of which 5 were waited for; matrix products, arithmetic and copies ran while one was open for 1% of the time, Pallas kernels for 2%

profile of v10, /device:TPU:1, one launch (start us, length us, event | category | flops | bytes accessed | tf_op | source)
XLA Modules:
  0.0 76.2 jit_solution(4841690777892521374)
XLA Ops:
  0.0 2.6 %payload.1 = (bf16[64,2,3712]{2,1,0:T(2,128)(2,1)}, f32[8,128]{1,0:T(8,128)S(1)}) custom-call(bf16[8,32,512]{2,1,0:T(8,128)(2,1)} %bitcast.22, bf16[27,8,256]{2,1,0:T(8,128)(2,1)} %bitcast.33, bf16[8,256]{1,0:T(8,128)(2,1)} %skip.1, s32[2]{0:T(128)} %lengths.1), custom_call_target="tpu_custom_call" | custom-call | tf_op jit(solution)/shard_map/payload/pallas_call | solution.py:263
  2.6 17.1 %all-to-all-start = ((bf16[64,2,3712]{2,1,0:T(2,128)(2,1)}), bf16[64,2,3712]{2,1,0:T(2,128)(2,1)S(1)}, u32[]{:S(2)}, u32[]{:S(2)}) async-start(bf16[64,2,3712]{2,1,0:T(2,128)(2,1)} %get-tuple-element.15), calls=%async_computation | async-start | bytes 1900544 | tf_op jit(solution)/shard_map/all_to_all | solution.py:290
  19.8 0.4 member_shares.1
  20.2 2.9 %collective-permute-start = (bf16[4,4,16,256]{3,2,1,0:T(8,128)(2,1)S(1)}, bf16[4,4,16,256]{3,2,1,0:T(8,128)(2,1)S(1)}, u32[]{:S(2)}, u32[]{:S(2)}) collective-permute-start(bf16[4,4,16,256]{3,2,1,0:T(8,128)(2,1)S(1)} %get-tuple-element.17), channel_id=1, source_target_pairs={{0,64},{64,0},{1,65},{65,1},{2,66},{66,2},{3,67},{67,3},{4,68},{68... | collective-permute-start | bytes 393224 | tf_op jit(solution)/shard_map/ppermute | solution.py:306
  23.1 0.9 %collective-permute-done = bf16[4,4,16,256]{3,2,1,0:T(8,128)(2,1)S(1)} collective-permute-done((bf16[4,4,16,256]{3,2,1,0:T(8,128)(2,1)S(1)}, bf16[4,4,16,256]{3,2,1,0:T(8,128)(2,1)S(1)}, u32[]{:S(2)}, u32[]{:S(2)}) %collective-permute-start) | collective-permute-done | bytes 131104 | tf_op jit(solution)/shard_map/ppermute | solution.py:306
  24.0 3.1 %collective-permute-start.1 = (bf16[2,4,16,256]{3,2,1,0:T(8,128)(2,1)S(1)}, bf16[2,4,16,256]{3,2,1,0:T(8,128)(2,1)S(1)}, u32[]{:S(2)}, u32[]{:S(2)}) collective-permute-start(bf16[2,4,16,256]{3,2,1,0:T(8,128)(2,1)S(1)} %get-tuple-element.26), channel_id=1, source_target_pairs={{0,128},{128,256},{256,384},{384,0},{1,129},{129,257},{257,385},{3... | collective-permute-start | bytes 196616 | tf_op jit(solution)/shard_map/ppermute | solution.py:311
  27.1 4.4 %collective-permute-start.2 = (bf16[2,4,16,256]{3,2,1,0:T(8,128)(2,1)S(1)}, bf16[2,4,16,256]{3,2,1,0:T(8,128)(2,1)S(1)}, u32[]{:S(2)}, u32[]{:S(2)}) collective-permute-start(bf16[2,4,16,256]{3,2,1,0:T(8,128)(2,1)S(1)} %get-tuple-element.27), channel_id=1, source_target_pairs={{0,256},{128,384},{256,0},{384,128},{1,257},{129,385},{257,1},{385... | collective-permute-start | bytes 196616 | tf_op jit(solution)/shard_map/ppermute | solution.py:311
  31.5 3.1 %collective-permute-start.3 = (bf16[2,4,16,256]{3,2,1,0:T(8,128)(2,1)S(1)}, bf16[2,4,16,256]{3,2,1,0:T(8,128)(2,1)S(1)}, u32[]{:S(2)}, u32[]{:S(2)}) collective-permute-start(bf16[2,4,16,256]{3,2,1,0:T(8,128)(2,1)S(1)} %get-tuple-element.28), channel_id=1, source_target_pairs={{0,384},{128,0},{256,128},{384,256},{1,385},{129,1},{257,129},{385... | collective-permute-start | bytes 196616 | tf_op jit(solution)/shard_map/ppermute | solution.py:311
  34.6 0.0 collective-permute-done.1
  34.6 0.0 collective-permute-done.2
  34.6 2.2 %collective-permute-done.3 = bf16[2,4,16,256]{3,2,1,0:T(8,128)(2,1)S(1)} collective-permute-done((bf16[2,4,16,256]{3,2,1,0:T(8,128)(2,1)S(1)}, bf16[2,4,16,256]{3,2,1,0:T(8,128)(2,1)S(1)}, u32[]{:S(2)}, u32[]{:S(2)}) %collective-permute-start.3) | collective-permute-done | bytes 65568 | tf_op jit(solution)/shard_map/ppermute | solution.py:311
  36.9 0.7 fusion.7
  37.6 1.3 %collective-permute-start.5 = (bf16[4,2,4,16,128]{4,3,2,1,0:T(8,128)(2,1)}, bf16[4,2,4,16,128]{4,3,2,1,0:T(8,128)(2,1)S(1)}, u32[]{:S(2)}, u32[]{:S(2)}) collective-permute-start(bf16[4,2,4,16,128]{4,3,2,1,0:T(8,128)(2,1)} %get-tuple-element.23), channel_id=1, source_target_pairs={{1,0},{2,1},{3,2},{4,3},{5,4},{6,5},{7,6},{8,7},{9,8},{10,9},{11,1... | collective-permute-start | bytes 393224 | tf_op jit(solution)/shard_map/ppermute | solution.py:316
  38.8 4.0 %collective-permute-start.4 = (bf16[4,2,4,16,128]{4,3,2,1,0:T(8,128)(2,1)S(1)}, bf16[4,2,4,16,128]{4,3,2,1,0:T(8,128)(2,1)S(1)}, u32[]{:S(2)}, u32[]{:S(2)}) collective-permute-start(bf16[4,2,4,16,128]{4,3,2,1,0:T(8,128)(2,1)S(1)} %get-tuple-element.24), channel_id=1, source_target_pairs={{0,1},{1,2},{2,3},{3,4},{4,5},{5,6},{6,7},{7,8},{8,9},{9,10},{10,1... | collective-permute-start | bytes 393224 | tf_op jit(solution)/shard_map/ppermute | solution.py:315
  42.8 1.6 %all-to-all-done.arrived = bf16[64,2,3712]{2,1,0:T(2,128)(2,1)S(1)} async-done(((bf16[64,2,3712]{2,1,0:T(2,128)(2,1)}), bf16[64,2,3712]{2,1,0:T(2,128)(2,1)S(1)}, u32[]{:S(2)}, u32[]{:S(2)}) %all-to-all-start) | async-done | bytes 950304 | tf_op jit(solution)/shard_map/all_to_all | solution.py:290
  44.4 0.7 sums.1
  45.2 8.2 %all-to-all-start.1 = ((f32[8,1,128]{2,1,0:T(1,128)}), f32[8,1,128]{2,1,0:T(1,128)S(1)}, u32[]{:S(2)}, u32[]{:S(2)}) async-start(f32[8,1,128]{2,1,0:T(1,128)} %sums.1), calls=%async_computation.1 | async-start | bytes 8192 | tf_op jit(solution)/shard_map/all_to_all | solution.py:327
  53.4 0.1 copy.12
  53.5 1.9 %collective-permute-start.6 = (bf16[2,64,3712]{2,1,0:T(8,128)(2,1)S(1)}, bf16[2,64,3712]{2,1,0:T(8,128)(2,1)S(1)}, u32[]{:S(2)}, u32[]{:S(2)}) collective-permute-start(bf16[2,64,3712]{2,1,0:T(8,128)(2,1)S(1)} %bitcast.24), channel_id=1, source_target_pairs={{0,64},{64,0},{1,65},{65,1},{2,66},{66,2},{3,67},{67,3},{4,68},{68... | collective-permute-start | bytes 2850824 | tf_op jit(solution)/shard_map/ppermute | solution.py:329
  55.4 0.0 collective-permute-done.5.below
  55.4 0.0 collective-permute-done.4.above
  55.4 2.5 %all-to-all-done.1 = f32[8,1,128]{2,1,0:T(1,128)S(1)} async-done(((f32[8,1,128]{2,1,0:T(1,128)}), f32[8,1,128]{2,1,0:T(1,128)S(1)}, u32[]{:S(2)}, u32[]{:S(2)}) %all-to-all-start.1) | async-done | bytes 4128 | tf_op jit(solution)/shard_map/all_to_all | solution.py:327
  57.9 0.8 %norm.1 = (bf16[3,34,16,512]{3,2,1,0:T(8,128)(2,1)S(1)}, bf16[32,16,256]{2,1,0:T(8,128)(2,1)S(1)}, f32[2,256]{1,0:T(2,128)S(1)}) custom-call(f32[8,128]{1,0:T(8,128)S(1)} %bitcast.27, f32[8,128]{1,0:T(8,128)S(1)} %get-tuple-element.14.counts, f32[2,128]{1,0:T(2,128)S(1)} %get-tuple-element.19.lanes, bf16[4,2,4,16,256]{4,3,2,1,0:T(8,128)(2,1)S(1)} %pad_maximum_fusion.signal, ...), custom_call_target="tpu_custom_call" | custom-call | flops 17179869184 | bytes 67108864 | tf_op jit(solution)/shard_map/norm/pallas_call | solution.py:331
  58.7 0.0 collective-permute-done.6.theirs
  58.7 2.1 %taps.1 = f32[8,4,32,256]{3,2,1,0:T(8,128)S(1)} custom-call(bf16[3,34,16,512]{3,2,1,0:T(8,128)(2,1)S(1)} %get-tuple-element.20.shifted, bf16[32,16,256]{2,1,0:T(8,128)(2,1)S(1)} %get-tuple-element.21.raw, bf16[2,64,3712]{2,1,0:T(8,128)(2,1)S(1)} %bitcast.25, bf16[2,64,3712]{2,1,0:T(8,128)(2,1)S(1)} %collective-permute-done.6.theirs, ...), custom_call_target="tpu_custom_call" | custom-call | flops 1879048192 | bytes 6291456 | tf_op jit(solution)/shard_map/taps/pallas_call | solution.py:351
  60.8 0.0 copy-start.3
  60.8 0.9 %convert_element_type.7 = f16[8,4,32,256]{3,2,1,0:T(8,128)(2,1)} convert(f32[8,4,32,256]{3,2,1,0:T(8,128)S(1)} %taps.1) | non-fusion elementwise | flops 262144 | bytes 1572864 | tf_op jit(solution)/shard_map/convert_element_type | solution.py:364
  61.8 4.1 %all-to-all-start.2 = ((f16[8,4,32,256]{3,2,1,0:T(8,128)(2,1)}), f16[8,4,32,256]{3,2,1,0:T(8,128)(2,1)S(1)}, u32[]{:S(2)}, u32[]{:S(2)}) async-start(f16[8,4,32,256]{3,2,1,0:T(8,128)(2,1)} %convert_element_type.7), calls=%async_computation.2 | async-start | bytes 1048576 | tf_op jit(solution)/shard_map/all_to_all | solution.py:365
  65.8 0.1 broadcast_compare_fusion
  65.9 9.4 %all-to-all-done.2 = f16[8,4,32,256]{3,2,1,0:T(8,128)(2,1)S(1)} async-done(((f16[8,4,32,256]{3,2,1,0:T(8,128)(2,1)}), f16[8,4,32,256]{3,2,1,0:T(8,128)(2,1)S(1)}, u32[]{:S(2)}, u32[]{:S(2)}) %all-to-all-start.2) | async-done | bytes 524320 | tf_op jit(solution)/shard_map/all_to_all | solution.py:365
  75.3 0.1 convert_reduce_fusion
  75.4 0.7 select_convert_fusion
  (10 shorter events, 0.1 us)
Async XLA Ops:
  0.0 19.7 %copy-start = (bf16[2,4,2,16,512]{4,3,2,1,0:T(8,128)(2,1)S(1)}, bf16[2,4,2,16,512]{4,3,2,1,0:T(8,128)(2,1)}, u32[]{:S(2)}) copy-start(bf16[2,4,2,16,512]{4,3,2,1,0:T(8,128)(2,1)} %param.6) | copy-start | bytes 786436
  0.0 19.7 %copy-start.2 = (f32[512]{0:T(512)S(1)}, f32[512]{0:T(512)}, u32[]{:S(2)}) copy-start(f32[512]{0:T(512)} %param.9) | copy-start | bytes 6148
  0.0 19.8 %copy-start.1 = (f32[512]{0:T(512)S(1)}, f32[512]{0:T(512)}, u32[]{:S(2)}) copy-start(f32[512]{0:T(512)} %param.8) | copy-start | bytes 6148
  2.6 41.8 %all-to-all-start = ((bf16[64,2,3712]{2,1,0:T(2,128)(2,1)}), bf16[64,2,3712]{2,1,0:T(2,128)(2,1)S(1)}, u32[]{:S(2)}, u32[]{:S(2)}) async-start(bf16[64,2,3712]{2,1,0:T(2,128)(2,1)} %get-tuple-element.15), calls=%async_computation | async-start | bytes 1900544 | tf_op jit(solution)/shard_map/all_to_all | solution.py:290
  20.2 3.8 %collective-permute-start = (bf16[4,4,16,256]{3,2,1,0:T(8,128)(2,1)S(1)}, bf16[4,4,16,256]{3,2,1,0:T(8,128)(2,1)S(1)}, u32[]{:S(2)}, u32[]{:S(2)}) collective-permute-start(bf16[4,4,16,256]{3,2,1,0:T(8,128)(2,1)S(1)} %get-tuple-element.17), channel_id=1, source_target_pairs={{0,64},{64,0},{1,65},{65,1},{2,66},{66,2},{3,67},{67,3},{4,68},{68... | collective-permute-start | bytes 393224 | tf_op jit(solution)/shard_map/ppermute | solution.py:306
  24.0 10.6 %collective-permute-start.1 = (bf16[2,4,16,256]{3,2,1,0:T(8,128)(2,1)S(1)}, bf16[2,4,16,256]{3,2,1,0:T(8,128)(2,1)S(1)}, u32[]{:S(2)}, u32[]{:S(2)}) collective-permute-start(bf16[2,4,16,256]{3,2,1,0:T(8,128)(2,1)S(1)} %get-tuple-element.26), channel_id=1, source_target_pairs={{0,128},{128,256},{256,384},{384,0},{1,129},{129,257},{257,385},{3... | collective-permute-start | bytes 196616 | tf_op jit(solution)/shard_map/ppermute | solution.py:311
  27.1 7.4 %collective-permute-start.2 = (bf16[2,4,16,256]{3,2,1,0:T(8,128)(2,1)S(1)}, bf16[2,4,16,256]{3,2,1,0:T(8,128)(2,1)S(1)}, u32[]{:S(2)}, u32[]{:S(2)}) collective-permute-start(bf16[2,4,16,256]{3,2,1,0:T(8,128)(2,1)S(1)} %get-tuple-element.27), channel_id=1, source_target_pairs={{0,256},{128,384},{256,0},{384,128},{1,257},{129,385},{257,1},{385... | collective-permute-start | bytes 196616 | tf_op jit(solution)/shard_map/ppermute | solution.py:311
  31.5 5.3 %collective-permute-start.3 = (bf16[2,4,16,256]{3,2,1,0:T(8,128)(2,1)S(1)}, bf16[2,4,16,256]{3,2,1,0:T(8,128)(2,1)S(1)}, u32[]{:S(2)}, u32[]{:S(2)}) collective-permute-start(bf16[2,4,16,256]{3,2,1,0:T(8,128)(2,1)S(1)} %get-tuple-element.28), channel_id=1, source_target_pairs={{0,384},{128,0},{256,128},{384,256},{1,385},{129,1},{257,129},{385... | collective-permute-start | bytes 196616 | tf_op jit(solution)/shard_map/ppermute | solution.py:311
  37.6 17.8 %collective-permute-start.5 = (bf16[4,2,4,16,128]{4,3,2,1,0:T(8,128)(2,1)}, bf16[4,2,4,16,128]{4,3,2,1,0:T(8,128)(2,1)S(1)}, u32[]{:S(2)}, u32[]{:S(2)}) collective-permute-start(bf16[4,2,4,16,128]{4,3,2,1,0:T(8,128)(2,1)} %get-tuple-element.23), channel_id=1, source_target_pairs={{1,0},{2,1},{3,2},{4,3},{5,4},{6,5},{7,6},{8,7},{9,8},{10,9},{11,1... | collective-permute-start | bytes 393224 | tf_op jit(solution)/shard_map/ppermute | solution.py:316
  38.8 16.6 %collective-permute-start.4 = (bf16[4,2,4,16,128]{4,3,2,1,0:T(8,128)(2,1)S(1)}, bf16[4,2,4,16,128]{4,3,2,1,0:T(8,128)(2,1)S(1)}, u32[]{:S(2)}, u32[]{:S(2)}) collective-permute-start(bf16[4,2,4,16,128]{4,3,2,1,0:T(8,128)(2,1)S(1)} %get-tuple-element.24), channel_id=1, source_target_pairs={{0,1},{1,2},{2,3},{3,4},{4,5},{5,6},{6,7},{7,8},{8,9},{9,10},{10,1... | collective-permute-start | bytes 393224 | tf_op jit(solution)/shard_map/ppermute | solution.py:315
  45.2 12.8 %all-to-all-start.1 = ((f32[8,1,128]{2,1,0:T(1,128)}), f32[8,1,128]{2,1,0:T(1,128)S(1)}, u32[]{:S(2)}, u32[]{:S(2)}) async-start(f32[8,1,128]{2,1,0:T(1,128)} %sums.1), calls=%async_computation.1 | async-start | bytes 8192 | tf_op jit(solution)/shard_map/all_to_all | solution.py:327
  53.5 5.2 %collective-permute-start.6 = (bf16[2,64,3712]{2,1,0:T(8,128)(2,1)S(1)}, bf16[2,64,3712]{2,1,0:T(8,128)(2,1)S(1)}, u32[]{:S(2)}, u32[]{:S(2)}) collective-permute-start(bf16[2,64,3712]{2,1,0:T(8,128)(2,1)S(1)} %bitcast.24), channel_id=1, source_target_pairs={{0,64},{64,0},{1,65},{65,1},{2,66},{66,2},{3,67},{67,3},{4,68},{68... | collective-permute-start | bytes 2850824 | tf_op jit(solution)/shard_map/ppermute | solution.py:329
  60.8 5.0 %copy-start.3 = (s32[2]{0:T(128)S(1)}, s32[2]{0:T(128)}, u32[]{:S(2)}) copy-start(s32[2]{0:T(128)} %lengths.1) | copy-start | bytes 28
  61.8 13.6 %all-to-all-start.2 = ((f16[8,4,32,256]{3,2,1,0:T(8,128)(2,1)}), f16[8,4,32,256]{3,2,1,0:T(8,128)(2,1)S(1)}, u32[]{:S(2)}, u32[]{:S(2)}) async-start(f16[8,4,32,256]{3,2,1,0:T(8,128)(2,1)} %convert_element_type.7), calls=%async_computation.2 | async-start | bytes 1048576 | tf_op jit(solution)/shard_map/all_to_all | solution.py:365

commit v11 on v10

--- a/solution.py
+++ b/solution.py
@@ -25,12 +25,6 @@
 WIDTH = LINE * OUT + 128
 
 
-def to_all(block, axis):
-    count = lax.axis_size(axis)
-    copies = jnp.broadcast_to(block[None], (count,) + block.shape)
-    return lax.all_to_all(copies, axis, 0, 0, tiled=True)
-
-
 def exact_dot(value, chosen):
     high = value.astype(jnp.bfloat16)
     rest = value - high.astype(jnp.float32)
@@ -52,7 +46,7 @@
     axis = value.ndim - 1
     turned = pltpu.roll(value, 2 * GROUPS, axis)
     upper = lax.broadcasted_iota(jnp.int32, (1,) * axis + (128,), axis) >= 2 * GROUPS
-    return jnp.where(upper, turned * turned * inverse, 0.0)
+    return jnp.where(upper, turned * (turned * inverse), 0.0)
 
 
 def payload_kernel(features, conv, skip, lengths, copies, counts, planes, taps, skips, valid, rows, packed, few, done, left):

time: 76.7 us -> 76.7 us (level)
  no operation moved by 1% of the time
where the time goes in v11:
time: 76.7 us; the launch traced here: 76.2 us
  starting transfers between devices  50 us (65%)
  waiting for transfers between devices  16.7 us (22%)
  Pallas kernels  6.57 us (9%)
  other arithmetic  1.9 us (2%)
  local copies, waits for them, and re-layouts  0.82 us (1%)
    all_to_all x1, starting transfers between devices, per_device(): arrived = lax.all_to_all(copies, TILE, 0, 0, tiled=True)  17.1 us
    ppermute x3, starting transfers between devices, per_device(): lax.ppermute(block, 'x', [(i, (i + step) % chips) for i in range(chips)])  10.5 us
    all_to_all x1, waiting for transfers between devices, per_device(): total = lax.all_to_all(total, TM, 0, 0, tiled=True).astype(jnp.float32)  9.42 us
    all_to_all x1, starting transfers between devices, per_device(): totals = lax.all_to_all(copies, TM, 0, 0, tiled=True).reshape(SPANS, -1)  8.21 us
    all_to_all x1, starting transfers between devices, per_device(): total = lax.all_to_all(total, TM, 0, 0, tiled=True).astype(jnp.float32)  4.06 us
    ppermute x1, starting transfers between devices, per_device(): above = lax.ppermute(upper, TILE, [(i, i + 1) for i in range(tiles - 1)])  3.99 us
    ppermute x1, starting transfers between devices, per_device(): shares = jnp.stack([kept, lax.ppermute(sent, 'core', swap)], axis=1)  2.86 us
    pallas_call x1, Pallas kernels, per_device(): pl.pallas_call(payload_kernel, out_shape=(jax.ShapeDtypeStruct((tiles, 2,...  2.56 us
  transfers between devices with their start and end apart: 10, of which 5 were waited for; matrix products, arithmetic and copies ran while one was open for 1% of the time, Pallas kernels for 2%

profile of v11, /device:TPU:1, one launch (start us, length us, event | category | flops | bytes accessed | tf_op | source)
XLA Modules:
  0.0 76.2 jit_solution(5320689000663318533)
XLA Ops:
  0.0 2.6 %payload.1 = (bf16[64,2,3712]{2,1,0:T(2,128)(2,1)}, f32[8,128]{1,0:T(8,128)S(1)}) custom-call(bf16[8,32,512]{2,1,0:T(8,128)(2,1)} %bitcast.22, bf16[27,8,256]{2,1,0:T(8,128)(2,1)} %bitcast.33, bf16[8,256]{1,0:T(8,128)(2,1)} %skip.1, s32[2]{0:T(128)} %lengths.1), custom_call_target="tpu_custom_call" | custom-call | tf_op jit(solution)/shard_map/payload/pallas_call | solution.py:257
  2.6 17.1 %all-to-all-start = ((bf16[64,2,3712]{2,1,0:T(2,128)(2,1)}), bf16[64,2,3712]{2,1,0:T(2,128)(2,1)S(1)}, u32[]{:S(2)}, u32[]{:S(2)}) async-start(bf16[64,2,3712]{2,1,0:T(2,128)(2,1)} %get-tuple-element.15), calls=%async_computation | async-start | bytes 1900544 | tf_op jit(solution)/shard_map/all_to_all | solution.py:284
  19.8 0.4 member_shares.1
  20.2 2.9 %collective-permute-start = (bf16[4,4,16,256]{3,2,1,0:T(8,128)(2,1)S(1)}, bf16[4,4,16,256]{3,2,1,0:T(8,128)(2,1)S(1)}, u32[]{:S(2)}, u32[]{:S(2)}) collective-permute-start(bf16[4,4,16,256]{3,2,1,0:T(8,128)(2,1)S(1)} %get-tuple-element.17), channel_id=1, source_target_pairs={{0,64},{64,0},{1,65},{65,1},{2,66},{66,2},{3,67},{67,3},{4,68},{68... | collective-permute-start | bytes 393224 | tf_op jit(solution)/shard_map/ppermute | solution.py:300
  23.1 0.9 %collective-permute-done = bf16[4,4,16,256]{3,2,1,0:T(8,128)(2,1)S(1)} collective-permute-done((bf16[4,4,16,256]{3,2,1,0:T(8,128)(2,1)S(1)}, bf16[4,4,16,256]{3,2,1,0:T(8,128)(2,1)S(1)}, u32[]{:S(2)}, u32[]{:S(2)}) %collective-permute-start) | collective-permute-done | bytes 131104 | tf_op jit(solution)/shard_map/ppermute | solution.py:300
  24.0 3.1 %collective-permute-start.1 = (bf16[2,4,16,256]{3,2,1,0:T(8,128)(2,1)S(1)}, bf16[2,4,16,256]{3,2,1,0:T(8,128)(2,1)S(1)}, u32[]{:S(2)}, u32[]{:S(2)}) collective-permute-start(bf16[2,4,16,256]{3,2,1,0:T(8,128)(2,1)S(1)} %get-tuple-element.26), channel_id=1, source_target_pairs={{0,128},{128,256},{256,384},{384,0},{1,129},{129,257},{257,385},{3... | collective-permute-start | bytes 196616 | tf_op jit(solution)/shard_map/ppermute | solution.py:305
  27.1 4.4 %collective-permute-start.2 = (bf16[2,4,16,256]{3,2,1,0:T(8,128)(2,1)S(1)}, bf16[2,4,16,256]{3,2,1,0:T(8,128)(2,1)S(1)}, u32[]{:S(2)}, u32[]{:S(2)}) collective-permute-start(bf16[2,4,16,256]{3,2,1,0:T(8,128)(2,1)S(1)} %get-tuple-element.27), channel_id=1, source_target_pairs={{0,256},{128,384},{256,0},{384,128},{1,257},{129,385},{257,1},{385... | collective-permute-start | bytes 196616 | tf_op jit(solution)/shard_map/ppermute | solution.py:305
  31.5 3.1 %collective-permute-start.3 = (bf16[2,4,16,256]{3,2,1,0:T(8,128)(2,1)S(1)}, bf16[2,4,16,256]{3,2,1,0:T(8,128)(2,1)S(1)}, u32[]{:S(2)}, u32[]{:S(2)}) collective-permute-start(bf16[2,4,16,256]{3,2,1,0:T(8,128)(2,1)S(1)} %get-tuple-element.28), channel_id=1, source_target_pairs={{0,384},{128,0},{256,128},{384,256},{1,385},{129,1},{257,129},{385... | collective-permute-start | bytes 196616 | tf_op jit(solution)/shard_map/ppermute | solution.py:305
  34.6 0.0 collective-permute-done.1
  34.6 0.0 collective-permute-done.2
  34.6 2.2 %collective-permute-done.3 = bf16[2,4,16,256]{3,2,1,0:T(8,128)(2,1)S(1)} collective-permute-done((bf16[2,4,16,256]{3,2,1,0:T(8,128)(2,1)S(1)}, bf16[2,4,16,256]{3,2,1,0:T(8,128)(2,1)S(1)}, u32[]{:S(2)}, u32[]{:S(2)}) %collective-permute-start.3) | collective-permute-done | bytes 65568 | tf_op jit(solution)/shard_map/ppermute | solution.py:305
  36.9 0.7 fusion.7
  37.6 1.3 %collective-permute-start.5 = (bf16[4,2,4,16,128]{4,3,2,1,0:T(8,128)(2,1)}, bf16[4,2,4,16,128]{4,3,2,1,0:T(8,128)(2,1)S(1)}, u32[]{:S(2)}, u32[]{:S(2)}) collective-permute-start(bf16[4,2,4,16,128]{4,3,2,1,0:T(8,128)(2,1)} %get-tuple-element.23), channel_id=1, source_target_pairs={{1,0},{2,1},{3,2},{4,3},{5,4},{6,5},{7,6},{8,7},{9,8},{10,9},{11,1... | collective-permute-start | bytes 393224 | tf_op jit(solution)/shard_map/ppermute | solution.py:310
  38.8 4.0 %collective-permute-start.4 = (bf16[4,2,4,16,128]{4,3,2,1,0:T(8,128)(2,1)S(1)}, bf16[4,2,4,16,128]{4,3,2,1,0:T(8,128)(2,1)S(1)}, u32[]{:S(2)}, u32[]{:S(2)}) collective-permute-start(bf16[4,2,4,16,128]{4,3,2,1,0:T(8,128)(2,1)S(1)} %get-tuple-element.24), channel_id=1, source_target_pairs={{0,1},{1,2},{2,3},{3,4},{4,5},{5,6},{6,7},{7,8},{8,9},{9,10},{10,1... | collective-permute-start | bytes 393224 | tf_op jit(solution)/shard_map/ppermute | solution.py:309
  42.8 1.6 %all-to-all-done.arrived = bf16[64,2,3712]{2,1,0:T(2,128)(2,1)S(1)} async-done(((bf16[64,2,3712]{2,1,0:T(2,128)(2,1)}), bf16[64,2,3712]{2,1,0:T(2,128)(2,1)S(1)}, u32[]{:S(2)}, u32[]{:S(2)}) %all-to-all-start) | async-done | bytes 950304 | tf_op jit(solution)/shard_map/all_to_all | solution.py:284
  44.4 0.7 sums.1
  45.2 8.2 %all-to-all-start.1 = ((f32[8,1,128]{2,1,0:T(1,128)}), f32[8,1,128]{2,1,0:T(1,128)S(1)}, u32[]{:S(2)}, u32[]{:S(2)}) async-start(f32[8,1,128]{2,1,0:T(1,128)} %sums.1), calls=%async_computation.1 | async-start | bytes 8192 | tf_op jit(solution)/shard_map/all_to_all | solution.py:321
  53.4 0.1 copy.12
  53.5 1.9 %collective-permute-start.6 = (bf16[2,64,3712]{2,1,0:T(8,128)(2,1)S(1)}, bf16[2,64,3712]{2,1,0:T(8,128)(2,1)S(1)}, u32[]{:S(2)}, u32[]{:S(2)}) collective-permute-start(bf16[2,64,3712]{2,1,0:T(8,128)(2,1)S(1)} %bitcast.24), channel_id=1, source_target_pairs={{0,64},{64,0},{1,65},{65,1},{2,66},{66,2},{3,67},{67,3},{4,68},{68... | collective-permute-start | bytes 2850824 | tf_op jit(solution)/shard_map/ppermute | solution.py:323
  55.4 0.0 collective-permute-done.5.below
  55.4 0.0 collective-permute-done.4.above
  55.4 2.5 %all-to-all-done.1 = f32[8,1,128]{2,1,0:T(1,128)S(1)} async-done(((f32[8,1,128]{2,1,0:T(1,128)}), f32[8,1,128]{2,1,0:T(1,128)S(1)}, u32[]{:S(2)}, u32[]{:S(2)}) %all-to-all-start.1) | async-done | bytes 4128 | tf_op jit(solution)/shard_map/all_to_all | solution.py:321
  57.9 0.8 %norm.1 = (bf16[3,34,16,512]{3,2,1,0:T(8,128)(2,1)S(1)}, bf16[32,16,256]{2,1,0:T(8,128)(2,1)S(1)}, f32[2,256]{1,0:T(2,128)S(1)}) custom-call(f32[8,128]{1,0:T(8,128)S(1)} %bitcast.27, f32[8,128]{1,0:T(8,128)S(1)} %get-tuple-element.14.counts, f32[2,128]{1,0:T(2,128)S(1)} %get-tuple-element.19.lanes, bf16[4,2,4,16,256]{4,3,2,1,0:T(8,128)(2,1)S(1)} %pad_maximum_fusion.signal, ...), custom_call_target="tpu_custom_call" | custom-call | flops 17179869184 | bytes 67108864 | tf_op jit(solution)/shard_map/norm/pallas_call | solution.py:325
  58.7 0.0 collective-permute-done.6.theirs
  58.7 2.1 %taps.1 = f32[8,4,32,256]{3,2,1,0:T(8,128)S(1)} custom-call(bf16[3,34,16,512]{3,2,1,0:T(8,128)(2,1)S(1)} %get-tuple-element.20.shifted, bf16[32,16,256]{2,1,0:T(8,128)(2,1)S(1)} %get-tuple-element.21.raw, bf16[2,64,3712]{2,1,0:T(8,128)(2,1)S(1)} %bitcast.25, bf16[2,64,3712]{2,1,0:T(8,128)(2,1)S(1)} %collective-permute-done.6.theirs, ...), custom_call_target="tpu_custom_call" | custom-call | flops 1879048192 | bytes 6291456 | tf_op jit(solution)/shard_map/taps/pallas_call | solution.py:345
  60.8 0.0 copy-start.3
  60.8 0.9 %convert_element_type.7 = f16[8,4,32,256]{3,2,1,0:T(8,128)(2,1)} convert(f32[8,4,32,256]{3,2,1,0:T(8,128)S(1)} %taps.1) | non-fusion elementwise | flops 262144 | bytes 1572864 | tf_op jit(solution)/shard_map/convert_element_type | solution.py:358
  61.8 4.1 %all-to-all-start.2 = ((f16[8,4,32,256]{3,2,1,0:T(8,128)(2,1)}), f16[8,4,32,256]{3,2,1,0:T(8,128)(2,1)S(1)}, u32[]{:S(2)}, u32[]{:S(2)}) async-start(f16[8,4,32,256]{3,2,1,0:T(8,128)(2,1)} %convert_element_type.7), calls=%async_computation.2 | async-start | bytes 1048576 | tf_op jit(solution)/shard_map/all_to_all | solution.py:359
  65.8 0.1 broadcast_compare_fusion
  65.9 9.4 %all-to-all-done.2 = f16[8,4,32,256]{3,2,1,0:T(8,128)(2,1)S(1)} async-done(((f16[8,4,32,256]{3,2,1,0:T(8,128)(2,1)}), f16[8,4,32,256]{3,2,1,0:T(8,128)(2,1)S(1)}, u32[]{:S(2)}, u32[]{:S(2)}) %all-to-all-start.2) | async-done | bytes 524320 | tf_op jit(solution)/shard_map/all_to_all | solution.py:359
  75.3 0.1 convert_reduce_fusion
  75.4 0.7 select_convert_fusion
  (10 shorter events, 0.1 us)
Async XLA Ops:
  0.0 19.7 %copy-start = (bf16[2,4,2,16,512]{4,3,2,1,0:T(8,128)(2,1)S(1)}, bf16[2,4,2,16,512]{4,3,2,1,0:T(8,128)(2,1)}, u32[]{:S(2)}) copy-start(bf16[2,4,2,16,512]{4,3,2,1,0:T(8,128)(2,1)} %param.6) | copy-start | bytes 786436
  0.0 19.7 %copy-start.2 = (f32[512]{0:T(512)S(1)}, f32[512]{0:T(512)}, u32[]{:S(2)}) copy-start(f32[512]{0:T(512)} %param.9) | copy-start | bytes 6148
  0.0 19.8 %copy-start.1 = (f32[512]{0:T(512)S(1)}, f32[512]{0:T(512)}, u32[]{:S(2)}) copy-start(f32[512]{0:T(512)} %param.8) | copy-start | bytes 6148
  2.6 41.8 %all-to-all-start = ((bf16[64,2,3712]{2,1,0:T(2,128)(2,1)}), bf16[64,2,3712]{2,1,0:T(2,128)(2,1)S(1)}, u32[]{:S(2)}, u32[]{:S(2)}) async-start(bf16[64,2,3712]{2,1,0:T(2,128)(2,1)} %get-tuple-element.15), calls=%async_computation | async-start | bytes 1900544 | tf_op jit(solution)/shard_map/all_to_all | solution.py:284
  20.2 3.8 %collective-permute-start = (bf16[4,4,16,256]{3,2,1,0:T(8,128)(2,1)S(1)}, bf16[4,4,16,256]{3,2,1,0:T(8,128)(2,1)S(1)}, u32[]{:S(2)}, u32[]{:S(2)}) collective-permute-start(bf16[4,4,16,256]{3,2,1,0:T(8,128)(2,1)S(1)} %get-tuple-element.17), channel_id=1, source_target_pairs={{0,64},{64,0},{1,65},{65,1},{2,66},{66,2},{3,67},{67,3},{4,68},{68... | collective-permute-start | bytes 393224 | tf_op jit(solution)/shard_map/ppermute | solution.py:300
  24.0 10.6 %collective-permute-start.1 = (bf16[2,4,16,256]{3,2,1,0:T(8,128)(2,1)S(1)}, bf16[2,4,16,256]{3,2,1,0:T(8,128)(2,1)S(1)}, u32[]{:S(2)}, u32[]{:S(2)}) collective-permute-start(bf16[2,4,16,256]{3,2,1,0:T(8,128)(2,1)S(1)} %get-tuple-element.26), channel_id=1, source_target_pairs={{0,128},{128,256},{256,384},{384,0},{1,129},{129,257},{257,385},{3... | collective-permute-start | bytes 196616 | tf_op jit(solution)/shard_map/ppermute | solution.py:305
  27.1 7.4 %collective-permute-start.2 = (bf16[2,4,16,256]{3,2,1,0:T(8,128)(2,1)S(1)}, bf16[2,4,16,256]{3,2,1,0:T(8,128)(2,1)S(1)}, u32[]{:S(2)}, u32[]{:S(2)}) collective-permute-start(bf16[2,4,16,256]{3,2,1,0:T(8,128)(2,1)S(1)} %get-tuple-element.27), channel_id=1, source_target_pairs={{0,256},{128,384},{256,0},{384,128},{1,257},{129,385},{257,1},{385... | collective-permute-start | bytes 196616 | tf_op jit(solution)/shard_map/ppermute | solution.py:305
  31.5 5.3 %collective-permute-start.3 = (bf16[2,4,16,256]{3,2,1,0:T(8,128)(2,1)S(1)}, bf16[2,4,16,256]{3,2,1,0:T(8,128)(2,1)S(1)}, u32[]{:S(2)}, u32[]{:S(2)}) collective-permute-start(bf16[2,4,16,256]{3,2,1,0:T(8,128)(2,1)S(1)} %get-tuple-element.28), channel_id=1, source_target_pairs={{0,384},{128,0},{256,128},{384,256},{1,385},{129,1},{257,129},{385... | collective-permute-start | bytes 196616 | tf_op jit(solution)/shard_map/ppermute | solution.py:305
  37.6 17.8 %collective-permute-start.5 = (bf16[4,2,4,16,128]{4,3,2,1,0:T(8,128)(2,1)}, bf16[4,2,4,16,128]{4,3,2,1,0:T(8,128)(2,1)S(1)}, u32[]{:S(2)}, u32[]{:S(2)}) collective-permute-start(bf16[4,2,4,16,128]{4,3,2,1,0:T(8,128)(2,1)} %get-tuple-element.23), channel_id=1, source_target_pairs={{1,0},{2,1},{3,2},{4,3},{5,4},{6,5},{7,6},{8,7},{9,8},{10,9},{11,1... | collective-permute-start | bytes 393224 | tf_op jit(solution)/shard_map/ppermute | solution.py:310
  38.8 16.6 %collective-permute-start.4 = (bf16[4,2,4,16,128]{4,3,2,1,0:T(8,128)(2,1)S(1)}, bf16[4,2,4,16,128]{4,3,2,1,0:T(8,128)(2,1)S(1)}, u32[]{:S(2)}, u32[]{:S(2)}) collective-permute-start(bf16[4,2,4,16,128]{4,3,2,1,0:T(8,128)(2,1)S(1)} %get-tuple-element.24), channel_id=1, source_target_pairs={{0,1},{1,2},{2,3},{3,4},{4,5},{5,6},{6,7},{7,8},{8,9},{9,10},{10,1... | collective-permute-start | bytes 393224 | tf_op jit(solution)/shard_map/ppermute | solution.py:309
  45.2 12.8 %all-to-all-start.1 = ((f32[8,1,128]{2,1,0:T(1,128)}), f32[8,1,128]{2,1,0:T(1,128)S(1)}, u32[]{:S(2)}, u32[]{:S(2)}) async-start(f32[8,1,128]{2,1,0:T(1,128)} %sums.1), calls=%async_computation.1 | async-start | bytes 8192 | tf_op jit(solution)/shard_map/all_to_all | solution.py:321
  53.5 5.2 %collective-permute-start.6 = (bf16[2,64,3712]{2,1,0:T(8,128)(2,1)S(1)}, bf16[2,64,3712]{2,1,0:T(8,128)(2,1)S(1)}, u32[]{:S(2)}, u32[]{:S(2)}) collective-permute-start(bf16[2,64,3712]{2,1,0:T(8,128)(2,1)S(1)} %bitcast.24), channel_id=1, source_target_pairs={{0,64},{64,0},{1,65},{65,1},{2,66},{66,2},{3,67},{67,3},{4,68},{68... | collective-permute-start | bytes 2850824 | tf_op jit(solution)/shard_map/ppermute | solution.py:323
  60.8 5.0 %copy-start.3 = (s32[2]{0:T(128)S(1)}, s32[2]{0:T(128)}, u32[]{:S(2)}) copy-start(s32[2]{0:T(128)} %lengths.1) | copy-start | bytes 28
  61.8 13.6 %all-to-all-start.2 = ((f16[8,4,32,256]{3,2,1,0:T(8,128)(2,1)}), f16[8,4,32,256]{3,2,1,0:T(8,128)(2,1)S(1)}, u32[]{:S(2)}, u32[]{:S(2)}) async-start(f16[8,4,32,256]{3,2,1,0:T(8,128)(2,1)} %convert_element_type.7), calls=%async_computation.2 | async-start | bytes 1048576 | tf_op jit(solution)/shard_map/all_to_all | solution.py:359

commit v12 on v11

--- a/solution.py
+++ b/solution.py
@@ -304,8 +304,9 @@
         if step:
             block = lax.ppermute(block, "x", [(i, (i + step) % chips) for i in range(chips)])
         signal.append(block)
+    upper = jnp.stack([block[..., PART:] for block in signal])
+    lower = jnp.stack([block[..., :PART] for block in signal])
     signal = jnp.stack(signal)
-    upper, lower = signal[..., PART:], signal[..., :PART]
     above = lax.ppermute(upper, TILE, [(i, i + 1) for i in range(tiles - 1)])
     below = lax.ppermute(lower, TILE, [(i + 1, i) for i in range(tiles - 1)])
 

time: 76.7 us -> 76.7 us (level)
  starting transfers between devices: 50 us -> 49.2 us
    all_to_all x1, waiting for transfers between devices: 1.57 us -> 2.38 us  [per_device(): arrived = lax.all_to_all(copies, TILE, 0, 0, tiled=True)]
    ppermute x1, starting transfers between devices: 3.99 us -> 3.2 us  [per_device(): above = lax.ppermute(upper, TILE, [(i, i + 1) for i in range(tiles - 1)])]
where the time goes in v12:
time: 76.7 us; the launch traced here: 76.2 us
  starting transfers between devices  49.2 us (64%)
  waiting for transfers between devices  17.4 us (23%)
  Pallas kernels  6.57 us (9%)
  other arithmetic  2.6 us (3%)
    all_to_all x1, starting transfers between devices, per_device(): arrived = lax.all_to_all(copies, TILE, 0, 0, tiled=True)  17.1 us
    ppermute x3, starting transfers between devices, per_device(): lax.ppermute(block, 'x', [(i, (i + step) % chips) for i in range(chips)])  10.5 us
    all_to_all x1, waiting for transfers between devices, per_device(): total = lax.all_to_all(total, TM, 0, 0, tiled=True).astype(jnp.float32)  9.42 us
    all_to_all x1, starting transfers between devices, per_device(): totals = lax.all_to_all(copies, TM, 0, 0, tiled=True).reshape(SPANS, -1)  8.18 us
    all_to_all x1, starting transfers between devices, per_device(): total = lax.all_to_all(total, TM, 0, 0, tiled=True).astype(jnp.float32)  4.07 us
    ppermute x1, starting transfers between devices, per_device(): above = lax.ppermute(upper, TILE, [(i, i + 1) for i in range(tiles - 1)])  3.2 us
    ppermute x1, starting transfers between devices, per_device(): shares = jnp.stack([kept, lax.ppermute(sent, 'core', swap)], axis=1)  2.86 us
    pallas_call x1, Pallas kernels, per_device(): pl.pallas_call(payload_kernel, out_shape=(jax.ShapeDtypeStruct((tiles, 2,...  2.56 us
  transfers between devices with their start and end apart: 10, of which 5 were waited for; matrix products, arithmetic and copies ran while one was open for 1% of the time, Pallas kernels for 2%

profile of v12, /device:TPU:1, one launch (start us, length us, event | category | flops | bytes accessed | tf_op | source)
XLA Modules:
  0.0 76.2 jit_solution(5749981980057161188)
XLA Ops:
  0.0 2.6 %payload.1 = (bf16[64,2,3712]{2,1,0:T(2,128)(2,1)}, f32[8,128]{1,0:T(8,128)S(1)}) custom-call(bf16[8,32,512]{2,1,0:T(8,128)(2,1)} %bitcast.39, bf16[27,8,256]{2,1,0:T(8,128)(2,1)} %bitcast.54, bf16[8,256]{1,0:T(8,128)(2,1)} %skip.1, s32[2]{0:T(128)} %lengths.1), custom_call_target="tpu_custom_call" | custom-call | tf_op jit(solution)/shard_map/payload/pallas_call | solution.py:257
  2.6 17.1 %all-to-all-start = ((bf16[64,2,3712]{2,1,0:T(2,128)(2,1)}), bf16[64,2,3712]{2,1,0:T(2,128)(2,1)S(1)}, u32[]{:S(2)}, u32[]{:S(2)}) async-start(bf16[64,2,3712]{2,1,0:T(2,128)(2,1)} %get-tuple-element.15), calls=%async_computation | async-start | bytes 1900544 | tf_op jit(solution)/shard_map/all_to_all | solution.py:284
  19.8 0.4 member_shares.1
  20.2 2.9 %collective-permute-start = (bf16[4,4,16,256]{3,2,1,0:T(8,128)(2,1)S(1)}, bf16[4,4,16,256]{3,2,1,0:T(8,128)(2,1)S(1)}, u32[]{:S(2)}, u32[]{:S(2)}) collective-permute-start(bf16[4,4,16,256]{3,2,1,0:T(8,128)(2,1)S(1)} %get-tuple-element.17), channel_id=1, source_target_pairs={{0,64},{64,0},{1,65},{65,1},{2,66},{66,2},{3,67},{67,3},{4,68},{68... | collective-permute-start | bytes 393224 | tf_op jit(solution)/shard_map/ppermute | solution.py:300
  23.1 0.9 %collective-permute-done = bf16[4,4,16,256]{3,2,1,0:T(8,128)(2,1)S(1)} collective-permute-done((bf16[4,4,16,256]{3,2,1,0:T(8,128)(2,1)S(1)}, bf16[4,4,16,256]{3,2,1,0:T(8,128)(2,1)S(1)}, u32[]{:S(2)}, u32[]{:S(2)}) %collective-permute-start) | collective-permute-done | bytes 131104 | tf_op jit(solution)/shard_map/ppermute | solution.py:300
  24.0 3.1 %collective-permute-start.1 = (bf16[2,4,16,256]{3,2,1,0:T(8,128)(2,1)S(1)}, bf16[2,4,16,256]{3,2,1,0:T(8,128)(2,1)S(1)}, u32[]{:S(2)}, u32[]{:S(2)}) collective-permute-start(bf16[2,4,16,256]{3,2,1,0:T(8,128)(2,1)S(1)} %get-tuple-element.24), channel_id=1, source_target_pairs={{0,128},{128,256},{256,384},{384,0},{1,129},{129,257},{257,385},{3... | collective-permute-start | bytes 196616 | tf_op jit(solution)/shard_map/ppermute | solution.py:305
  27.2 4.4 %collective-permute-start.2 = (bf16[2,4,16,256]{3,2,1,0:T(8,128)(2,1)S(1)}, bf16[2,4,16,256]{3,2,1,0:T(8,128)(2,1)S(1)}, u32[]{:S(2)}, u32[]{:S(2)}) collective-permute-start(bf16[2,4,16,256]{3,2,1,0:T(8,128)(2,1)S(1)} %get-tuple-element.25), channel_id=1, source_target_pairs={{0,256},{128,384},{256,0},{384,128},{1,257},{129,385},{257,1},{385... | collective-permute-start | bytes 196616 | tf_op jit(solution)/shard_map/ppermute | solution.py:305
  31.5 3.1 %collective-permute-start.3 = (bf16[2,4,16,256]{3,2,1,0:T(8,128)(2,1)S(1)}, bf16[2,4,16,256]{3,2,1,0:T(8,128)(2,1)S(1)}, u32[]{:S(2)}, u32[]{:S(2)}) collective-permute-start(bf16[2,4,16,256]{3,2,1,0:T(8,128)(2,1)S(1)} %get-tuple-element.26), channel_id=1, source_target_pairs={{0,384},{128,0},{256,128},{384,256},{1,385},{129,1},{257,129},{385... | collective-permute-start | bytes 196616 | tf_op jit(solution)/shard_map/ppermute | solution.py:305
  34.6 0.0 collective-permute-done.1
  34.6 0.0 collective-permute-done.2
  34.7 2.2 %collective-permute-done.3 = bf16[2,4,16,256]{3,2,1,0:T(8,128)(2,1)S(1)} collective-permute-done((bf16[2,4,16,256]{3,2,1,0:T(8,128)(2,1)S(1)}, bf16[2,4,16,256]{3,2,1,0:T(8,128)(2,1)S(1)}, u32[]{:S(2)}, u32[]{:S(2)}) %collective-permute-start.3) | collective-permute-done | bytes 65568 | tf_op jit(solution)/shard_map/ppermute | solution.py:305
  36.9 3.2 %collective-permute-start.4 = (bf16[4,2,4,16,128]{4,3,2,1,0:T(8,128)(2,1)S(1)}, bf16[4,2,4,16,128]{4,3,2,1,0:T(8,128)(2,1)S(1)}, u32[]{:S(2)}, u32[]{:S(2)}) collective-permute-start(bf16[4,2,4,16,128]{4,3,2,1,0:T(8,128)(2,1)S(1)} %pad_maximum_fusion.1), channel_id=1, source_target_pairs={{0,1},{1,2},{2,3},{3,4},{4,5},{5,6},{6,7},{7,8},{8,9},{9,10},{10,1... | collective-permute-start | bytes 393224 | tf_op jit(solution)/shard_map/ppermute | solution.py:310
  40.1 0.7 pad_maximum_fusion.2
  40.8 1.3 %collective-permute-start.5 = (bf16[4,2,4,16,128]{4,3,2,1,0:T(8,128)(2,1)}, bf16[4,2,4,16,128]{4,3,2,1,0:T(8,128)(2,1)S(1)}, u32[]{:S(2)}, u32[]{:S(2)}) collective-permute-start(bf16[4,2,4,16,128]{4,3,2,1,0:T(8,128)(2,1)} %pad_maximum_fusion.2), channel_id=1, source_target_pairs={{1,0},{2,1},{3,2},{4,3},{5,4},{6,5},{7,6},{8,7},{9,8},{10,9},{11,1... | collective-permute-start | bytes 393224 | tf_op jit(solution)/shard_map/ppermute | solution.py:311
  42.1 2.4 %all-to-all-done.arrived = bf16[64,2,3712]{2,1,0:T(2,128)(2,1)S(1)} async-done(((bf16[64,2,3712]{2,1,0:T(2,128)(2,1)}), bf16[64,2,3712]{2,1,0:T(2,128)(2,1)S(1)}, u32[]{:S(2)}, u32[]{:S(2)}) %all-to-all-start) | async-done | bytes 950304 | tf_op jit(solution)/shard_map/all_to_all | solution.py:284
  44.4 0.7 sums.1
  45.2 8.2 %all-to-all-start.1 = ((f32[8,1,128]{2,1,0:T(1,128)}), f32[8,1,128]{2,1,0:T(1,128)S(1)}, u32[]{:S(2)}, u32[]{:S(2)}) async-start(f32[8,1,128]{2,1,0:T(1,128)} %sums.1), calls=%async_computation.1 | async-start | bytes 8192 | tf_op jit(solution)/shard_map/all_to_all | solution.py:322
  53.4 0.1 copy.12
  53.5 1.9 %collective-permute-start.6 = (bf16[2,64,3712]{2,1,0:T(8,128)(2,1)S(1)}, bf16[2,64,3712]{2,1,0:T(8,128)(2,1)S(1)}, u32[]{:S(2)}, u32[]{:S(2)}) collective-permute-start(bf16[2,64,3712]{2,1,0:T(8,128)(2,1)S(1)} %bitcast.41), channel_id=1, source_target_pairs={{0,64},{64,0},{1,65},{65,1},{2,66},{66,2},{3,67},{67,3},{4,68},{68... | collective-permute-start | bytes 2850824 | tf_op jit(solution)/shard_map/ppermute | solution.py:324
  55.4 0.0 collective-permute-done.4.above
  55.4 0.0 collective-permute-done.5.below
  55.5 2.5 %all-to-all-done.1 = f32[8,1,128]{2,1,0:T(1,128)S(1)} async-done(((f32[8,1,128]{2,1,0:T(1,128)}), f32[8,1,128]{2,1,0:T(1,128)S(1)}, u32[]{:S(2)}, u32[]{:S(2)}) %all-to-all-start.1) | async-done | bytes 4128 | tf_op jit(solution)/shard_map/all_to_all | solution.py:322
  57.9 0.8 %norm.1 = (bf16[3,34,16,512]{3,2,1,0:T(8,128)(2,1)S(1)}, bf16[32,16,256]{2,1,0:T(8,128)(2,1)S(1)}, f32[2,256]{1,0:T(2,128)S(1)}) custom-call(f32[8,128]{1,0:T(8,128)S(1)} %bitcast.44, f32[8,128]{1,0:T(8,128)S(1)} %get-tuple-element.14.counts, f32[2,128]{1,0:T(2,128)S(1)} %get-tuple-element.19.lanes, bf16[4,2,4,16,256]{4,3,2,1,0:T(8,128)(2,1)S(1)} %pad_maximum_fusion.signal, ...), custom_call_target="tpu_custom_call" | custom-call | flops 17179869184 | bytes 67108864 | tf_op jit(solution)/shard_map/norm/pallas_call | solution.py:326
  58.7 0.0 collective-permute-done.6.theirs
  58.7 2.1 %taps.1 = f32[8,4,32,256]{3,2,1,0:T(8,128)S(1)} custom-call(bf16[3,34,16,512]{3,2,1,0:T(8,128)(2,1)S(1)} %get-tuple-element.20.shifted, bf16[32,16,256]{2,1,0:T(8,128)(2,1)S(1)} %get-tuple-element.21.raw, bf16[2,64,3712]{2,1,0:T(8,128)(2,1)S(1)} %bitcast.42, bf16[2,64,3712]{2,1,0:T(8,128)(2,1)S(1)} %collective-permute-done.6.theirs, ...), custom_call_target="tpu_custom_call" | custom-call | flops 1879048192 | bytes 6291456 | tf_op jit(solution)/shard_map/taps/pallas_call | solution.py:346
  60.8 0.0 copy-start.3
  60.8 0.9 %convert_element_type.7 = f16[8,4,32,256]{3,2,1,0:T(8,128)(2,1)} convert(f32[8,4,32,256]{3,2,1,0:T(8,128)S(1)} %taps.1) | non-fusion elementwise | flops 262144 | bytes 1572864 | tf_op jit(solution)/shard_map/convert_element_type | solution.py:359
  61.8 4.1 %all-to-all-start.2 = ((f16[8,4,32,256]{3,2,1,0:T(8,128)(2,1)}), f16[8,4,32,256]{3,2,1,0:T(8,128)(2,1)S(1)}, u32[]{:S(2)}, u32[]{:S(2)}) async-start(f16[8,4,32,256]{3,2,1,0:T(8,128)(2,1)} %convert_element_type.7), calls=%async_computation.2 | async-start | bytes 1048576 | tf_op jit(solution)/shard_map/all_to_all | solution.py:360
  65.8 0.1 broadcast_compare_fusion
  65.9 9.4 %all-to-all-done.2 = f16[8,4,32,256]{3,2,1,0:T(8,128)(2,1)S(1)} async-done(((f16[8,4,32,256]{3,2,1,0:T(8,128)(2,1)}), f16[8,4,32,256]{3,2,1,0:T(8,128)(2,1)S(1)}, u32[]{:S(2)}, u32[]{:S(2)}) %all-to-all-start.2) | async-done | bytes 524320 | tf_op jit(solution)/shard_map/all_to_all | solution.py:360
  75.3 0.1 convert_reduce_fusion
  75.4 0.7 select_convert_fusion
  (15 shorter events, 0.1 us)
Async XLA Ops:
  0.0 19.7 %copy-start = (bf16[2,4,2,16,512]{4,3,2,1,0:T(8,128)(2,1)S(1)}, bf16[2,4,2,16,512]{4,3,2,1,0:T(8,128)(2,1)}, u32[]{:S(2)}) copy-start(bf16[2,4,2,16,512]{4,3,2,1,0:T(8,128)(2,1)} %param.6) | copy-start | bytes 786436
  0.0 19.7 %copy-start.2 = (f32[512]{0:T(512)S(1)}, f32[512]{0:T(512)}, u32[]{:S(2)}) copy-start(f32[512]{0:T(512)} %param.9) | copy-start | bytes 6148
  0.0 19.8 %copy-start.1 = (f32[512]{0:T(512)S(1)}, f32[512]{0:T(512)}, u32[]{:S(2)}) copy-start(f32[512]{0:T(512)} %param.8) | copy-start | bytes 6148
  2.6 41.9 %all-to-all-start = ((bf16[64,2,3712]{2,1,0:T(2,128)(2,1)}), bf16[64,2,3712]{2,1,0:T(2,128)(2,1)S(1)}, u32[]{:S(2)}, u32[]{:S(2)}) async-start(bf16[64,2,3712]{2,1,0:T(2,128)(2,1)} %get-tuple-element.15), calls=%async_computation | async-start | bytes 1900544 | tf_op jit(solution)/shard_map/all_to_all | solution.py:284
  20.2 3.8 %collective-permute-start = (bf16[4,4,16,256]{3,2,1,0:T(8,128)(2,1)S(1)}, bf16[4,4,16,256]{3,2,1,0:T(8,128)(2,1)S(1)}, u32[]{:S(2)}, u32[]{:S(2)}) collective-permute-start(bf16[4,4,16,256]{3,2,1,0:T(8,128)(2,1)S(1)} %get-tuple-element.17), channel_id=1, source_target_pairs={{0,64},{64,0},{1,65},{65,1},{2,66},{66,2},{3,67},{67,3},{4,68},{68... | collective-permute-start | bytes 393224 | tf_op jit(solution)/shard_map/ppermute | solution.py:300
  24.0 10.6 %collective-permute-start.1 = (bf16[2,4,16,256]{3,2,1,0:T(8,128)(2,1)S(1)}, bf16[2,4,16,256]{3,2,1,0:T(8,128)(2,1)S(1)}, u32[]{:S(2)}, u32[]{:S(2)}) collective-permute-start(bf16[2,4,16,256]{3,2,1,0:T(8,128)(2,1)S(1)} %get-tuple-element.24), channel_id=1, source_target_pairs={{0,128},{128,256},{256,384},{384,0},{1,129},{129,257},{257,385},{3... | collective-permute-start | bytes 196616 | tf_op jit(solution)/shard_map/ppermute | solution.py:305
  27.2 7.5 %collective-permute-start.2 = (bf16[2,4,16,256]{3,2,1,0:T(8,128)(2,1)S(1)}, bf16[2,4,16,256]{3,2,1,0:T(8,128)(2,1)S(1)}, u32[]{:S(2)}, u32[]{:S(2)}) collective-permute-start(bf16[2,4,16,256]{3,2,1,0:T(8,128)(2,1)S(1)} %get-tuple-element.25), channel_id=1, source_target_pairs={{0,256},{128,384},{256,0},{384,128},{1,257},{129,385},{257,1},{385... | collective-permute-start | bytes 196616 | tf_op jit(solution)/shard_map/ppermute | solution.py:305
  31.5 5.3 %collective-permute-start.3 = (bf16[2,4,16,256]{3,2,1,0:T(8,128)(2,1)S(1)}, bf16[2,4,16,256]{3,2,1,0:T(8,128)(2,1)S(1)}, u32[]{:S(2)}, u32[]{:S(2)}) collective-permute-start(bf16[2,4,16,256]{3,2,1,0:T(8,128)(2,1)S(1)} %get-tuple-element.26), channel_id=1, source_target_pairs={{0,384},{128,0},{256,128},{384,256},{1,385},{129,1},{257,129},{385... | collective-permute-start | bytes 196616 | tf_op jit(solution)/shard_map/ppermute | solution.py:305
  36.9 18.5 %collective-permute-start.4 = (bf16[4,2,4,16,128]{4,3,2,1,0:T(8,128)(2,1)S(1)}, bf16[4,2,4,16,128]{4,3,2,1,0:T(8,128)(2,1)S(1)}, u32[]{:S(2)}, u32[]{:S(2)}) collective-permute-start(bf16[4,2,4,16,128]{4,3,2,1,0:T(8,128)(2,1)S(1)} %pad_maximum_fusion.1), channel_id=1, source_target_pairs={{0,1},{1,2},{2,3},{3,4},{4,5},{5,6},{6,7},{7,8},{8,9},{9,10},{10,1... | collective-permute-start | bytes 393224 | tf_op jit(solution)/shard_map/ppermute | solution.py:310
  40.8 14.7 %collective-permute-start.5 = (bf16[4,2,4,16,128]{4,3,2,1,0:T(8,128)(2,1)}, bf16[4,2,4,16,128]{4,3,2,1,0:T(8,128)(2,1)S(1)}, u32[]{:S(2)}, u32[]{:S(2)}) collective-permute-start(bf16[4,2,4,16,128]{4,3,2,1,0:T(8,128)(2,1)} %pad_maximum_fusion.2), channel_id=1, source_target_pairs={{1,0},{2,1},{3,2},{4,3},{5,4},{6,5},{7,6},{8,7},{9,8},{10,9},{11,1... | collective-permute-start | bytes 393224 | tf_op jit(solution)/shard_map/ppermute | solution.py:311
  45.2 12.8 %all-to-all-start.1 = ((f32[8,1,128]{2,1,0:T(1,128)}), f32[8,1,128]{2,1,0:T(1,128)S(1)}, u32[]{:S(2)}, u32[]{:S(2)}) async-start(f32[8,1,128]{2,1,0:T(1,128)} %sums.1), calls=%async_computation.1 | async-start | bytes 8192 | tf_op jit(solution)/shard_map/all_to_all | solution.py:322
  53.5 5.2 %collective-permute-start.6 = (bf16[2,64,3712]{2,1,0:T(8,128)(2,1)S(1)}, bf16[2,64,3712]{2,1,0:T(8,128)(2,1)S(1)}, u32[]{:S(2)}, u32[]{:S(2)}) collective-permute-start(bf16[2,64,3712]{2,1,0:T(8,128)(2,1)S(1)} %bitcast.41), channel_id=1, source_target_pairs={{0,64},{64,0},{1,65},{65,1},{2,66},{66,2},{3,67},{67,3},{4,68},{68... | collective-permute-start | bytes 2850824 | tf_op jit(solution)/shard_map/ppermute | solution.py:324
  60.8 5.0 %copy-start.3 = (s32[2]{0:T(128)S(1)}, s32[2]{0:T(128)}, u32[]{:S(2)}) copy-start(s32[2]{0:T(128)} %lengths.1) | copy-start | bytes 28
  61.8 13.6 %all-to-all-start.2 = ((f16[8,4,32,256]{3,2,1,0:T(8,128)(2,1)}), f16[8,4,32,256]{3,2,1,0:T(8,128)(2,1)S(1)}, u32[]{:S(2)}, u32[]{:S(2)}) async-start(f16[8,4,32,256]{3,2,1,0:T(8,128)(2,1)} %convert_element_type.7), calls=%async_computation.2 | async-start | bytes 1048576 | tf_op jit(solution)/shard_map/all_to_all | solution.py:360

commit v13 on v11

--- a/solution.py
+++ b/solution.py
@@ -213,7 +213,7 @@
         shifted[side, 1] = shifted[side, 2]
 
 
-def taps_kernel(shifted, raw, mine, theirs, factor, out, weights):
+def taps_kernel(shifted, raw, mine, theirs, out, weights):
     core = lax.axis_index("core")
     count = weights.shape[0]
     for tap in range(count):
@@ -222,7 +222,6 @@
             rows = pl.ds(pl.multiple_of(place * SHARE, SHARE), SHARE)
             weights[tap, rows] = half[line, :, at : at + OUT]
     length = SPANS * FRAMES
-    scale = jnp.where(core == 0, factor[0:1, :], factor[1:2, :])
     for row in range(2):
         total = None
         for pair in range(count // 2):
@@ -240,7 +239,7 @@
                 preferred_element_type=jnp.float32,
             )
             total = term if total is None else total + term
-        total = (total * scale).reshape(SPANS, FRAMES, COLS, OUT)
+        total = total.reshape(SPANS, FRAMES, COLS, OUT)
         out[:, :, row * COLS : (row + 1) * COLS, :] = total
 
 
@@ -345,7 +344,7 @@
     total = pl.pallas_call(
         taps_kernel,
         out_shape=jax.ShapeDtypeStruct((SPANS, frames, row_count * col_count, OUT), jnp.float32),
-        in_specs=[on_chip] * 5,
+        in_specs=[on_chip] * 4,
         out_specs=on_chip,
         scratch_shapes=[pltpu.VMEM((taps + 1, PART, OUT), jnp.bfloat16)],
         compiler_params=params,
@@ -353,9 +352,10 @@
             flops=2 * 28 * 1024 * 128 * 256, bytes_accessed=6 << 20, transcendentals=0
         ),
         name="taps",
-    )(shifted, raw, mine, theirs, factor)
-
-    total = total.astype(jnp.float16)
+    )(shifted, raw, mine, theirs)
+
+    scale = jnp.where(lax.axis_index("core") == 0, factor[0], factor[1])
+    total = (total * scale).astype(jnp.float16)
     total = lax.all_to_all(total, TM, 0, 0, tiled=True).astype(jnp.float32)
     total = jnp.sum(total.reshape((chips, videos) + total.shape[1:]), axis=0)
     total = total / factor[:, None, None, :]

time: 76.7 us -> 76.7 us (level)
  no operation moved by 1% of the time
where the time goes in v13:
time: 76.7 us; the launch traced here: 76.2 us
  starting transfers between devices  50 us (65%)
  waiting for transfers between devices  16.7 us (22%)
  Pallas kernels  6.56 us (9%)
  other arithmetic  1.91 us (2%)
  local copies, waits for them, and re-layouts  0.82 us (1%)
    all_to_all x1, starting transfers between devices, per_device(): arrived = lax.all_to_all(copies, TILE, 0, 0, tiled=True)  17.1 us
    ppermute x3, starting transfers between devices, per_device(): lax.ppermute(block, 'x', [(i, (i + step) % chips) for i in range(chips)])  10.5 us
    all_to_all x1, waiting for transfers between devices, per_device(): total = lax.all_to_all(total, TM, 0, 0, tiled=True).astype(jnp.float32)  9.42 us
    all_to_all x1, starting transfers between devices, per_device(): totals = lax.all_to_all(copies, TM, 0, 0, tiled=True).reshape(SPANS, -1)  8.21 us
    all_to_all x1, starting transfers between devices, per_device(): total = lax.all_to_all(total, TM, 0, 0, tiled=True).astype(jnp.float32)  4.07 us
    ppermute x1, starting transfers between devices, per_device(): above = lax.ppermute(upper, TILE, [(i, i + 1) for i in range(tiles - 1)])  3.99 us
    ppermute x1, starting transfers between devices, per_device(): shares = jnp.stack([kept, lax.ppermute(sent, 'core', swap)], axis=1)  2.86 us
    pallas_call x1, Pallas kernels, per_device(): pl.pallas_call(payload_kernel, out_shape=(jax.ShapeDtypeStruct((tiles, 2,...  2.56 us
  transfers between devices with their start and end apart: 10, of which 5 were waited for; matrix products, arithmetic and copies ran while one was open for 1% of the time, Pallas kernels for 2%

profile of v13, /device:TPU:1, one launch (start us, length us, event | category | flops | bytes accessed | tf_op | source)
XLA Modules:
  0.0 76.2 jit_solution(5355933609137562005)
XLA Ops:
  0.0 2.6 %payload.1 = (bf16[64,2,3712]{2,1,0:T(2,128)(2,1)}, f32[8,128]{1,0:T(8,128)S(1)}) custom-call(bf16[8,32,512]{2,1,0:T(8,128)(2,1)} %bitcast.23, bf16[27,8,256]{2,1,0:T(8,128)(2,1)} %bitcast.34, bf16[8,256]{1,0:T(8,128)(2,1)} %skip.1, s32[2]{0:T(128)} %lengths.1), custom_call_target="tpu_custom_call" | custom-call | tf_op jit(solution)/shard_map/payload/pallas_call | solution.py:256
  2.6 17.1 %all-to-all-start = ((bf16[64,2,3712]{2,1,0:T(2,128)(2,1)}), bf16[64,2,3712]{2,1,0:T(2,128)(2,1)S(1)}, u32[]{:S(2)}, u32[]{:S(2)}) async-start(bf16[64,2,3712]{2,1,0:T(2,128)(2,1)} %get-tuple-element.15), calls=%async_computation | async-start | bytes 1900544 | tf_op jit(solution)/shard_map/all_to_all | solution.py:283
  19.8 0.4 member_shares.1
  20.2 2.9 %collective-permute-start = (bf16[4,4,16,256]{3,2,1,0:T(8,128)(2,1)S(1)}, bf16[4,4,16,256]{3,2,1,0:T(8,128)(2,1)S(1)}, u32[]{:S(2)}, u32[]{:S(2)}) collective-permute-start(bf16[4,4,16,256]{3,2,1,0:T(8,128)(2,1)S(1)} %get-tuple-element.17), channel_id=1, source_target_pairs={{0,64},{64,0},{1,65},{65,1},{2,66},{66,2},{3,67},{67,3},{4,68},{68... | collective-permute-start | bytes 393224 | tf_op jit(solution)/shard_map/ppermute | solution.py:299
  23.1 0.9 %collective-permute-done = bf16[4,4,16,256]{3,2,1,0:T(8,128)(2,1)S(1)} collective-permute-done((bf16[4,4,16,256]{3,2,1,0:T(8,128)(2,1)S(1)}, bf16[4,4,16,256]{3,2,1,0:T(8,128)(2,1)S(1)}, u32[]{:S(2)}, u32[]{:S(2)}) %collective-permute-start) | collective-permute-done | bytes 131104 | tf_op jit(solution)/shard_map/ppermute | solution.py:299
  24.0 3.1 %collective-permute-start.1 = (bf16[2,4,16,256]{3,2,1,0:T(8,128)(2,1)S(1)}, bf16[2,4,16,256]{3,2,1,0:T(8,128)(2,1)S(1)}, u32[]{:S(2)}, u32[]{:S(2)}) collective-permute-start(bf16[2,4,16,256]{3,2,1,0:T(8,128)(2,1)S(1)} %get-tuple-element.26), channel_id=1, source_target_pairs={{0,128},{128,256},{256,384},{384,0},{1,129},{129,257},{257,385},{3... | collective-permute-start | bytes 196616 | tf_op jit(solution)/shard_map/ppermute | solution.py:304
  27.1 4.4 %collective-permute-start.2 = (bf16[2,4,16,256]{3,2,1,0:T(8,128)(2,1)S(1)}, bf16[2,4,16,256]{3,2,1,0:T(8,128)(2,1)S(1)}, u32[]{:S(2)}, u32[]{:S(2)}) collective-permute-start(bf16[2,4,16,256]{3,2,1,0:T(8,128)(2,1)S(1)} %get-tuple-element.27), channel_id=1, source_target_pairs={{0,256},{128,384},{256,0},{384,128},{1,257},{129,385},{257,1},{385... | collective-permute-start | bytes 196616 | tf_op jit(solution)/shard_map/ppermute | solution.py:304
  31.5 3.1 %collective-permute-start.3 = (bf16[2,4,16,256]{3,2,1,0:T(8,128)(2,1)S(1)}, bf16[2,4,16,256]{3,2,1,0:T(8,128)(2,1)S(1)}, u32[]{:S(2)}, u32[]{:S(2)}) collective-permute-start(bf16[2,4,16,256]{3,2,1,0:T(8,128)(2,1)S(1)} %get-tuple-element.28), channel_id=1, source_target_pairs={{0,384},{128,0},{256,128},{384,256},{1,385},{129,1},{257,129},{385... | collective-permute-start | bytes 196616 | tf_op jit(solution)/shard_map/ppermute | solution.py:304
  34.6 0.0 collective-permute-done.1
  34.6 0.0 collective-permute-done.2
  34.6 2.2 %collective-permute-done.3 = bf16[2,4,16,256]{3,2,1,0:T(8,128)(2,1)S(1)} collective-permute-done((bf16[2,4,16,256]{3,2,1,0:T(8,128)(2,1)S(1)}, bf16[2,4,16,256]{3,2,1,0:T(8,128)(2,1)S(1)}, u32[]{:S(2)}, u32[]{:S(2)}) %collective-permute-start.3) | collective-permute-done | bytes 65568 | tf_op jit(solution)/shard_map/ppermute | solution.py:304
  36.9 0.7 fusion.7
  37.6 1.3 %collective-permute-start.5 = (bf16[4,2,4,16,128]{4,3,2,1,0:T(8,128)(2,1)}, bf16[4,2,4,16,128]{4,3,2,1,0:T(8,128)(2,1)S(1)}, u32[]{:S(2)}, u32[]{:S(2)}) collective-permute-start(bf16[4,2,4,16,128]{4,3,2,1,0:T(8,128)(2,1)} %get-tuple-element.23), channel_id=1, source_target_pairs={{1,0},{2,1},{3,2},{4,3},{5,4},{6,5},{7,6},{8,7},{9,8},{10,9},{11,1... | collective-permute-start | bytes 393224 | tf_op jit(solution)/shard_map/ppermute | solution.py:309
  38.8 4.0 %collective-permute-start.4 = (bf16[4,2,4,16,128]{4,3,2,1,0:T(8,128)(2,1)S(1)}, bf16[4,2,4,16,128]{4,3,2,1,0:T(8,128)(2,1)S(1)}, u32[]{:S(2)}, u32[]{:S(2)}) collective-permute-start(bf16[4,2,4,16,128]{4,3,2,1,0:T(8,128)(2,1)S(1)} %get-tuple-element.24), channel_id=1, source_target_pairs={{0,1},{1,2},{2,3},{3,4},{4,5},{5,6},{6,7},{7,8},{8,9},{9,10},{10,1... | collective-permute-start | bytes 393224 | tf_op jit(solution)/shard_map/ppermute | solution.py:308
  42.8 1.6 %all-to-all-done.arrived = bf16[64,2,3712]{2,1,0:T(2,128)(2,1)S(1)} async-done(((bf16[64,2,3712]{2,1,0:T(2,128)(2,1)}), bf16[64,2,3712]{2,1,0:T(2,128)(2,1)S(1)}, u32[]{:S(2)}, u32[]{:S(2)}) %all-to-all-start) | async-done | bytes 950304 | tf_op jit(solution)/shard_map/all_to_all | solution.py:283
  44.4 0.7 sums.1
  45.2 8.2 %all-to-all-start.1 = ((f32[8,1,128]{2,1,0:T(1,128)}), f32[8,1,128]{2,1,0:T(1,128)S(1)}, u32[]{:S(2)}, u32[]{:S(2)}) async-start(f32[8,1,128]{2,1,0:T(1,128)} %sums.1), calls=%async_computation.1 | async-start | bytes 8192 | tf_op jit(solution)/shard_map/all_to_all | solution.py:320
  53.4 0.1 copy.12
  53.5 1.9 %collective-permute-start.6 = (bf16[2,64,3712]{2,1,0:T(8,128)(2,1)S(1)}, bf16[2,64,3712]{2,1,0:T(8,128)(2,1)S(1)}, u32[]{:S(2)}, u32[]{:S(2)}) collective-permute-start(bf16[2,64,3712]{2,1,0:T(8,128)(2,1)S(1)} %bitcast.25), channel_id=1, source_target_pairs={{0,64},{64,0},{1,65},{65,1},{2,66},{66,2},{3,67},{67,3},{4,68},{68... | collective-permute-start | bytes 2850824 | tf_op jit(solution)/shard_map/ppermute | solution.py:322
  55.4 0.0 collective-permute-done.5.below
  55.4 0.0 collective-permute-done.4.above
  55.4 2.5 %all-to-all-done.1 = f32[8,1,128]{2,1,0:T(1,128)S(1)} async-done(((f32[8,1,128]{2,1,0:T(1,128)}), f32[8,1,128]{2,1,0:T(1,128)S(1)}, u32[]{:S(2)}, u32[]{:S(2)}) %all-to-all-start.1) | async-done | bytes 4128 | tf_op jit(solution)/shard_map/all_to_all | solution.py:320
  57.9 0.8 %norm.1 = (bf16[3,34,16,512]{3,2,1,0:T(8,128)(2,1)S(1)}, bf16[32,16,256]{2,1,0:T(8,128)(2,1)S(1)}, f32[2,256]{1,0:T(2,128)S(1)}) custom-call(f32[8,128]{1,0:T(8,128)S(1)} %bitcast.28, f32[8,128]{1,0:T(8,128)S(1)} %get-tuple-element.14.counts, f32[2,128]{1,0:T(2,128)S(1)} %get-tuple-element.19.lanes, bf16[4,2,4,16,256]{4,3,2,1,0:T(8,128)(2,1)S(1)} %pad_maximum_fusion.signal, ...), custom_call_target="tpu_custom_call" | custom-call | flops 17179869184 | bytes 67108864 | tf_op jit(solution)/shard_map/norm/pallas_call | solution.py:324
  58.7 0.0 collective-permute-done.6.theirs
  58.7 2.1 %taps.1 = f32[8,4,32,256]{3,2,1,0:T(8,128)S(1)} custom-call(bf16[3,34,16,512]{3,2,1,0:T(8,128)(2,1)S(1)} %get-tuple-element.20.shifted, bf16[32,16,256]{2,1,0:T(8,128)(2,1)S(1)} %get-tuple-element.21.raw, bf16[2,64,3712]{2,1,0:T(8,128)(2,1)S(1)} %bitcast.26, bf16[2,64,3712]{2,1,0:T(8,128)(2,1)S(1)} %collective-permute-done.6.theirs), custom_call_target="tpu_custom_call" | custom-call | flops 1879048192 | bytes 6291456 | tf_op jit(solution)/shard_map/taps/pallas_call | solution.py:344
  60.8 0.0 copy-start.3
  60.8 0.9 %multiply_convert_fusion = f16[8,4,32,256]{3,2,1,0:T(8,128)(2,1)} fusion(f32[8,4,32,256]{3,2,1,0:T(8,128)S(1)} %taps.1, f32[256]{0:T(256)S(1)} %bitcast.38), kind=kLoop, calls=%fused_computation.1 | loop fusion | flops 524288 | bytes 1573888 | tf_op jit(solution)/shard_map/convert_element_type | solution.py:358
  61.8 4.1 %all-to-all-start.2 = ((f16[8,4,32,256]{3,2,1,0:T(8,128)(2,1)}), f16[8,4,32,256]{3,2,1,0:T(8,128)(2,1)S(1)}, u32[]{:S(2)}, u32[]{:S(2)}) async-start(f16[8,4,32,256]{3,2,1,0:T(8,128)(2,1)} %multiply_convert_fusion), calls=%async_computation.2 | async-start | bytes 1048576 | tf_op jit(solution)/shard_map/all_to_all | solution.py:359
  65.8 0.1 broadcast_compare_fusion
  65.9 9.4 %all-to-all-done.2 = f16[8,4,32,256]{3,2,1,0:T(8,128)(2,1)S(1)} async-done(((f16[8,4,32,256]{3,2,1,0:T(8,128)(2,1)}), f16[8,4,32,256]{3,2,1,0:T(8,128)(2,1)S(1)}, u32[]{:S(2)}, u32[]{:S(2)}) %all-to-all-start.2) | async-done | bytes 524320 | tf_op jit(solution)/shard_map/all_to_all | solution.py:359
  75.3 0.1 convert_reduce_fusion
  75.4 0.7 select_convert_fusion
  (11 shorter events, 0.1 us)
Async XLA Ops:
  0.0 19.7 %copy-start = (bf16[2,4,2,16,512]{4,3,2,1,0:T(8,128)(2,1)S(1)}, bf16[2,4,2,16,512]{4,3,2,1,0:T(8,128)(2,1)}, u32[]{:S(2)}) copy-start(bf16[2,4,2,16,512]{4,3,2,1,0:T(8,128)(2,1)} %param.6) | copy-start | bytes 786436
  0.0 19.7 %copy-start.2 = (f32[512]{0:T(512)S(1)}, f32[512]{0:T(512)}, u32[]{:S(2)}) copy-start(f32[512]{0:T(512)} %param.9) | copy-start | bytes 6148
  0.0 19.8 %copy-start.1 = (f32[512]{0:T(512)S(1)}, f32[512]{0:T(512)}, u32[]{:S(2)}) copy-start(f32[512]{0:T(512)} %param.8) | copy-start | bytes 6148
  2.6 41.8 %all-to-all-start = ((bf16[64,2,3712]{2,1,0:T(2,128)(2,1)}), bf16[64,2,3712]{2,1,0:T(2,128)(2,1)S(1)}, u32[]{:S(2)}, u32[]{:S(2)}) async-start(bf16[64,2,3712]{2,1,0:T(2,128)(2,1)} %get-tuple-element.15), calls=%async_computation | async-start | bytes 1900544 | tf_op jit(solution)/shard_map/all_to_all | solution.py:283
  20.2 3.8 %collective-permute-start = (bf16[4,4,16,256]{3,2,1,0:T(8,128)(2,1)S(1)}, bf16[4,4,16,256]{3,2,1,0:T(8,128)(2,1)S(1)}, u32[]{:S(2)}, u32[]{:S(2)}) collective-permute-start(bf16[4,4,16,256]{3,2,1,0:T(8,128)(2,1)S(1)} %get-tuple-element.17), channel_id=1, source_target_pairs={{0,64},{64,0},{1,65},{65,1},{2,66},{66,2},{3,67},{67,3},{4,68},{68... | collective-permute-start | bytes 393224 | tf_op jit(solution)/shard_map/ppermute | solution.py:299
  24.0 10.6 %collective-permute-start.1 = (bf16[2,4,16,256]{3,2,1,0:T(8,128)(2,1)S(1)}, bf16[2,4,16,256]{3,2,1,0:T(8,128)(2,1)S(1)}, u32[]{:S(2)}, u32[]{:S(2)}) collective-permute-start(bf16[2,4,16,256]{3,2,1,0:T(8,128)(2,1)S(1)} %get-tuple-element.26), channel_id=1, source_target_pairs={{0,128},{128,256},{256,384},{384,0},{1,129},{129,257},{257,385},{3... | collective-permute-start | bytes 196616 | tf_op jit(solution)/shard_map/ppermute | solution.py:304
  27.1 7.4 %collective-permute-start.2 = (bf16[2,4,16,256]{3,2,1,0:T(8,128)(2,1)S(1)}, bf16[2,4,16,256]{3,2,1,0:T(8,128)(2,1)S(1)}, u32[]{:S(2)}, u32[]{:S(2)}) collective-permute-start(bf16[2,4,16,256]{3,2,1,0:T(8,128)(2,1)S(1)} %get-tuple-element.27), channel_id=1, source_target_pairs={{0,256},{128,384},{256,0},{384,128},{1,257},{129,385},{257,1},{385... | collective-permute-start | bytes 196616 | tf_op jit(solution)/shard_map/ppermute | solution.py:304
  31.5 5.3 %collective-permute-start.3 = (bf16[2,4,16,256]{3,2,1,0:T(8,128)(2,1)S(1)}, bf16[2,4,16,256]{3,2,1,0:T(8,128)(2,1)S(1)}, u32[]{:S(2)}, u32[]{:S(2)}) collective-permute-start(bf16[2,4,16,256]{3,2,1,0:T(8,128)(2,1)S(1)} %get-tuple-element.28), channel_id=1, source_target_pairs={{0,384},{128,0},{256,128},{384,256},{1,385},{129,1},{257,129},{385... | collective-permute-start | bytes 196616 | tf_op jit(solution)/shard_map/ppermute | solution.py:304
  37.6 17.8 %collective-permute-start.5 = (bf16[4,2,4,16,128]{4,3,2,1,0:T(8,128)(2,1)}, bf16[4,2,4,16,128]{4,3,2,1,0:T(8,128)(2,1)S(1)}, u32[]{:S(2)}, u32[]{:S(2)}) collective-permute-start(bf16[4,2,4,16,128]{4,3,2,1,0:T(8,128)(2,1)} %get-tuple-element.23), channel_id=1, source_target_pairs={{1,0},{2,1},{3,2},{4,3},{5,4},{6,5},{7,6},{8,7},{9,8},{10,9},{11,1... | collective-permute-start | bytes 393224 | tf_op jit(solution)/shard_map/ppermute | solution.py:309
  38.8 16.6 %collective-permute-start.4 = (bf16[4,2,4,16,128]{4,3,2,1,0:T(8,128)(2,1)S(1)}, bf16[4,2,4,16,128]{4,3,2,1,0:T(8,128)(2,1)S(1)}, u32[]{:S(2)}, u32[]{:S(2)}) collective-permute-start(bf16[4,2,4,16,128]{4,3,2,1,0:T(8,128)(2,1)S(1)} %get-tuple-element.24), channel_id=1, source_target_pairs={{0,1},{1,2},{2,3},{3,4},{4,5},{5,6},{6,7},{7,8},{8,9},{9,10},{10,1... | collective-permute-start | bytes 393224 | tf_op jit(solution)/shard_map/ppermute | solution.py:308
  45.2 12.8 %all-to-all-start.1 = ((f32[8,1,128]{2,1,0:T(1,128)}), f32[8,1,128]{2,1,0:T(1,128)S(1)}, u32[]{:S(2)}, u32[]{:S(2)}) async-start(f32[8,1,128]{2,1,0:T(1,128)} %sums.1), calls=%async_computation.1 | async-start | bytes 8192 | tf_op jit(solution)/shard_map/all_to_all | solution.py:320
  53.5 5.3 %collective-permute-start.6 = (bf16[2,64,3712]{2,1,0:T(8,128)(2,1)S(1)}, bf16[2,64,3712]{2,1,0:T(8,128)(2,1)S(1)}, u32[]{:S(2)}, u32[]{:S(2)}) collective-permute-start(bf16[2,64,3712]{2,1,0:T(8,128)(2,1)S(1)} %bitcast.25), channel_id=1, source_target_pairs={{0,64},{64,0},{1,65},{65,1},{2,66},{66,2},{3,67},{67,3},{4,68},{68... | collective-permute-start | bytes 2850824 | tf_op jit(solution)/shard_map/ppermute | solution.py:322
  60.8 5.0 %copy-start.3 = (s32[2]{0:T(128)S(1)}, s32[2]{0:T(128)}, u32[]{:S(2)}) copy-start(s32[2]{0:T(128)} %lengths.1) | copy-start | bytes 28
  61.8 13.6 %all-to-all-start.2 = ((f16[8,4,32,256]{3,2,1,0:T(8,128)(2,1)}), f16[8,4,32,256]{3,2,1,0:T(8,128)(2,1)S(1)}, u32[]{:S(2)}, u32[]{:S(2)}) async-start(f16[8,4,32,256]{3,2,1,0:T(8,128)(2,1)} %multiply_convert_fusion), calls=%async_computation.2 | async-start | bytes 1048576 | tf_op jit(solution)/shard_map/all_to_all | solution.py:359
